TPU v7x, 32 devices: a whole 2x2x4 slice. The times are simulated.
32 devices in a mesh: pipe: 4 (over z), head: 8 (over y, x, core).
Axes of the slice: x: 2, y: 2, z: 4, core: 2. Of those that a mesh axis runs over, the one named last changes fastest.
Arguments:
- hidden: bfloat16 [2, 64, 8192], P(None, 'head'), may hold values from -6 to 6
- norm_gain: float32 [4, 8192], P('pipe'), may hold values from 0.1 to 1.9
- w_x: bfloat16 [4, 8192, 16384], P('pipe', None, 'head'), may hold values from -0.0625 to 0.0625
- w_bc: bfloat16 [4, 8192, 4096], P('pipe', None, 'head'), may hold values from -0.03125 to 0.03125
- w_dt: bfloat16 [4, 8192, 256], P('pipe', None, 'head'), may hold values from -0.0625 to 0.0625
- conv_x: float32 [4, 4, 16384], P('pipe', None, 'head'), may hold values from -3 to 3
- conv_bc: float32 [4, 4, 4096], P('pipe'), may hold values from -3 to 3
- dt_bias: float32 [4, 256], P('pipe', 'head'), may hold values from -3 to 0.5
- a_rate: float32 [4, 256], P('pipe', 'head'), may hold values from 0.002 to 0.2
- d_skip: float32 [4, 256], P('pipe', 'head'), may hold values from 0.5 to 1.5
- w_out: bfloat16 [4, 16384, 8192], P('pipe', 'head'), may hold values from -0.046875 to 0.046875
- ssm_init: float32 [4, 256, 64, 256], P('pipe', 'head'), may hold values from -0.6 to 0.6
- conv_x_init: float32 [4, 3, 16384], P('pipe', None, 'head'), may hold values from -6 to 6
- conv_bc_init: float32 [4, 3, 4096], P('pipe'), may hold values from -3 to 3
Outputs:
- segment_out: bfloat16 [4, 2, 64, 8192], P('pipe', None, 'head')
- state_out: float32 [4, 256, 64, 256], P('pipe', 'head')
All inputs are finite; a program needn't handle non-finite values.
Results may differ from a plain program's by a relative error of at most 0.039.
Values may be sent and summed in bfloat16 or wider, within the bound.
No kernel may reach another device: no remote copies, remote signals or barrier semaphores. Data moves between devices by JAX's collectives and lax.ppermute only.
A program may use at most 192 MiB of HBM per device.

v0:
```python
import jax
import jax.numpy as jnp
from jax import lax
from jax.sharding import PartitionSpec as P

HEADS = 256
STATE = 256
GROUPS = 8


def passed_along(value, axis, steps):
    count = lax.axis_size(axis)
    initial, last = (max(0, -steps), min(count, count - steps))
    return lax.ppermute(value, axis, [(source, source + steps) for source in range(initial, last)])


def rms_rows(block_in, norm_weight):
    floats = block_in.astype(jnp.float32)
    scaled = floats * lax.rsqrt(jnp.mean(floats * floats, axis=-1, keepdims=True) + 1e-05)
    return (scaled * norm_weight[None, :]).astype(jnp.bfloat16)


def causal_conv(tail_rows, values, taps):
    padded = jnp.concatenate([tail_rows, values], axis=0)
    length = values.shape[0]
    conv_sum = taps[0][None, :] * padded[0:length]
    for offset in range(1, taps.shape[0]):
        conv_sum = conv_sum + taps[offset][None, :] * padded[offset : offset + length]
    return (jax.nn.silu(conv_sum), padded[length:])


def scan_block(values, b_heads, c_heads, step_size, decay_rate, skip_gain, ssm_state):
    highest = lax.Precision.HIGHEST
    log_decay = jnp.cumsum(-step_size * decay_rate[None, :], axis=0)
    length = values.shape[0]
    causal = (jnp.arange(length)[:, None] >= jnp.arange(length)[None, :])[:, :, None]
    gap_log = log_decay[:, None, :] - log_decay[None, :, :]
    decay_pairs = jnp.where(causal, jnp.exp(jnp.where(causal, gap_log, 0.0)), 0.0)
    scores = jnp.einsum("thn,shn->tsh", c_heads, b_heads, precision=highest)
    pair_weight = scores * decay_pairs * step_size[None, :, :]
    within = jnp.einsum("tsh,shp->thp", pair_weight, values, precision=highest)
    carried = jnp.exp(log_decay)[:, :, None] * jnp.einsum(
        "thn,hpn->thp", c_heads, ssm_state, precision=highest
    )
    mixed_out = within + carried + skip_gain[None, :, None] * values
    end_log = log_decay[-1]
    to_end = jnp.exp(end_log[None, :] - log_decay) * step_size
    new_state = jnp.exp(end_log)[:, None, None] * ssm_state + jnp.einsum(
        "sh,shp,shn->hpn", to_end, values, b_heads, precision=highest
    )
    return (mixed_out, new_state)


def mix_block(
    block_in,
    norm_weight,
    proj_x,
    proj_bc,
    proj_dt,
    taps_x,
    taps_bc,
    step_bias,
    decay_rate,
    skip_gain,
    ssm_state,
    tail_x,
    tail_bc,
    group_pick,
):
    highest = lax.Precision.HIGHEST
    normed = rms_rows(block_in, norm_weight)
    x_proj = jnp.dot(normed, proj_x, preferred_element_type=jnp.float32)
    bc_part = jnp.dot(normed, proj_bc, preferred_element_type=jnp.float32).astype(jnp.bfloat16)
    bc_all = lax.all_gather(bc_part, "head", axis=1, tiled=True)
    dt_raw = jnp.dot(normed, proj_dt, preferred_element_type=jnp.float32)
    x_conv, new_tail_x = causal_conv(tail_x, x_proj, taps_x)
    bc_conv, new_tail_bc = causal_conv(tail_bc, bc_all.astype(jnp.float32), taps_bc)
    length = block_in.shape[0]
    grouped = bc_conv.reshape(length, 2, STATE, GROUPS)
    b_heads = jnp.einsum("tng,hg->thn", grouped[:, 0], group_pick, precision=highest)
    c_heads = jnp.einsum("tng,hg->thn", grouped[:, 1], group_pick, precision=highest)
    step_size = jax.nn.softplus(dt_raw + step_bias[None, :])
    local_heads = step_bias.shape[0]
    mixed, new_state = scan_block(
        x_conv.reshape(length, local_heads, -1),
        b_heads,
        c_heads,
        step_size,
        decay_rate,
        skip_gain,
        ssm_state,
    )
    return (mixed.reshape(length, -1).astype(jnp.bfloat16), new_state, new_tail_x, new_tail_bc)


def per_device(
    hidden,
    norm_gain,
    w_x,
    w_bc,
    w_dt,
    conv_x,
    conv_bc,
    dt_bias,
    a_rate,
    d_skip,
    w_out,
    ssm_init,
    conv_x_init,
    conv_bc_init,
):
    segment_index = lax.axis_index("pipe")
    pipe_count = lax.axis_size("pipe")
    head_index = lax.axis_index("head")
    head_count = lax.axis_size("head")
    micro_count, local_rows, model_width = hidden.shape
    block_rows = local_rows * head_count
    local_heads = dt_bias.shape[1]
    global_heads = head_index * local_heads + jnp.arange(local_heads)
    group_pick = (global_heads[:, None] // (HEADS // GROUPS) == jnp.arange(GROUPS)[None, :]).astype(
        jnp.float32
    )
    out_weight = w_out[0]
    ssm_state = ssm_init[0]
    tail_x = conv_x_init[0]
    tail_bc = conv_bc_init[0]
    out_rows = jnp.zeros((micro_count, local_rows, model_width), jnp.bfloat16)
    recv_full = jnp.zeros((block_rows, model_width), jnp.bfloat16)
    for tick_number in range(micro_count + pipe_count - 1):
        position = tick_number - segment_index
        active = jnp.logical_and(position >= 0, position < micro_count)
        clamped = jnp.clip(position, 0, micro_count - 1)
        own_rows = lax.dynamic_index_in_dim(hidden, clamped, 0, keepdims=False)
        entry_rows = lax.all_gather(own_rows, "head", axis=0, tiled=True)
        block_in = jnp.where(segment_index == 0, entry_rows, recv_full)
        mixed_bf, new_state, new_tail_x, new_tail_bc = mix_block(
            block_in,
            norm_gain[0],
            w_x[0],
            w_bc[0],
            w_dt[0],
            conv_x[0],
            conv_bc[0],
            dt_bias[0],
            a_rate[0],
            d_skip[0],
            ssm_state,
            tail_x,
            tail_bc,
            group_pick,
        )
        summed = lax.psum(
            jnp.dot(mixed_bf, out_weight, preferred_element_type=jnp.float32).astype(jnp.bfloat16),
            "head",
        ).astype(jnp.float32)
        new_full = (block_in.astype(jnp.float32) + summed).astype(jnp.bfloat16)
        new_rows = lax.dynamic_slice_in_dim(new_full, head_index * local_rows, local_rows, 0)
        recv_full = passed_along(new_full, "pipe", 1)
        ssm_state = jnp.where(active, new_state, ssm_state)
        tail_x = jnp.where(active, new_tail_x, tail_x)
        tail_bc = jnp.where(active, new_tail_bc, tail_bc)
        current = lax.dynamic_index_in_dim(out_rows, clamped, 0, keepdims=False)
        out_rows = lax.dynamic_update_index_in_dim(
            out_rows, jnp.where(active, new_rows, current), clamped, 0
        )
    return (out_rows[None], ssm_state[None])


def solution(mesh):
    in_specs = (
        P(None, "head", None),
        P("pipe", None),
        P("pipe", None, "head"),
        P("pipe", None, "head"),
        P("pipe", None, "head"),
        P("pipe", None, "head"),
        P("pipe", None, None),
        P("pipe", "head"),
        P("pipe", "head"),
        P("pipe", "head"),
        P("pipe", "head", None),
        P("pipe", "head", None, None),
        P("pipe", None, "head"),
        P("pipe", None, None),
    )
    out_specs = (P("pipe", None, "head", None), P("pipe", "head", None, None))
    return jax.shard_map(
        per_device, mesh=mesh, in_specs=in_specs, out_specs=out_specs, check_vma=False
    )
```

profile of v0, /device:TPU:0, one launch (start us, length us, event | category | flops | bytes accessed | tf_op | source)
XLA Modules:
  0.0 823.5 jit_solution(7606754174385004784)
XLA Ops:
  13.1 23.7 %all-gather.11.cloned.1.call-done = bf16[1,64,8192]{2,1,0:T(8,128)(2,1)} async-done(((bf16[1,8,8192]{2,1,0:T(8,128)(2,1)}), bf16[1,64,8192]{2,1,0:T(8,128)(2,1)}) %all-gather.11.cloned.1.call-update) | async-done | bytes 1048592 | tf_op jit(solution)/shard_map/all_gather | solution.py:134
  46.1 9.8 %all_gather.31 = bf16[64,4096]{1,0:T(8,128)(2,1)S(1)} all-gather(bf16[64,512]{1,0:T(8,128)(2,1)S(1)} %fusion.232), channel_id=1, replica_groups=mesh['pipe'=4,'head'=8] {'head'}, dimensions={1}, use_global_device_ids=true | all-gather | bytes 589824 | tf_op jit(solution)/shard_map/all_gather | solution.py:74
  64.8 13.9 %fusion.18 = f32[64,2048]{1,0:T(8,128)S(1)} fusion(bf16[1,8192,2048]{2,1,0:T(8,128)(2,1)} %param.16, f32[8192]{0:T(1024)S(1)} %bitcast.395, f32[64]{0:T(128)S(1)} %add_rsqrt_fusion.4, bf16[1,64,8192]{2,1,0:T(8,128)(2,1)S(1)} %copy-done.1, pred[]{:T(512)S(6)} %eq.8), kind=kOutput, calls=%fused_computation.18 | convolution fusion | flops 2150105088 | bytes 35160320 | tf_op jit(solution)/shard_map/dot_general | solution.py:72
  97.4 14.7 %fusion.20 = bf16[64,8192]{1,0:T(8,128)(2,1)} fusion(bf16[64,2048]{0,1:T(8,128)(2,1)S(1)} %bitcast.412, bf16[1,2048,8192]{2,1,0:T(8,128)(2,1)} %param.24), kind=kOutput, calls=%fused_computation.20 | convolution fusion | flops 2148007936 | bytes 34865152 | tf_op jit(solution)/shard_map/dot_general | solution.py:153
  112.9 53.5 %all-reduce.6.cloned.1.call-done = bf16[64,8192]{1,0:T(8,128)(2,1)} async-done(((bf16[64,8192]{1,0:T(8,128)(2,1)}), bf16[64,8192]{1,0:T(8,128)(2,1)}) %all-reduce.6.cloned.1.call-update) | async-done | bytes 1048592 | tf_op jit(solution)/shard_map/psum | solution.py:152
  173.4 6.1 bitcast_select_fusion
  179.5 11.4 %all-gather.13.cloned.1.call-done = bf16[1,64,8192]{2,1,0:T(8,128)(2,1)} async-done(((bf16[1,8,8192]{2,1,0:T(8,128)(2,1)}), bf16[1,64,8192]{2,1,0:T(8,128)(2,1)}) %all-gather.13.cloned.1.call-update) | async-done | bytes 1048592 | tf_op jit(solution)/shard_map/all_gather | solution.py:134
  202.0 14.4 %fusion.16 = f32[64,2048]{1,0:T(8,128)} fusion(bf16[1,8192,2048]{2,1,0:T(8,128)(2,1)} %param.16, bf16[64,8192]{1,0:T(8,128)(2,1)S(1)} %get-tuple-element.17, f32[64]{0:T(128)S(1)} %add_rsqrt_fusion.3, f32[8192]{0:T(1024)S(1)} %bitcast.398), kind=kOutput, calls=%fused_computation.16 | convolution fusion | flops 2149580800 | bytes 35160320 | tf_op jit(solution)/shard_map/dot_general | solution.py:72
  216.7 9.1 %all_gather.33 = bf16[64,4096]{1,0:T(8,128)(2,1)S(1)} all-gather(bf16[64,512]{1,0:T(8,128)(2,1)S(1)} %fusion.235), channel_id=1, replica_groups=mesh['pipe'=4,'head'=8] {'head'}, dimensions={1}, use_global_device_ids=true | all-gather | bytes 589824 | tf_op jit(solution)/shard_map/all_gather | solution.py:74
  243.0 5.5 fusion.121
  255.4 14.7 %fusion.23 = bf16[64,8192]{1,0:T(8,128)(2,1)} fusion(bf16[64,2048]{0,1:T(8,128)(2,1)S(1)} %bitcast.413, bf16[1,2048,8192]{2,1,0:T(8,128)(2,1)} %param.24), kind=kOutput, calls=%fused_computation.21 | convolution fusion | flops 2148007936 | bytes 34865152 | tf_op jit(solution)/shard_map/dot_general | solution.py:153
  270.8 57.5 %all-reduce.8.cloned.1.call-done = bf16[64,8192]{1,0:T(8,128)(2,1)} async-done(((bf16[64,8192]{1,0:T(8,128)(2,1)}), bf16[64,8192]{1,0:T(8,128)(2,1)}) %all-reduce.8.cloned.1.call-update) | async-done | bytes 1048592 | tf_op jit(solution)/shard_map/psum | solution.py:152
  335.2 6.1 add_select_fusion.2
  341.3 11.9 %all-gather.15.cloned.1.call-done = bf16[1,64,8192]{2,1,0:T(8,128)(2,1)} async-done(((bf16[1,8,8192]{2,1,0:T(8,128)(2,1)}), bf16[1,64,8192]{2,1,0:T(8,128)(2,1)}) %all-gather.15.cloned.1.call-update) | async-done | bytes 1048592 | tf_op jit(solution)/shard_map/all_gather | solution.py:134
  363.8 13.7 %fusion.14 = f32[64,2048]{1,0:T(8,128)S(1)} fusion(bf16[1,8192,2048]{2,1,0:T(8,128)(2,1)} %param.16, bf16[64,8192]{1,0:T(8,128)(2,1)S(1)} %get-tuple-element.15, f32[64]{0:T(128)S(1)} %add_rsqrt_fusion.2, f32[8192]{0:T(1024)S(1)} %bitcast.401), kind=kOutput, calls=%fused_computation.14 | convolution fusion | flops 2149580800 | bytes 35160320 | tf_op jit(solution)/shard_map/dot_general | solution.py:72
  377.7 9.1 %all_gather.35 = bf16[64,4096]{1,0:T(8,128)(2,1)S(1)} all-gather(bf16[64,512]{1,0:T(8,128)(2,1)S(1)} %fusion.238), channel_id=1, replica_groups=mesh['pipe'=4,'head'=8] {'head'}, dimensions={1}, use_global_device_ids=true | all-gather | bytes 589824 | tf_op jit(solution)/shard_map/all_gather | solution.py:74
  418.7 14.7 %fusion.26 = bf16[64,8192]{1,0:T(8,128)(2,1)} fusion(bf16[64,2048]{0,1:T(8,128)(2,1)S(1)} %bitcast.414, bf16[1,2048,8192]{2,1,0:T(8,128)(2,1)} %param.24), kind=kOutput, calls=%fused_computation.22 | convolution fusion | flops 2148007936 | bytes 34865152 | tf_op jit(solution)/shard_map/dot_general | solution.py:153
  434.3 57.3 %all-reduce.10.cloned.1.call-done = bf16[64,8192]{1,0:T(8,128)(2,1)} async-done(((bf16[64,8192]{1,0:T(8,128)(2,1)}), bf16[64,8192]{1,0:T(8,128)(2,1)}) %all-reduce.10.cloned.1.call-update) | async-done | bytes 1048592 | tf_op jit(solution)/shard_map/psum | solution.py:152
  498.7 6.1 add_select_fusion.1
  504.8 11.3 %all-gather.17.cloned.1.call-done = bf16[1,64,8192]{2,1,0:T(8,128)(2,1)} async-done(((bf16[1,8,8192]{2,1,0:T(8,128)(2,1)}), bf16[1,64,8192]{2,1,0:T(8,128)(2,1)}) %all-gather.17.cloned.1.call-update) | async-done | bytes 1048592 | tf_op jit(solution)/shard_map/all_gather | solution.py:134
  527.2 14.4 %fusion.12 = f32[64,2048]{1,0:T(8,128)} fusion(bf16[1,8192,2048]{2,1,0:T(8,128)(2,1)} %param.16, bf16[64,8192]{1,0:T(8,128)(2,1)S(1)} %get-tuple-element.9, f32[64]{0:T(128)S(1)} %add_rsqrt_fusion.1, f32[8192]{0:T(1024)S(1)} %bitcast.404), kind=kOutput, calls=%fused_computation.12 | convolution fusion | flops 2149580800 | bytes 35160320 | tf_op jit(solution)/shard_map/dot_general | solution.py:72
  541.9 9.1 %all_gather.37 = bf16[64,4096]{1,0:T(8,128)(2,1)S(1)} all-gather(bf16[64,512]{1,0:T(8,128)(2,1)S(1)} %fusion.241), channel_id=1, replica_groups=mesh['pipe'=4,'head'=8] {'head'}, dimensions={1}, use_global_device_ids=true | all-gather | bytes 589824 | tf_op jit(solution)/shard_map/all_gather | solution.py:74
  569.4 5.5 fusion.153
  581.8 14.8 %fusion.29 = bf16[64,8192]{1,0:T(8,128)(2,1)} fusion(bf16[64,2048]{0,1:T(8,128)(2,1)S(1)} %bitcast.415, bf16[1,2048,8192]{2,1,0:T(8,128)(2,1)} %param.24), kind=kOutput, calls=%fused_computation.23 | convolution fusion | flops 2148007936 | bytes 34865152 | tf_op jit(solution)/shard_map/dot_general | solution.py:153
  600.7 6.1 add_select_fusion
  606.7 48.1 %all-reduce.12.cloned.1.call-done = bf16[64,8192]{1,0:T(8,128)(2,1)} async-done(((bf16[64,8192]{1,0:T(8,128)(2,1)}), bf16[64,8192]{1,0:T(8,128)(2,1)}) %all-reduce.12.cloned.1.call-update) | async-done | bytes 1048592 | tf_op jit(solution)/shard_map/psum | solution.py:152
  660.4 18.9 %all-gather.19.cloned.1.call-done = bf16[1,64,8192]{2,1,0:T(8,128)(2,1)} async-done(((bf16[1,8,8192]{2,1,0:T(8,128)(2,1)}), bf16[1,64,8192]{2,1,0:T(8,128)(2,1)}) %all-gather.19.cloned.1.call-update) | async-done | bytes 1048592 | tf_op jit(solution)/shard_map/all_gather | solution.py:134
  690.4 13.6 %fusion.10 = f32[64,2048]{1,0:T(8,128)S(1)} fusion(bf16[64,8192]{1,0:T(8,128)(2,1)S(1)} %multiply_convert_fusion, bf16[1,8192,2048]{2,1,0:T(8,128)(2,1)} %param.16), kind=kOutput, calls=%fused_computation.10 | convolution fusion | flops 2147483648 | bytes 35127296 | tf_op jit(solution)/shard_map/dot_general | solution.py:72
  706.0 9.1 %all_gather.39 = bf16[64,4096]{1,0:T(8,128)(2,1)S(1)} all-gather(bf16[64,512]{1,0:T(8,128)(2,1)S(1)} %fusion.244), channel_id=1, replica_groups=mesh['pipe'=4,'head'=8] {'head'}, dimensions={1}, use_global_device_ids=true | all-gather | bytes 589824 | tf_op jit(solution)/shard_map/all_gather | solution.py:74
  742.0 14.9 %fusion.32 = bf16[64,8192]{1,0:T(8,128)(2,1)} fusion(bf16[64,2048]{0,1:T(8,128)(2,1)S(1)} %bitcast.416, bf16[1,2048,8192]{2,1,0:T(8,128)(2,1)} %param.24), kind=kOutput, calls=%fused_computation.24 | convolution fusion | flops 2148007936 | bytes 34865152 | tf_op jit(solution)/shard_map/dot_general | solution.py:153
  757.0 6.4 select_bitcast_fusion
  763.4 51.3 %all-reduce.14.cloned.1.call-done = bf16[64,8192]{1,0:T(8,128)(2,1)} async-done(((bf16[64,8192]{1,0:T(8,128)(2,1)}), bf16[64,8192]{1,0:T(8,128)(2,1)}) %all-reduce.14.cloned.1.call-update) | async-done | bytes 1048592 | tf_op jit(solution)/shard_map/psum | solution.py:152
  (279 shorter events, 231.3 us)
Async XLA Ops:
  7.2 31.3 %copy-start = (bf16[1,8192,32]{1,2,0:T(8,128)(2,1)S(1)}, bf16[1,8192,32]{1,2,0:T(8,128)(2,1)}, u32[]{:S(2)}) copy-start(bf16[1,8192,32]{1,2,0:T(8,128)(2,1)} %param.18) | copy-start | bytes 1572868
  7.2 31.3 %copy-start.18 = (f32[1,8192]{1,0:T(1,128)S(1)}, f32[1,8192]{1,0:T(1,128)}, u32[]{:S(2)}) copy-start(f32[1,8192]{1,0:T(1,128)} %param.15) | copy-start | bytes 98308
  7.2 31.3 %copy-start.40 = (f32[1,32]{1,0:T(1,128)S(1)}, f32[1,32]{1,0:T(1,128)}, u32[]{:S(2)}) copy-start(f32[1,32]{1,0:T(1,128)} %param.22) | copy-start | bytes 388
  7.2 31.3 %copy-start.45 = (f32[1,32]{1,0:T(1,128)S(1)}, f32[1,32]{1,0:T(1,128)}, u32[]{:S(2)}) copy-start(f32[1,32]{1,0:T(1,128)} %param.21) | copy-start | bytes 388
  7.2 29.5 %all-gather.11.cloned.1.call-start = ((), (), s32[]{:S(2)}) async-start(), calls=%async_computation.5 | async-start | bytes 1179648 | tf_op jit(solution)/shard_map/all_gather | solution.py:134
  9.4 157.0 %all-reduce.6.cloned.1.call-start = ((), (), s32[]{:S(2)}) async-start(), calls=%async_computation | async-start | bytes 2097152 | tf_op jit(solution)/shard_map/psum | solution.py:152
  112.1 78.8 %all-gather.13.cloned.1.call-start = ((), (), s32[]{:S(2)}) async-start(), calls=%async_computation.6 | async-start | bytes 1179648 | tf_op jit(solution)/shard_map/all_gather | solution.py:134
  112.8 215.5 %all-reduce.8.cloned.1.call-start = ((), (), s32[]{:S(2)}) async-start(), calls=%async_computation.1 | async-start | bytes 2097152 | tf_op jit(solution)/shard_map/psum | solution.py:152
  166.4 7.0 copy-start.10
  169.1 25.0 %collective-permute-start = (bf16[64,8192]{1,0:T(8,128)(2,1)}, bf16[64,8192]{1,0:T(8,128)(2,1)}, u32[]{:S(2)}, u32[]{:S(2)}) collective-permute-start(bf16[64,8192]{1,0:T(8,128)(2,1)} %fusion.60), channel_id=1, source_target_pairs={{0,8},{8,16},{16,24},{1,9},{9,17},{17,25},{2,10},{10,18},{18,26},{... | collective-permute-start | bytes 3145736 | tf_op jit(solution)/shard_map/ppermute | solution.py:14
  216.4 9.4 %copy-start.29 = (f32[1,3,4096]{2,0,1:T(1,128)S(1)}, f32[1,3,4096]{2,0,1:T(1,128)}, u32[]{:S(2)}) copy-start(f32[1,3,4096]{2,0,1:T(1,128)} %param.27) | copy-start | bytes 147460
  243.0 5.5 copy-start.11
  243.0 5.5 copy-start.38
  270.2 83.1 %all-gather.15.cloned.1.call-start = ((), (), s32[]{:S(2)}) async-start(), calls=%async_computation.7 | async-start | bytes 1179648 | tf_op jit(solution)/shard_map/all_gather | solution.py:134
  270.8 220.9 %all-reduce.10.cloned.1.call-start = ((), (), s32[]{:S(2)}) async-start(), calls=%async_computation.2 | async-start | bytes 2097152 | tf_op jit(solution)/shard_map/psum | solution.py:152
  328.3 6.9 copy-start.12
  330.9 25.0 %collective-permute-start.1 = (bf16[64,8192]{1,0:T(8,128)(2,1)}, bf16[64,8192]{1,0:T(8,128)(2,1)}, u32[]{:S(2)}, u32[]{:S(2)}) collective-permute-start(bf16[64,8192]{1,0:T(8,128)(2,1)} %fusion.48), channel_id=1, source_target_pairs={{0,8},{8,16},{16,24},{1,9},{9,17},{17,25},{2,10},{10,18},{18,26},{... | collective-permute-start | bytes 3145736 | tf_op jit(solution)/shard_map/ppermute | solution.py:14
  406.3 5.5 copy-start.7
  406.3 5.5 copy-start.37
  433.5 82.6 %all-gather.17.cloned.1.call-start = ((), (), s32[]{:S(2)}) async-start(), calls=%async_computation.8 | async-start | bytes 1179648 | tf_op jit(solution)/shard_map/all_gather | solution.py:134
  434.2 220.6 %all-reduce.12.cloned.1.call-start = ((), (), s32[]{:S(2)}) async-start(), calls=%async_computation.3 | async-start | bytes 2097152 | tf_op jit(solution)/shard_map/psum | solution.py:152
  491.6 7.0 copy-start.8
  494.2 25.0 %collective-permute-start.2 = (bf16[64,8192]{1,0:T(8,128)(2,1)}, bf16[64,8192]{1,0:T(8,128)(2,1)}, u32[]{:S(2)}, u32[]{:S(2)}) collective-permute-start(bf16[64,8192]{1,0:T(8,128)(2,1)} %fusion.52), channel_id=1, source_target_pairs={{0,8},{8,16},{16,24},{1,9},{9,17},{17,25},{2,10},{10,18},{18,26},{... | collective-permute-start | bytes 3145736 | tf_op jit(solution)/shard_map/ppermute | solution.py:14
  569.4 5.5 copy-start.5
  569.4 5.5 copy-start.35
  596.7 82.6 %all-gather.19.cloned.1.call-start = ((), (), s32[]{:S(2)}) async-start(), calls=%async_computation.9 | async-start | bytes 1179648 | tf_op jit(solution)/shard_map/all_gather | solution.py:134
  597.4 217.3 %all-reduce.14.cloned.1.call-start = ((), (), s32[]{:S(2)}) async-start(), calls=%async_computation.4 | async-start | bytes 2097152 | tf_op jit(solution)/shard_map/psum | solution.py:152
  656.3 24.7 %collective-permute-start.3 = (bf16[64,8192]{1,0:T(8,128)(2,1)S(1)}, bf16[64,8192]{1,0:T(8,128)(2,1)S(1)}, u32[]{:S(2)}, u32[]{:S(2)}) collective-permute-start(bf16[64,8192]{1,0:T(8,128)(2,1)S(1)} %fusion.56), channel_id=1, source_target_pairs={{0,8},{8,16},{16,24},{1,9},{9,17},{17,25},{2,10},{10,18},{18,26},{... | collective-permute-start | bytes 3145736 | tf_op jit(solution)/shard_map/ppermute | solution.py:14
  704.0 11.2 %copy-start.25 = (f32[3,4096]{1,0:T(4,128)S(1)}, f32[3,4096]{1,0:T(4,128)}, u32[]{:S(2)}) copy-start(f32[3,4096]{1,0:T(4,128)} %get-tuple-element.4) | copy-start | bytes 147460
  742.0 14.9 %copy-start.50 = (f32[32]{0:T(128)S(1)}, f32[32]{0:T(128)}, u32[]{:S(2)}) copy-start(f32[32]{0:T(128)} %slice_bitcast_fusion) | copy-start | bytes 388
  742.0 15.0 %copy-start.14 = (f32[64,32,256]{2,1,0:T(8,128)S(1)}, f32[64,32,256]{2,1,0:T(8,128)}, u32[]{:S(2)}) copy-start(f32[64,32,256]{2,1,0:T(8,128)} %copy-done.13) | copy-start | bytes 6291460
  757.0 57.7 %copy-start.26 = (bf16[1,2,8,8192]{3,2,1,0:T(8,128)(2,1)S(1)}, bf16[1,2,8,8192]{3,2,1,0:T(8,128)(2,1)}, u32[]{:S(2)}) copy-start(bf16[1,2,8,8192]{3,2,1,0:T(8,128)(2,1)} %copy.310) | copy-start | bytes 786436
  (33 other events, 122.7 us)
Sparse Core Ops, SparseCore 0:
  10.5 26.1 all-gather.10
  112.2 54.1 all-reduce.5
  168.3 22.5 all-gather.12
  270.3 57.9 all-reduce.7
  330.6 22.5 all-gather.14
  433.6 57.9 all-reduce.9
  493.5 22.5 all-gather.16
  596.8 57.9 all-reduce.11
  656.7 22.5 all-gather.18
  757.0 57.6 all-reduce.13
where the time goes:
time: 831 us; the launch traced here: 823 us
  waiting for transfers between devices  358 us (43%)
  matrix products  285 us (34%)
  local copies, waits for them, and re-layouts  63.2 us (8%)
  blocking collectives  46.1 us (6%)
  other arithmetic  38.9 us (5%)
  starting transfers between devices  16.5 us (2%)
  between operations  15.6 us (2%)
    psum x5, waiting for transfers between devices, per_device(): lax.psum(jnp.dot(mixed_bf, out_weight, preferred_element_type=jnp.float32...  268 us
    all_gather x5, waiting for transfers between devices, per_device(): entry_rows = lax.all_gather(own_rows, 'head', axis=0, tiled=True)  77.2 us
    dot_general x5, matrix products, per_device(): jnp.dot(mixed_bf, out_weight, preferred_element_type=jnp.float32)  73.8 us
    dot_general x5, matrix products, mix_block(): x_proj = jnp.dot(normed, proj_x, preferred_element_type=jnp.float32)  70 us
    all_gather x5, blocking collectives, mix_block(): bc_all = lax.all_gather(bc_part, 'head', axis=1, tiled=True)  46.1 us
    dot_general x5, matrix products, scan_block(): jnp.einsum('sh,shp,shn->hpn', to_end, values, b_heads, precision=highest)  30.8 us
    dot_general x5, matrix products, mix_block(): jnp.dot(normed, proj_bc, preferred_element_type=jnp.float32)  25 us
    dot_general x5, matrix products, scan_block(): scores = jnp.einsum('thn,shn->tsh', c_heads, b_heads, precision=highest)  24.6 us
  transfers between devices with their start and end apart: 14, of which 14 were waited for; matrix products, arithmetic and copies ran while one was open for 6% of the time, Pallas kernels for 0%

commit v1 on v0

v1 whole, which is shorter than its diff:
```python
import functools

import jax
import jax.numpy as jnp
from jax import lax
from jax.experimental import pallas as pl
from jax.experimental.pallas import tpu as pltpu
from jax.sharding import PartitionSpec as P

STATE = 256
GROUPS = 8
MIB = 1 << 20
BF = jnp.bfloat16
F32 = jnp.float32
HIGHEST = lax.Precision.HIGHEST
VMEM_LIMIT = 40 * MIB
OUT_PARTS = 2


def whole(shape):
    return pl.BlockSpec(shape, lambda *_: (0,) * len(shape))


def cost(flops, nbytes):
    return pl.CostEstimate(flops=int(flops), bytes_accessed=int(nbytes), transcendentals=0)


def params():
    return pltpu.CompilerParams(vmem_limit_bytes=VMEM_LIMIT)


def dot(a, b, **kw):
    return jnp.dot(a, b, preferred_element_type=F32, **kw)


def chip_ring(chips):
    return [0, 1, 3, 2] if chips == 4 else list(range(chips))


def core_swap(value):
    count = lax.axis_size("head")
    return lax.ppermute(value, "head", [(i, i ^ 1) for i in range(count)])


def ring_shift(value, steps):
    chips = lax.axis_size("head") // 2
    ring = chip_ring(chips)
    pairs = [
        (2 * ring[i] + c, 2 * ring[(i + steps) % chips] + c) for i in range(chips) for c in range(2)
    ]
    return lax.ppermute(value, "head", pairs)


def next_segment(value, tick):
    count = lax.axis_size("pipe")
    pairs = []
    for low in range(tick % 2, count - 1, 2):
        pairs += [(low, low + 1), (low + 1, low)]
    return lax.ppermute(value, "pipe", pairs)


def relative_devices(sign):
    head = lax.axis_index("head")
    chips = lax.axis_size("head") // 2
    ring = chip_ring(chips)
    place = [ring.index(chip) for chip in range(chips)]
    mine = jnp.array(place, jnp.int32)[head // 2]
    steps = (mine + sign * jnp.arange(chips)) % chips
    chip = jnp.array(ring, jnp.int32)[steps]
    core = (head % 2) ^ jnp.arange(2)
    return 2 * chip[None, :] + core[:, None]


def first_kernel(own_ref, other_ref, order_ref, same_pick_ref, other_pick_ref, wbc_ref, wdt_ref,
                 normed_ref, dt_ref, same_ref, cross_ref):
    step = pl.program_id(0)
    half = own_ref.shape[0]
    width = own_ref.shape[1]
    block = 512

    @pl.when(step == 0)
    def _():
        @pl.loop(0, width // block)
        def _(i):
            cols = pl.ds(pl.multiple_of(i * block, block), block)
            normed_ref[:, cols] = (
                dot(order_ref[:, :half], own_ref[:, cols])
                + dot(order_ref[:, half:], other_ref[:, cols])
            ).astype(BF)

        dt_ref[...] = dot(normed_ref[...], wdt_ref[...])

    part = dot(normed_ref[...], wbc_ref[...]).astype(BF)
    same = dot(part, same_pick_ref[...]).astype(BF)
    cross = dot(part, other_pick_ref[...]).astype(BF)

    @pl.when(step == 0)
    def _():
        same_ref[...] = same
        cross_ref[...] = cross

    @pl.when(step > 0)
    def _():
        same_ref[...] += same
        cross_ref[...] += cross


def project_first(own, other, order, same_pick, cross_pick, w_bc, w_dt):
    width, bc_cols = w_bc.shape
    rows = order.shape[0]
    heads = w_dt.shape[1]
    out_cols = same_pick.shape[1]
    block = min(256, bc_cols)
    return pl.pallas_call(
        first_kernel,
        grid=(bc_cols // block,),
        in_specs=[
            whole(own.shape),
            whole(other.shape),
            whole(order.shape),
            pl.BlockSpec((block, out_cols), lambda i: (i, 0)),
            pl.BlockSpec((block, out_cols), lambda i: (i, 0)),
            pl.BlockSpec((width, block), lambda i: (0, i)),
            whole(w_dt.shape),
        ],
        out_specs=[whole((rows, width)), whole((rows, heads)), whole((rows, out_cols)), whole((rows, out_cols))],
        out_shape=[
            jax.ShapeDtypeStruct((rows, width), BF),
            jax.ShapeDtypeStruct((rows, heads), F32),
            jax.ShapeDtypeStruct((rows, out_cols), BF),
            jax.ShapeDtypeStruct((rows, out_cols), BF),
        ],
        compiler_params=params(),
        cost_estimate=cost(2 * rows * width * (bc_cols + heads), 2 * w_bc.size + 4 * rows * width),
    )(own, other, order, same_pick, cross_pick, w_bc, w_dt)


def inner_kernel(normed_ref, w_ref, x_ref):
    x_ref[...] = dot(normed_ref[...], w_ref[...])


def project_inner(normed, w_x):
    rows, width = normed.shape
    cols = w_x.shape[1]
    block = min(256, cols)
    return pl.pallas_call(
        inner_kernel,
        grid=(cols // block,),
        in_specs=[whole(normed.shape), pl.BlockSpec((width, block), lambda i: (0, i))],
        out_specs=pl.BlockSpec((rows, block), lambda i: (0, i)),
        out_shape=jax.ShapeDtypeStruct((rows, cols), F32),
        compiler_params=params(),
        cost_estimate=cost(2 * rows * width * cols, 2 * w_x.size + 2 * normed.size),
    )(normed, w_x)


def conv_silu(pad_ref, tail_ref, taps_ref):
    taps, rows = taps_ref.shape[0], pad_ref.shape[0] - 8
    pad_ref[8 - (taps - 1):8, :] = tail_ref[...]
    total = taps_ref[0:1, :] * pad_ref[pl.ds(9 - taps, rows), :]
    for k in range(1, taps):
        total = total + taps_ref[k:k + 1, :] * pad_ref[pl.ds(9 - taps + k, rows), :]
    return total * jax.nn.sigmoid(total)


def scan_kernel(x_ref, bc_ref, dt_ref, place_ref, spread_ref, tail_x_ref, taps_x_ref, tail_bc_ref, taps_bc_ref,
                bias_ref, rate_ref, skip_ref, state_ref, y_ref, weighted_ref, b_ref, end_ref,
                pad_x, pad_bc, scaled):
    rows, channels = x_ref.shape
    heads = dt_ref.shape[1]
    dim = channels // heads
    half = bc_ref.shape[1] // 2

    pad_bc[8:, :] = dot(bc_ref[...], place_ref[...])
    bc = conv_silu(pad_bc, tail_bc_ref, taps_bc_ref)
    b_mat, c_mat = bc[:, :half], bc[:, half:]
    b_bf, c_bf = b_mat.astype(BF), c_mat.astype(BF)
    b_ref[...] = b_bf
    contract = (((1,), (1,)), ((), ()))
    scores = lax.dot_general(c_mat, b_mat, contract, precision=HIGHEST, preferred_element_type=F32)
    t_ids = lax.broadcasted_iota(jnp.int32, (rows, rows), 0)
    s_ids = lax.broadcasted_iota(jnp.int32, (rows, rows), 1)
    causal = t_ids >= s_ids
    scores = jnp.where(causal, scores, 0.0)

    raw = dt_ref[...] + bias_ref[...]
    step = jnp.maximum(raw, 0.0) + jnp.log1p(jnp.exp(-jnp.abs(raw)))
    log_decay = dot(causal.astype(F32), -step * rate_ref[...], precision=HIGHEST)
    end_log = log_decay[rows - 1:rows, :]
    end_ref[...] = jnp.exp(end_log)
    spread = spread_ref[...]
    step_full = dot(step, spread, precision=HIGHEST)
    to_end_full = dot(jnp.exp(end_log - log_decay), spread, precision=HIGHEST)
    decay_full = dot(jnp.exp(log_decay), spread, precision=HIGHEST)
    log_rows = log_decay.T

    pad_x[8:, :] = x_ref[...]
    x_conv = conv_silu(pad_x, tail_x_ref, taps_x_ref)
    stepped = x_conv * step_full
    scaled[...] = stepped.astype(BF)
    weighted_ref[...] = (stepped * to_end_full).astype(BF)
    state = state_ref[...].reshape(channels, half).astype(BF)
    carried = lax.dot_general(c_bf, state, contract, preferred_element_type=F32)
    base = carried * decay_full + skip_ref[...] * x_conv
    for j in range(heads):
        gap = jnp.minimum(log_decay[:, j:j + 1] - log_rows[j:j + 1, :], 0.0)
        weight = (scores * jnp.exp(gap)).astype(BF)
        cols = slice(j * dim, (j + 1) * dim)
        y_ref[:, cols] = (base[:, cols] + dot(weight, scaled[:, cols])).astype(BF)


def scan(x_proj, bc, dt_raw, place, spread, tail_x, taps_x, tail_bc, taps_bc, bias, rate, skip, state):
    rows, channels = x_proj.shape
    heads = dt_raw.shape[1]
    half = bc.shape[1] // 2
    args = (x_proj, bc, dt_raw, place, spread, tail_x, taps_x, tail_bc, taps_bc, bias, rate, skip, state)
    shapes = [
        jax.ShapeDtypeStruct((rows, channels), BF),
        jax.ShapeDtypeStruct((rows, channels), BF),
        jax.ShapeDtypeStruct((rows, half), BF),
        jax.ShapeDtypeStruct((1, heads), F32),
    ]
    return pl.pallas_call(
        scan_kernel,
        in_specs=[whole(a.shape) for a in args],
        out_specs=[whole(s.shape) for s in shapes],
        out_shape=shapes,
        grid=(1,),
        scratch_shapes=[
            pltpu.VMEM((rows + 8, channels), F32),
            pltpu.VMEM((rows + 8, 2 * half), F32),
            pltpu.VMEM((rows, channels), BF),
        ],
        compiler_params=params(),
        cost_estimate=cost(2 * rows * channels * (rows + half), 8 * rows * channels + 4 * state.size),
    )(*args)


def state_kernel(active_ref, end_ref, weighted_ref, b_ref, state_ref, kept_ref, out_ref):
    heads, dim, width = state_ref.shape

    @pl.when(active_ref[0] == 1)
    def _():
        added = lax.dot_general(
            weighted_ref[...], b_ref[...], (((0,), (0,)), ((), ())), preferred_element_type=F32
        )
        for j in range(heads):
            out_ref[j] = end_ref[0, j] * state_ref[j] + added[j * dim:(j + 1) * dim, :]

    @pl.when(active_ref[0] == 0)
    def _():
        out_ref[...] = kept_ref[...]


def state_update(active, end, weighted, b_mat, state, kept):
    smem = pl.BlockSpec(memory_space=pltpu.SMEM)
    return pl.pallas_call(
        state_kernel,
        grid=(1,),
        in_specs=[smem, smem, whole(weighted.shape), whole(b_mat.shape), whole(state.shape), whole(state.shape)],
        out_specs=whole(state.shape),
        out_shape=jax.ShapeDtypeStruct(state.shape, F32),
        compiler_params=params(),
        cost_estimate=cost(2 * weighted.size * b_mat.shape[1], 12 * state.size),
    )(active, end, weighted, b_mat, state, kept)


def out_kernel(y_ref, order_ref, w_ref, p_ref, sorted_ref):
    @pl.when(pl.program_id(0) == 0)
    def _():
        sorted_ref[...] = dot(order_ref[...], y_ref[...]).astype(BF)

    p_ref[...] = dot(sorted_ref[...], w_ref[...]).astype(BF)


def project_out(y, order, w_out, part, parts):
    rows, depth = y.shape
    cols = w_out.shape[1] // parts
    block = min(1024, cols)
    first = part * (cols // block)
    return pl.pallas_call(
        out_kernel,
        grid=(cols // block,),
        in_specs=[whole(y.shape), whole(order.shape), pl.BlockSpec((depth, block), lambda i: (0, first + i))],
        out_specs=pl.BlockSpec((rows, block), lambda i: (0, i)),
        out_shape=jax.ShapeDtypeStruct((rows, cols), BF),
        scratch_shapes=[pltpu.VMEM((rows, depth), BF)],
        compiler_params=params(),
        cost_estimate=cost(2 * rows * depth * cols, 2 * depth * cols),
    )(y, order, w_out)


def rms_rows(rows_in, gain):
    floats = rows_in.astype(F32)
    scaled = floats * lax.rsqrt(jnp.mean(floats * floats, axis=-1, keepdims=True) + 1e-05)
    return (scaled * gain[None, :]).astype(BF)


def per_device(hidden, norm_gain, w_x, w_bc, w_dt, conv_x, conv_bc, dt_bias, a_rate, d_skip, w_out,
               ssm_init, conv_x_init, conv_bc_init):
    segment = lax.axis_index("pipe")
    segments = lax.axis_size("pipe")
    head = lax.axis_index("head")
    devices = lax.axis_size("head")
    chips = devices // 2
    micro, local, width = hidden.shape
    own_rows = micro * local
    rows = own_rows * devices
    half = rows // 2
    local_heads = dt_bias.shape[1]
    channels = w_x.shape[2]
    bc_cols = w_bc.shape[2]
    span = bc_cols // GROUPS

    sources = relative_devices(-1)
    targets = relative_devices(1)

    def token_of(devs):
        ids = jnp.arange(micro)[:, None] * (local * devices) + jnp.arange(local)[None, :]
        return (devs[:, :, None, None] * local + ids).reshape(-1)

    tokens = jnp.arange(rows)
    gather_order = (tokens[:, None] == token_of(sources)[None, :]).astype(BF)
    scatter_order = (token_of(targets)[:, None] == tokens[None, :]).astype(BF)
    group_of = targets * GROUPS // devices
    lanes = jnp.arange(span) * GROUPS
    columns = jnp.arange(bc_cols)
    none = jnp.full((chips, span), -1)
    same_lane = jnp.stack([group_of[0][:, None] + lanes[None, :], none], axis=1).reshape(-1)
    cross_lane = jnp.stack([none, group_of[1][:, None] + lanes[None, :]], axis=1).reshape(-1)
    same_pick = (columns[:, None] == same_lane[None, :]).astype(BF)
    cross_pick = (columns[:, None] == cross_lane[None, :]).astype(BF)
    place_of = (sources.T[:, :, None] * span + jnp.arange(span)[None, None, :]).reshape(-1)
    place = (place_of[:, None] == jnp.arange(2 * STATE)[None, :]).astype(BF)
    spread = (jnp.arange(local_heads)[:, None] == (jnp.arange(channels) // (channels // local_heads))[None, :]).astype(F32)

    my_group = head * GROUPS // devices
    tail_bc = lax.dynamic_index_in_dim(conv_bc_init[0].reshape(-1, 2 * STATE, GROUPS), my_group, 2, keepdims=False)
    taps_bc = lax.dynamic_index_in_dim(conv_bc[0].reshape(-1, 2 * STATE, GROUPS), my_group, 2, keepdims=False)
    skip = jnp.repeat(d_skip[0], channels // local_heads)[None, :]

    current = hidden.reshape(own_rows, width)
    out_rows = jnp.zeros((own_rows, width), BF)
    state_out = ssm_init[0]
    for tick in range(segments):
        active = segment == tick
        flag = active.astype(jnp.int32).reshape(1)
        normed = rms_rows(current, norm_gain[0])
        pieces = [normed] + [ring_shift(normed, s) for s in range(1, chips)]
        gathered = jnp.concatenate(pieces, axis=0)
        gathered_other = core_swap(gathered)
        normed_all, dt_raw, bc_same, bc_cross = project_first(
            gathered, gathered_other, gather_order, same_pick, cross_pick, w_bc[0], w_dt[0]
        )
        bc_pair = bc_same + core_swap(bc_cross)
        bc_parts = [bc_pair[:, s * 2 * span:(s + 1) * 2 * span] for s in range(chips)]
        bc_parts = [bc_parts[0]] + [ring_shift(bc_parts[s], s) for s in range(1, chips)]
        bc_rel = jnp.concatenate(bc_parts, axis=1)
        x_proj = project_inner(normed_all, w_x[0])
        y, weighted, b_mat, end = scan(
            x_proj, bc_rel, dt_raw, place, spread, conv_x_init[0], conv_x[0], tail_bc, taps_bc,
            dt_bias, a_rate, skip, ssm_init[0],
        )
        state_out = state_update(flag, end, weighted, b_mat, ssm_init[0], state_out)
        new_parts = []
        part_cols = width // OUT_PARTS
        for part in range(OUT_PARTS):
            partial = project_out(y, scatter_order, w_out[0], part, OUT_PARTS)
            received = core_swap(partial[half:])
            pair = (partial[:half].astype(F32) + received.astype(F32)).astype(BF)
            moved = [ring_shift(pair[s * own_rows:(s + 1) * own_rows], s) for s in range(1, chips)]
            total = pair[:own_rows].astype(F32)
            for piece in moved:
                total = total + piece.astype(F32)
            new_parts.append(total)
        summed = jnp.concatenate(new_parts, axis=1)
        new_rows = (current.astype(F32) + summed).astype(BF)
        out_rows = jnp.where(active, new_rows, out_rows)
        if tick + 1 < segments:
            current = next_segment(new_rows, tick)
    return (out_rows.reshape(1, micro, local, width), state_out[None])


def solution(mesh):
    in_specs = (
        P(None, "head", None),
        P("pipe", None),
        P("pipe", None, "head"),
        P("pipe", None, "head"),
        P("pipe", None, "head"),
        P("pipe", None, "head"),
        P("pipe", None, None),
        P("pipe", "head"),
        P("pipe", "head"),
        P("pipe", "head"),
        P("pipe", "head", None),
        P("pipe", "head", None, None),
        P("pipe", None, "head"),
        P("pipe", None, None),
    )
    out_specs = (P("pipe", None, "head", None), P("pipe", "head", None, None))
    return jax.shard_map(
        per_device, mesh=mesh, in_specs=in_specs, out_specs=out_specs, check_vma=False
    )
```

time: 831 us -> 374 us (0.45)
  matrix products: 285 us -> 0 us
  waiting for transfers between devices: 358 us -> 94.3 us
  Pallas kernels: 0 us -> 175 us
  starting transfers between devices: 16.5 us -> 74.4 us
  local copies, waits for them, and re-layouts: 63.2 us -> 12.8 us
  blocking collectives: 46.1 us -> 0 us
  other arithmetic: 38.9 us -> 10.1 us
  between operations: 15.6 us -> 2.23 us
    dot_general x50 -> x0, matrix products: 285 us -> none  [the longest x5 73.8 us: per_device(): jnp.dot(mixed_bf, out_weight, preferred_element_type=jnp.float32)]
    psum x5 -> x0, waiting for transfers between devices: 268 us -> none  [per_device(): lax.psum(jnp.dot(mixed_bf, out_weight, preferred_element_type=jnp.float32...]
    pallas_call x0 -> x24, Pallas kernels: none -> 175 us  [the longest x8 61.8 us: project_out(): pl.pallas_call(out_kernel, grid=(cols // block,), in_specs=[whole(y.shape...]
    ppermute x4 -> x67, waiting for transfers between devices: 10.9 us -> 94.3 us  [the longest x48 66.8 us: ring_shift(): return lax.ppermute(value, 'head', pairs)]
    all_gather x5 -> x0, waiting for transfers between devices: 77.2 us -> none  [per_device(): entry_rows = lax.all_gather(own_rows, 'head', axis=0, tiled=True)]
    ppermute x4 -> x67, starting transfers between devices: 16.1 us -> 74.4 us  [the longest x48 58.1 us: ring_shift(): return lax.ppermute(value, 'head', pairs)]
    all_gather x5 -> x0, blocking collectives: 46.1 us -> none  [mix_block(): bc_all = lax.all_gather(bc_part, 'head', axis=1, tiled=True)]
    unnamed x115 -> x64, local copies, waits for them, and re-layouts: 23 us -> 2.91 us
  transfers between devices with their start and end apart: 14 -> 67, of which waited for: 14 -> 44; matrix products, arithmetic and copies ran while one was open for 6% -> 4% of each run, Pallas kernels for 0% -> 24%
where the time goes in v1:
time: 374 us; the launch traced here: 369 us
  Pallas kernels  175 us (47%)
  waiting for transfers between devices  94.3 us (25%)
  starting transfers between devices  74.4 us (20%)
  local copies, waits for them, and re-layouts  12.8 us (3%)
  other arithmetic  10.1 us (3%)
    ppermute x48, waiting for transfers between devices, ring_shift(): return lax.ppermute(value, 'head', pairs)  66.8 us
    pallas_call x8, Pallas kernels, project_out(): pl.pallas_call(out_kernel, grid=(cols // block,), in_specs=[whole(y.shape...  61.8 us
    ppermute x48, starting transfers between devices, ring_shift(): return lax.ppermute(value, 'head', pairs)  58.1 us
    pallas_call x4, Pallas kernels, project_inner(): pl.pallas_call(inner_kernel, grid=(cols // block,), in_specs=[whole(norme...  54.9 us
    pallas_call x4, Pallas kernels, project_first(): pl.pallas_call(first_kernel, grid=(bc_cols // block,), in_specs=[whole(ow...  36.6 us
    pallas_call x4, Pallas kernels, scan(): pl.pallas_call(scan_kernel, in_specs=[whole(a.shape) for a in args], out_...  17.2 us
    ppermute x16, waiting for transfers between devices, core_swap(): return lax.ppermute(value, 'head', [(i, i ^ 1) for i in range(count)])  14.5 us
    ppermute x3, waiting for transfers between devices, next_segment(): return lax.ppermute(value, 'pipe', pairs)  13 us
  transfers between devices with their start and end apart: 67, of which 44 were waited for; matrix products, arithmetic and copies ran while one was open for 4% of the time, Pallas kernels for 24%

profile of v1, /device:TPU:0, one launch (start us, length us, event | category | flops | bytes accessed | tf_op | source)
XLA Modules:
  0.0 368.7 jit_solution(7714602763572527159)
XLA Ops:
  24.3 9.2 %shard_map.185 = (bf16[128,8192]{1,0:T(8,128)(2,1)S(1)}, f32[128,32]{1,0:T(8,128)S(1)}, bf16[128,512]{1,0:T(8,128)(2,1)S(1)}, bf16[128,512]{1,0:T(8,128)(2,1)S(1)}) custom-call(bf16[64,8192]{1,0:T(8,128)(2,1)S(1)} %pad_maximum_fusion.own_ref, bf16[64,8192]{1,0:T(8,128)(2,1)S(1)} %collective-permute-done.3.other_ref, bf16[128,128]{1,0:T(8,128)(2,1)S(1)} %fusion.24.order_ref, ...), custom_call_target="tpu_custom_call" | custom-call | flops 1140850688 | bytes 12582912 | tf_op jit(solution)/shard_map/pallas_call | solution.py:114
  39.0 13.9 %shard_map.186.x_ref = f32[128,2048]{1,0:T(8,128)S(1)} custom-call(bf16[128,8192]{1,0:T(8,128)(2,1)S(1)} %get-tuple-element.34.normed_ref, bf16[8192,2048]{1,0:T(8,128)(2,1)} %bitcast.68), custom_call_target="tpu_custom_call" | custom-call | flops 4294967296 | bytes 35651584 | tf_op jit(solution)/shard_map/pallas_call | solution.py:146
  52.9 4.3 %shard_map.187 = (bf16[128,2048]{1,0:T(8,128)(2,1)S(1)}, bf16[128,2048]{1,0:T(8,128)(2,1)S(1)}, bf16[128,256]{1,0:T(8,128)(2,1)S(1)}, f32[1,32]{1,0:T(1,128)S(1)}) custom-call(f32[128,2048]{1,0:T(8,128)S(1)} %shard_map.186.x_ref, bf16[128,512]{1,0:T(8,128)(2,1)S(1)} %pad_maximum_fusion.4.bc_ref, f32[128,32]{1,0:T(8,128)S(1)} %get-tuple-element.37.dt_ref, ...), custom_call_target="tpu_custom_call" | custom-call | flops 201326592 | bytes 4194304 | tf_op jit(solution)/shard_map/pallas_call | solution.py:223
  57.3 7.8 %shard_map.189 = bf16[128,4096]{1,0:T(8,128)(2,1)S(1)} custom-call(bf16[128,2048]{1,0:T(8,128)(2,1)S(1)} %get-tuple-element.38.y_ref, bf16[128,128]{1,0:T(8,128)(2,1)S(1)} %fusion.25.order_ref, bf16[2048,8192]{1,0:T(8,128)(2,1)} %bitcast.60), custom_call_target="tpu_custom_call" | custom-call | flops 2147483648 | bytes 16777216 | tf_op jit(solution)/shard_map/pallas_call | solution.py:281
  65.2 7.6 %shard_map.188 = bf16[128,4096]{1,0:T(8,128)(2,1)S(1)} custom-call(bf16[128,2048]{1,0:T(8,128)(2,1)S(1)} %get-tuple-element.38.y_ref, bf16[128,128]{1,0:T(8,128)(2,1)S(1)} %fusion.25.order_ref, bf16[2048,8192]{1,0:T(8,128)(2,1)} %bitcast.61), custom_call_target="tpu_custom_call" | custom-call | flops 2147483648 | bytes 16777216 | tf_op jit(solution)/shard_map/pallas_call | solution.py:281
  81.5 3.4 collective-permute-done.13
  90.5 6.6 %collective-permute-done.16 = bf16[16,8192]{1,0:T(8,128)(2,1)S(1)} collective-permute-done((bf16[16,8192]{1,0:T(8,128)(2,1)S(1)}, bf16[16,8192]{1,0:T(8,128)(2,1)S(1)}, u32[]{:S(2)}, u32[]{:S(2)}) %collective-permute-start.16) | collective-permute-done | bytes 262176 | tf_op jit(solution)/shard_map/ppermute | solution.py:59
  101.1 5.7 %collective-permute-done.19 = bf16[16,8192]{1,0:T(8,128)(2,1)S(1)} collective-permute-done((bf16[16,8192]{1,0:T(8,128)(2,1)S(1)}, bf16[16,8192]{1,0:T(8,128)(2,1)S(1)}, u32[]{:S(2)}, u32[]{:S(2)}) %collective-permute-start.19) | collective-permute-done | bytes 262176 | tf_op jit(solution)/shard_map/ppermute | solution.py:51
  107.7 3.7 collective-permute-done.17
  114.2 9.2 %shard_map.190 = (bf16[128,8192]{1,0:T(8,128)(2,1)S(1)}, f32[128,32]{1,0:T(8,128)S(1)}, bf16[128,512]{1,0:T(8,128)(2,1)S(1)}, bf16[128,512]{1,0:T(8,128)(2,1)S(1)}) custom-call(bf16[64,8192]{1,0:T(8,128)(2,1)S(1)} %pad_maximum_fusion.1.own_ref, bf16[64,8192]{1,0:T(8,128)(2,1)S(1)} %collective-permute-done.20.other_ref, ...), custom_call_target="tpu_custom_call" | custom-call | flops 1140850688 | bytes 12582912 | tf_op jit(solution)/shard_map/pallas_call | solution.py:114
  128.7 13.7 %shard_map.191.x_ref = f32[128,2048]{1,0:T(8,128)S(1)} custom-call(bf16[128,8192]{1,0:T(8,128)(2,1)S(1)} %get-tuple-element.39.normed_ref, bf16[8192,2048]{1,0:T(8,128)(2,1)} %bitcast.69), custom_call_target="tpu_custom_call" | custom-call | flops 4294967296 | bytes 35651584 | tf_op jit(solution)/shard_map/pallas_call | solution.py:146
  142.4 4.3 %shard_map.192 = (bf16[128,2048]{1,0:T(8,128)(2,1)S(1)}, bf16[128,2048]{1,0:T(8,128)(2,1)S(1)}, bf16[128,256]{1,0:T(8,128)(2,1)S(1)}, f32[1,32]{1,0:T(1,128)S(1)}) custom-call(f32[128,2048]{1,0:T(8,128)S(1)} %shard_map.191.x_ref, bf16[128,512]{1,0:T(8,128)(2,1)S(1)} %pad_maximum_fusion.5.bc_ref, f32[128,32]{1,0:T(8,128)S(1)} %get-tuple-element.42.dt_ref, ...), custom_call_target="tpu_custom_call" | custom-call | flops 201326592 | bytes 4194304 | tf_op jit(solution)/shard_map/pallas_call | solution.py:223
  146.8 7.8 %shard_map.194 = bf16[128,4096]{1,0:T(8,128)(2,1)S(1)} custom-call(bf16[128,2048]{1,0:T(8,128)(2,1)S(1)} %get-tuple-element.43.y_ref, bf16[128,128]{1,0:T(8,128)(2,1)S(1)} %fusion.25.order_ref, bf16[2048,8192]{1,0:T(8,128)(2,1)} %bitcast.62), custom_call_target="tpu_custom_call" | custom-call | flops 2147483648 | bytes 16777216 | tf_op jit(solution)/shard_map/pallas_call | solution.py:281
  154.7 7.6 %shard_map.193 = bf16[128,4096]{1,0:T(8,128)(2,1)S(1)} custom-call(bf16[128,2048]{1,0:T(8,128)(2,1)S(1)} %get-tuple-element.43.y_ref, bf16[128,128]{1,0:T(8,128)(2,1)S(1)} %fusion.25.order_ref, bf16[2048,8192]{1,0:T(8,128)(2,1)} %bitcast.63), custom_call_target="tpu_custom_call" | custom-call | flops 2147483648 | bytes 16777216 | tf_op jit(solution)/shard_map/pallas_call | solution.py:281
  182.8 5.8 %collective-permute-done.36 = bf16[16,8192]{1,0:T(8,128)(2,1)S(1)} collective-permute-done((bf16[16,8192]{1,0:T(8,128)(2,1)S(1)}, bf16[16,8192]{1,0:T(8,128)(2,1)S(1)}, u32[]{:S(2)}, u32[]{:S(2)}) %collective-permute-start.36) | collective-permute-done | bytes 262176 | tf_op jit(solution)/shard_map/ppermute | solution.py:51
  190.2 4.1 %collective-permute-done.34 = bf16[16,8192]{1,0:T(8,128)(2,1)S(1)} collective-permute-done((bf16[16,8192]{1,0:T(8,128)(2,1)S(1)}, bf16[16,8192]{1,0:T(8,128)(2,1)S(1)}, u32[]{:S(2)}, u32[]{:S(2)}) %collective-permute-start.34) | collective-permute-done | bytes 262176 | tf_op jit(solution)/shard_map/ppermute | solution.py:51
  197.0 9.2 %shard_map.195 = (bf16[128,8192]{1,0:T(8,128)(2,1)S(1)}, f32[128,32]{1,0:T(8,128)S(1)}, bf16[128,512]{1,0:T(8,128)(2,1)S(1)}, bf16[128,512]{1,0:T(8,128)(2,1)S(1)}) custom-call(bf16[64,8192]{1,0:T(8,128)(2,1)S(1)} %pad_maximum_fusion.2.own_ref, bf16[64,8192]{1,0:T(8,128)(2,1)S(1)} %collective-permute-done.37.other_ref, ...), custom_call_target="tpu_custom_call" | custom-call | flops 1140850688 | bytes 12582912 | tf_op jit(solution)/shard_map/pallas_call | solution.py:114
  211.2 13.7 %shard_map.196.x_ref = f32[128,2048]{1,0:T(8,128)S(1)} custom-call(bf16[128,8192]{1,0:T(8,128)(2,1)S(1)} %get-tuple-element.44.normed_ref, bf16[8192,2048]{1,0:T(8,128)(2,1)} %bitcast.70), custom_call_target="tpu_custom_call" | custom-call | flops 4294967296 | bytes 35651584 | tf_op jit(solution)/shard_map/pallas_call | solution.py:146
  224.9 4.3 %shard_map.197 = (bf16[128,2048]{1,0:T(8,128)(2,1)S(1)}, bf16[128,2048]{1,0:T(8,128)(2,1)S(1)}, bf16[128,256]{1,0:T(8,128)(2,1)S(1)}, f32[1,32]{1,0:T(1,128)S(1)}) custom-call(f32[128,2048]{1,0:T(8,128)S(1)} %shard_map.196.x_ref, bf16[128,512]{1,0:T(8,128)(2,1)S(1)} %pad_maximum_fusion.6.bc_ref, f32[128,32]{1,0:T(8,128)S(1)} %get-tuple-element.47.dt_ref, ...), custom_call_target="tpu_custom_call" | custom-call | flops 201326592 | bytes 4194304 | tf_op jit(solution)/shard_map/pallas_call | solution.py:223
  229.3 7.8 %shard_map.199 = bf16[128,4096]{1,0:T(8,128)(2,1)S(1)} custom-call(bf16[128,2048]{1,0:T(8,128)(2,1)S(1)} %get-tuple-element.48.y_ref, bf16[128,128]{1,0:T(8,128)(2,1)S(1)} %fusion.25.order_ref, bf16[2048,8192]{1,0:T(8,128)(2,1)} %bitcast.64), custom_call_target="tpu_custom_call" | custom-call | flops 2147483648 | bytes 16777216 | tf_op jit(solution)/shard_map/pallas_call | solution.py:281
  237.2 7.6 %shard_map.198 = bf16[128,4096]{1,0:T(8,128)(2,1)S(1)} custom-call(bf16[128,2048]{1,0:T(8,128)(2,1)S(1)} %get-tuple-element.48.y_ref, bf16[128,128]{1,0:T(8,128)(2,1)S(1)} %fusion.25.order_ref, bf16[2048,8192]{1,0:T(8,128)(2,1)} %bitcast.65), custom_call_target="tpu_custom_call" | custom-call | flops 2147483648 | bytes 16777216 | tf_op jit(solution)/shard_map/pallas_call | solution.py:281
  253.5 3.5 collective-permute-done.47
  260.8 10.3 %collective-permute-start.50 = (bf16[16,8192]{1,0:T(8,128)(2,1)S(1)}, bf16[16,8192]{1,0:T(8,128)(2,1)S(1)}, u32[]{:S(2)}, u32[]{:S(2)}) collective-permute-start(bf16[16,8192]{1,0:T(8,128)(2,1)S(1)} %fusion.16), channel_id=1, source_target_pairs={{0,8},{8,0},{16,24},{24,16},{1,9},{9,1},{17,25},{25,17},{2,10},{10... | collective-permute-start | bytes 786440 | tf_op jit(solution)/shard_map/ppermute | solution.py:59
  271.1 6.4 %collective-permute-done.50 = bf16[16,8192]{1,0:T(8,128)(2,1)S(1)} collective-permute-done((bf16[16,8192]{1,0:T(8,128)(2,1)S(1)}, bf16[16,8192]{1,0:T(8,128)(2,1)S(1)}, u32[]{:S(2)}, u32[]{:S(2)}) %collective-permute-start.50) | collective-permute-done | bytes 262176 | tf_op jit(solution)/shard_map/ppermute | solution.py:59
  281.6 5.5 %collective-permute-done.53 = bf16[16,8192]{1,0:T(8,128)(2,1)S(1)} collective-permute-done((bf16[16,8192]{1,0:T(8,128)(2,1)S(1)}, bf16[16,8192]{1,0:T(8,128)(2,1)S(1)}, u32[]{:S(2)}, u32[]{:S(2)}) %collective-permute-start.53) | collective-permute-done | bytes 262176 | tf_op jit(solution)/shard_map/ppermute | solution.py:51
  288.2 3.9 %collective-permute-done.51 = bf16[16,8192]{1,0:T(8,128)(2,1)S(1)} collective-permute-done((bf16[16,8192]{1,0:T(8,128)(2,1)S(1)}, bf16[16,8192]{1,0:T(8,128)(2,1)S(1)}, u32[]{:S(2)}, u32[]{:S(2)}) %collective-permute-start.51) | collective-permute-done | bytes 262176 | tf_op jit(solution)/shard_map/ppermute | solution.py:51
  294.9 9.1 %shard_map.200 = (bf16[128,8192]{1,0:T(8,128)(2,1)S(1)}, f32[128,32]{1,0:T(8,128)S(1)}, bf16[128,512]{1,0:T(8,128)(2,1)S(1)}, bf16[128,512]{1,0:T(8,128)(2,1)S(1)}) custom-call(bf16[64,8192]{1,0:T(8,128)(2,1)S(1)} %pad_maximum_fusion.3.own_ref, bf16[64,8192]{1,0:T(8,128)(2,1)S(1)} %collective-permute-done.54.other_ref, ...), custom_call_target="tpu_custom_call" | custom-call | flops 1140850688 | bytes 12582912 | tf_op jit(solution)/shard_map/pallas_call | solution.py:114
  309.7 13.7 %shard_map.201.x_ref = f32[128,2048]{1,0:T(8,128)S(1)} custom-call(bf16[128,8192]{1,0:T(8,128)(2,1)S(1)} %get-tuple-element.49.normed_ref, bf16[8192,2048]{1,0:T(8,128)(2,1)} %bitcast.71), custom_call_target="tpu_custom_call" | custom-call | flops 4294967296 | bytes 35651584 | tf_op jit(solution)/shard_map/pallas_call | solution.py:146
  323.4 4.3 %shard_map.202 = (bf16[128,2048]{1,0:T(8,128)(2,1)S(1)}, bf16[128,2048]{1,0:T(8,128)(2,1)S(1)}, bf16[128,256]{1,0:T(8,128)(2,1)S(1)}, f32[1,32]{1,0:T(1,128)S(1)}) custom-call(f32[128,2048]{1,0:T(8,128)S(1)} %shard_map.201.x_ref, bf16[128,512]{1,0:T(8,128)(2,1)S(1)} %pad_maximum_fusion.7.bc_ref, f32[128,32]{1,0:T(8,128)S(1)} %get-tuple-element.52.dt_ref, ...), custom_call_target="tpu_custom_call" | custom-call | flops 201326592 | bytes 4194304 | tf_op jit(solution)/shard_map/pallas_call | solution.py:223
  327.7 8.0 %shard_map.204 = bf16[128,4096]{1,0:T(8,128)(2,1)S(1)} custom-call(bf16[128,2048]{1,0:T(8,128)(2,1)S(1)} %get-tuple-element.53.y_ref, bf16[128,128]{1,0:T(8,128)(2,1)S(1)} %fusion.25.order_ref, bf16[2048,8192]{1,0:T(8,128)(2,1)} %bitcast.66), custom_call_target="tpu_custom_call" | custom-call | flops 2147483648 | bytes 16777216 | tf_op jit(solution)/shard_map/pallas_call | solution.py:281
  340.8 7.7 %shard_map.203 = bf16[128,4096]{1,0:T(8,128)(2,1)S(1)} custom-call(bf16[128,2048]{1,0:T(8,128)(2,1)S(1)} %copy-done.4, bf16[128,128]{1,0:T(8,128)(2,1)S(1)} %fusion.25.order_ref, bf16[2048,8192]{1,0:T(8,128)(2,1)} %bitcast.67), custom_call_target="tpu_custom_call" | custom-call | flops 2147483648 | bytes 16777216 | tf_op jit(solution)/shard_map/pallas_call | solution.py:281
  360.2 3.3 collective-permute-done.64
  (294 shorter events, 133.8 us)
Async XLA Ops:
  3.0 16.4 %collective-permute-start.2 = (bf16[16,8192]{1,0:T(8,128)(2,1)S(1)}, bf16[16,8192]{1,0:T(8,128)(2,1)}, u32[]{:S(2)}, u32[]{:S(2)}) collective-permute-start(bf16[16,8192]{1,0:T(8,128)(2,1)S(1)} %fusion.6), channel_id=1, source_target_pairs={{0,4},{1,5},{2,0},{3,1},{6,2},{7,3},{4,6},{5,7},{8,12},{9,13},{10,... | collective-permute-start | bytes 786440 | tf_op jit(solution)/shard_map/ppermute | solution.py:51
  6.0 13.4 %collective-permute-start.1 = (bf16[16,8192]{1,0:T(8,128)(2,1)S(1)}, bf16[16,8192]{1,0:T(8,128)(2,1)}, u32[]{:S(2)}, u32[]{:S(2)}) collective-permute-start(bf16[16,8192]{1,0:T(8,128)(2,1)S(1)} %fusion.6), channel_id=1, source_target_pairs={{0,6},{1,7},{2,4},{3,5},{6,0},{7,1},{4,2},{5,3},{8,14},{9,15},{10,... | collective-permute-start | bytes 786440 | tf_op jit(solution)/shard_map/ppermute | solution.py:51
  7.5 13.0 %collective-permute-start = (bf16[16,8192]{1,0:T(8,128)(2,1)S(1)}, bf16[16,8192]{1,0:T(8,128)(2,1)}, u32[]{:S(2)}, u32[]{:S(2)}) collective-permute-start(bf16[16,8192]{1,0:T(8,128)(2,1)S(1)} %fusion.6), channel_id=1, source_target_pairs={{0,2},{1,3},{2,6},{3,7},{6,4},{7,5},{4,0},{5,1},{8,10},{9,11},{10,... | collective-permute-start | bytes 786440 | tf_op jit(solution)/shard_map/ppermute | solution.py:51
  35.0 17.8 %collective-permute-start.7 = (bf16[128,128]{1,0:T(8,128)(2,1)S(1)}, bf16[128,128]{1,0:T(8,128)(2,1)S(1)}, u32[]{:S(2)}, u32[]{:S(2)}) collective-permute-start(bf16[128,128]{1,0:T(8,128)(2,1)S(1)} %get-tuple-element.103), channel_id=1, source_target_pairs={{0,4},{1,5},{2,0},{3,1},{6,2},{7,3},{4,6},{5,7},{8,12},{9,13},{10,... | collective-permute-start | bytes 98312 | tf_op jit(solution)/shard_map/ppermute | solution.py:51
  35.6 17.2 %collective-permute-start.6 = (bf16[128,128]{1,0:T(8,128)(2,1)S(1)}, bf16[128,128]{1,0:T(8,128)(2,1)S(1)}, u32[]{:S(2)}, u32[]{:S(2)}) collective-permute-start(bf16[128,128]{1,0:T(8,128)(2,1)S(1)} %get-tuple-element.104), channel_id=1, source_target_pairs={{0,6},{1,7},{2,4},{3,5},{6,0},{7,1},{4,2},{5,3},{8,14},{9,15},{10,... | collective-permute-start | bytes 98312 | tf_op jit(solution)/shard_map/ppermute | solution.py:51
  37.1 15.8 %collective-permute-start.5 = (bf16[128,128]{1,0:T(8,128)(2,1)S(1)}, bf16[128,128]{1,0:T(8,128)(2,1)S(1)}, u32[]{:S(2)}, u32[]{:S(2)}) collective-permute-start(bf16[128,128]{1,0:T(8,128)(2,1)S(1)} %get-tuple-element.105), channel_id=1, source_target_pairs={{0,2},{1,3},{2,6},{3,7},{6,4},{7,5},{4,0},{5,1},{8,10},{9,11},{10,... | collective-permute-start | bytes 98312 | tf_op jit(solution)/shard_map/ppermute | solution.py:51
  75.7 9.2 %collective-permute-start.13 = (bf16[16,4096]{1,0:T(8,128)(2,1)S(1)}, bf16[16,4096]{1,0:T(8,128)(2,1)S(1)}, u32[]{:S(2)}, u32[]{:S(2)}) collective-permute-start(bf16[16,4096]{1,0:T(8,128)(2,1)S(1)} %get-tuple-element.87), channel_id=1, source_target_pairs={{0,2},{1,3},{2,6},{3,7},{6,4},{7,5},{4,0},{5,1},{8,10},{9,11},{10,... | collective-permute-start | bytes 393224 | tf_op jit(solution)/shard_map/ppermute | solution.py:51
  97.4 9.3 %collective-permute-start.19 = (bf16[16,8192]{1,0:T(8,128)(2,1)S(1)}, bf16[16,8192]{1,0:T(8,128)(2,1)S(1)}, u32[]{:S(2)}, u32[]{:S(2)}) collective-permute-start(bf16[16,8192]{1,0:T(8,128)(2,1)S(1)} %fusion.11), channel_id=1, source_target_pairs={{0,4},{1,5},{2,0},{3,1},{6,2},{7,3},{4,6},{5,7},{8,12},{9,13},{10,... | collective-permute-start | bytes 786440 | tf_op jit(solution)/shard_map/ppermute | solution.py:51
  97.5 10.3 %collective-permute-start.18 = (bf16[16,8192]{1,0:T(8,128)(2,1)S(1)}, bf16[16,8192]{1,0:T(8,128)(2,1)S(1)}, u32[]{:S(2)}, u32[]{:S(2)}) collective-permute-start(bf16[16,8192]{1,0:T(8,128)(2,1)S(1)} %fusion.11), channel_id=1, source_target_pairs={{0,6},{1,7},{2,4},{3,5},{6,0},{7,1},{4,2},{5,3},{8,14},{9,15},{10,... | collective-permute-start | bytes 786440 | tf_op jit(solution)/shard_map/ppermute | solution.py:51
  99.1 12.3 %collective-permute-start.17 = (bf16[16,8192]{1,0:T(8,128)(2,1)S(1)}, bf16[16,8192]{1,0:T(8,128)(2,1)S(1)}, u32[]{:S(2)}, u32[]{:S(2)}) collective-permute-start(bf16[16,8192]{1,0:T(8,128)(2,1)S(1)} %fusion.11), channel_id=1, source_target_pairs={{0,2},{1,3},{2,6},{3,7},{6,4},{7,5},{4,0},{5,1},{8,10},{9,11},{10,... | collective-permute-start | bytes 786440 | tf_op jit(solution)/shard_map/ppermute | solution.py:51
  124.9 17.5 %collective-permute-start.24 = (bf16[128,128]{1,0:T(8,128)(2,1)S(1)}, bf16[128,128]{1,0:T(8,128)(2,1)S(1)}, u32[]{:S(2)}, u32[]{:S(2)}) collective-permute-start(bf16[128,128]{1,0:T(8,128)(2,1)S(1)} %get-tuple-element.99), channel_id=1, source_target_pairs={{0,4},{1,5},{2,0},{3,1},{6,2},{7,3},{4,6},{5,7},{8,12},{9,13},{10,... | collective-permute-start | bytes 98312 | tf_op jit(solution)/shard_map/ppermute | solution.py:51
  125.5 16.9 %collective-permute-start.23 = (bf16[128,128]{1,0:T(8,128)(2,1)S(1)}, bf16[128,128]{1,0:T(8,128)(2,1)S(1)}, u32[]{:S(2)}, u32[]{:S(2)}) collective-permute-start(bf16[128,128]{1,0:T(8,128)(2,1)S(1)} %get-tuple-element.100), channel_id=1, source_target_pairs={{0,6},{1,7},{2,4},{3,5},{6,0},{7,1},{4,2},{5,3},{8,14},{9,15},{10,... | collective-permute-start | bytes 98312 | tf_op jit(solution)/shard_map/ppermute | solution.py:51
  127.1 15.3 %collective-permute-start.22 = (bf16[128,128]{1,0:T(8,128)(2,1)S(1)}, bf16[128,128]{1,0:T(8,128)(2,1)S(1)}, u32[]{:S(2)}, u32[]{:S(2)}) collective-permute-start(bf16[128,128]{1,0:T(8,128)(2,1)S(1)} %get-tuple-element.101), channel_id=1, source_target_pairs={{0,2},{1,3},{2,6},{3,7},{6,4},{7,5},{4,0},{5,1},{8,10},{9,11},{10,... | collective-permute-start | bytes 98312 | tf_op jit(solution)/shard_map/ppermute | solution.py:51
  165.0 9.3 %collective-permute-start.30 = (bf16[16,4096]{1,0:T(8,128)(2,1)S(1)}, bf16[16,4096]{1,0:T(8,128)(2,1)S(1)}, u32[]{:S(2)}, u32[]{:S(2)}) collective-permute-start(bf16[16,4096]{1,0:T(8,128)(2,1)S(1)} %get-tuple-element.81), channel_id=1, source_target_pairs={{0,2},{1,3},{2,6},{3,7},{6,4},{7,5},{4,0},{5,1},{8,10},{9,11},{10,... | collective-permute-start | bytes 393224 | tf_op jit(solution)/shard_map/ppermute | solution.py:51
  167.3 9.3 %collective-permute-start.27 = (bf16[16,4096]{1,0:T(8,128)(2,1)S(1)}, bf16[16,4096]{1,0:T(8,128)(2,1)S(1)}, u32[]{:S(2)}, u32[]{:S(2)}) collective-permute-start(bf16[16,4096]{1,0:T(8,128)(2,1)S(1)} %get-tuple-element.80), channel_id=1, source_target_pairs={{0,6},{1,7},{2,4},{3,5},{6,0},{7,1},{4,2},{5,3},{8,14},{9,15},{10,... | collective-permute-start | bytes 393224 | tf_op jit(solution)/shard_map/ppermute | solution.py:51
  179.4 9.2 %collective-permute-start.36 = (bf16[16,8192]{1,0:T(8,128)(2,1)S(1)}, bf16[16,8192]{1,0:T(8,128)(2,1)S(1)}, u32[]{:S(2)}, u32[]{:S(2)}) collective-permute-start(bf16[16,8192]{1,0:T(8,128)(2,1)S(1)} %fusion.15), channel_id=1, source_target_pairs={{0,4},{1,5},{2,0},{3,1},{6,2},{7,3},{4,6},{5,7},{8,12},{9,13},{10,... | collective-permute-start | bytes 786440 | tf_op jit(solution)/shard_map/ppermute | solution.py:51
  180.0 10.2 %collective-permute-start.35 = (bf16[16,8192]{1,0:T(8,128)(2,1)S(1)}, bf16[16,8192]{1,0:T(8,128)(2,1)S(1)}, u32[]{:S(2)}, u32[]{:S(2)}) collective-permute-start(bf16[16,8192]{1,0:T(8,128)(2,1)S(1)} %fusion.15), channel_id=1, source_target_pairs={{0,6},{1,7},{2,4},{3,5},{6,0},{7,1},{4,2},{5,3},{8,14},{9,15},{10,... | collective-permute-start | bytes 786440 | tf_op jit(solution)/shard_map/ppermute | solution.py:51
  181.3 12.9 %collective-permute-start.34 = (bf16[16,8192]{1,0:T(8,128)(2,1)S(1)}, bf16[16,8192]{1,0:T(8,128)(2,1)S(1)}, u32[]{:S(2)}, u32[]{:S(2)}) collective-permute-start(bf16[16,8192]{1,0:T(8,128)(2,1)S(1)} %fusion.15), channel_id=1, source_target_pairs={{0,2},{1,3},{2,6},{3,7},{6,4},{7,5},{4,0},{5,1},{8,10},{9,11},{10,... | collective-permute-start | bytes 786440 | tf_op jit(solution)/shard_map/ppermute | solution.py:51
  207.7 17.2 %collective-permute-start.41 = (bf16[128,128]{1,0:T(8,128)(2,1)S(1)}, bf16[128,128]{1,0:T(8,128)(2,1)S(1)}, u32[]{:S(2)}, u32[]{:S(2)}) collective-permute-start(bf16[128,128]{1,0:T(8,128)(2,1)S(1)} %get-tuple-element.95), channel_id=1, source_target_pairs={{0,4},{1,5},{2,0},{3,1},{6,2},{7,3},{4,6},{5,7},{8,12},{9,13},{10,... | collective-permute-start | bytes 98312 | tf_op jit(solution)/shard_map/ppermute | solution.py:51
  208.3 16.6 %collective-permute-start.40 = (bf16[128,128]{1,0:T(8,128)(2,1)S(1)}, bf16[128,128]{1,0:T(8,128)(2,1)S(1)}, u32[]{:S(2)}, u32[]{:S(2)}) collective-permute-start(bf16[128,128]{1,0:T(8,128)(2,1)S(1)} %get-tuple-element.96), channel_id=1, source_target_pairs={{0,6},{1,7},{2,4},{3,5},{6,0},{7,1},{4,2},{5,3},{8,14},{9,15},{10,... | collective-permute-start | bytes 98312 | tf_op jit(solution)/shard_map/ppermute | solution.py:51
  209.6 15.3 %collective-permute-start.39 = (bf16[128,128]{1,0:T(8,128)(2,1)S(1)}, bf16[128,128]{1,0:T(8,128)(2,1)S(1)}, u32[]{:S(2)}, u32[]{:S(2)}) collective-permute-start(bf16[128,128]{1,0:T(8,128)(2,1)S(1)} %get-tuple-element.97), channel_id=1, source_target_pairs={{0,2},{1,3},{2,6},{3,7},{6,4},{7,5},{4,0},{5,1},{8,10},{9,11},{10,... | collective-permute-start | bytes 98312 | tf_op jit(solution)/shard_map/ppermute | solution.py:51
  247.9 9.2 %collective-permute-start.47 = (bf16[16,4096]{1,0:T(8,128)(2,1)S(1)}, bf16[16,4096]{1,0:T(8,128)(2,1)S(1)}, u32[]{:S(2)}, u32[]{:S(2)}) collective-permute-start(bf16[16,4096]{1,0:T(8,128)(2,1)S(1)} %get-tuple-element.75), channel_id=1, source_target_pairs={{0,2},{1,3},{2,6},{3,7},{6,4},{7,5},{4,0},{5,1},{8,10},{9,11},{10,... | collective-permute-start | bytes 393224 | tf_op jit(solution)/shard_map/ppermute | solution.py:51
  260.8 16.7 %collective-permute-start.50 = (bf16[16,8192]{1,0:T(8,128)(2,1)S(1)}, bf16[16,8192]{1,0:T(8,128)(2,1)S(1)}, u32[]{:S(2)}, u32[]{:S(2)}) collective-permute-start(bf16[16,8192]{1,0:T(8,128)(2,1)S(1)} %fusion.16), channel_id=1, source_target_pairs={{0,8},{8,0},{16,24},{24,16},{1,9},{9,1},{17,25},{25,17},{2,10},{10... | collective-permute-start | bytes 786440 | tf_op jit(solution)/shard_map/ppermute | solution.py:59
  277.9 9.3 %collective-permute-start.53 = (bf16[16,8192]{1,0:T(8,128)(2,1)S(1)}, bf16[16,8192]{1,0:T(8,128)(2,1)S(1)}, u32[]{:S(2)}, u32[]{:S(2)}) collective-permute-start(bf16[16,8192]{1,0:T(8,128)(2,1)S(1)} %fusion.19), channel_id=1, source_target_pairs={{0,4},{1,5},{2,0},{3,1},{6,2},{7,3},{4,6},{5,7},{8,12},{9,13},{10,... | collective-permute-start | bytes 786440 | tf_op jit(solution)/shard_map/ppermute | solution.py:51
  277.9 10.3 %collective-permute-start.52 = (bf16[16,8192]{1,0:T(8,128)(2,1)S(1)}, bf16[16,8192]{1,0:T(8,128)(2,1)S(1)}, u32[]{:S(2)}, u32[]{:S(2)}) collective-permute-start(bf16[16,8192]{1,0:T(8,128)(2,1)S(1)} %fusion.19), channel_id=1, source_target_pairs={{0,6},{1,7},{2,4},{3,5},{6,0},{7,1},{4,2},{5,3},{8,14},{9,15},{10,... | collective-permute-start | bytes 786440 | tf_op jit(solution)/shard_map/ppermute | solution.py:51
  279.7 12.4 %collective-permute-start.51 = (bf16[16,8192]{1,0:T(8,128)(2,1)S(1)}, bf16[16,8192]{1,0:T(8,128)(2,1)S(1)}, u32[]{:S(2)}, u32[]{:S(2)}) collective-permute-start(bf16[16,8192]{1,0:T(8,128)(2,1)S(1)} %fusion.19), channel_id=1, source_target_pairs={{0,2},{1,3},{2,6},{3,7},{6,4},{7,5},{4,0},{5,1},{8,10},{9,11},{10,... | collective-permute-start | bytes 786440 | tf_op jit(solution)/shard_map/ppermute | solution.py:51
  305.6 17.8 %collective-permute-start.58 = (bf16[128,128]{1,0:T(8,128)(2,1)S(1)}, bf16[128,128]{1,0:T(8,128)(2,1)S(1)}, u32[]{:S(2)}, u32[]{:S(2)}) collective-permute-start(bf16[128,128]{1,0:T(8,128)(2,1)S(1)} %get-tuple-element.91), channel_id=1, source_target_pairs={{0,4},{1,5},{2,0},{3,1},{6,2},{7,3},{4,6},{5,7},{8,12},{9,13},{10,... | collective-permute-start | bytes 98312 | tf_op jit(solution)/shard_map/ppermute | solution.py:51
  306.2 17.1 %collective-permute-start.57 = (bf16[128,128]{1,0:T(8,128)(2,1)S(1)}, bf16[128,128]{1,0:T(8,128)(2,1)S(1)}, u32[]{:S(2)}, u32[]{:S(2)}) collective-permute-start(bf16[128,128]{1,0:T(8,128)(2,1)S(1)} %get-tuple-element.92), channel_id=1, source_target_pairs={{0,6},{1,7},{2,4},{3,5},{6,0},{7,1},{4,2},{5,3},{8,14},{9,15},{10,... | collective-permute-start | bytes 98312 | tf_op jit(solution)/shard_map/ppermute | solution.py:51
  308.0 15.4 %collective-permute-start.56 = (bf16[128,128]{1,0:T(8,128)(2,1)S(1)}, bf16[128,128]{1,0:T(8,128)(2,1)S(1)}, u32[]{:S(2)}, u32[]{:S(2)}) collective-permute-start(bf16[128,128]{1,0:T(8,128)(2,1)S(1)} %get-tuple-element.93), channel_id=1, source_target_pairs={{0,2},{1,3},{2,6},{3,7},{6,4},{7,5},{4,0},{5,1},{8,10},{9,11},{10,... | collective-permute-start | bytes 98312 | tf_op jit(solution)/shard_map/ppermute | solution.py:51
  336.6 14.5 %collective-permute-start.63 = (bf16[64,4096]{1,0:T(8,128)(2,1)}, bf16[64,4096]{1,0:T(8,128)(2,1)}, u32[]{:S(2)}, u32[]{:S(2)}) collective-permute-start(bf16[64,4096]{1,0:T(8,128)(2,1)} %slice.327), channel_id=1, source_target_pairs={{0,1},{1,0},{2,3},{3,2},{4,5},{5,4},{6,7},{7,6},{8,9},{9,8},{10,11... | collective-permute-start | bytes 1572872 | tf_op jit(solution)/shard_map/ppermute | solution.py:42
  354.1 9.4 %collective-permute-start.64 = (bf16[16,4096]{1,0:T(8,128)(2,1)S(1)}, bf16[16,4096]{1,0:T(8,128)(2,1)S(1)}, u32[]{:S(2)}, u32[]{:S(2)}) collective-permute-start(bf16[16,4096]{1,0:T(8,128)(2,1)S(1)} %get-tuple-element.69), channel_id=1, source_target_pairs={{0,2},{1,3},{2,6},{3,7},{6,4},{7,5},{4,0},{5,1},{8,10},{9,11},{10,... | collective-permute-start | bytes 393224 | tf_op jit(solution)/shard_map/ppermute | solution.py:51
  356.4 9.5 %collective-permute-start.61 = (bf16[16,4096]{1,0:T(8,128)(2,1)S(1)}, bf16[16,4096]{1,0:T(8,128)(2,1)S(1)}, u32[]{:S(2)}, u32[]{:S(2)}) collective-permute-start(bf16[16,4096]{1,0:T(8,128)(2,1)S(1)} %get-tuple-element.68), channel_id=1, source_target_pairs={{0,6},{1,7},{2,4},{3,5},{6,0},{7,1},{4,2},{5,3},{8,14},{9,15},{10,... | collective-permute-start | bytes 393224 | tf_op jit(solution)/shard_map/ppermute | solution.py:51
  (66 other events, 580.1 us)

commit v2 on v0

v2 whole, which is shorter than its diff:
```python
import functools

import jax
import jax.numpy as jnp
from jax import lax
from jax.experimental import pallas as pl
from jax.experimental.pallas import tpu as pltpu
from jax.sharding import PartitionSpec as P

STATE = 256
GROUPS = 8
MIB = 1 << 20
BF = jnp.bfloat16
F32 = jnp.float32
HIGHEST = lax.Precision.HIGHEST
SUM_LOADS = 4
HELD = 6
OUT_COLS = 1024
SCAN_MIB = 28


def whole(shape):
    return pl.BlockSpec(shape, lambda *_: (0,) * len(shape))


def cost(flops, nbytes):
    return pl.CostEstimate(flops=int(flops), bytes_accessed=int(nbytes), transcendentals=0)


def params(mib):
    return pltpu.CompilerParams(vmem_limit_bytes=mib * MIB)


def dot(a, b, **kw):
    return jnp.dot(a, b, preferred_element_type=F32, **kw)


def ring_place(chip, chips):
    return chip ^ (chip >> 1) if chips == 4 else chip


def core_swap(value):
    count = lax.axis_size("head")
    return lax.ppermute(value, "head", [(i, i ^ 1) for i in range(count)])


def ring_shift(value, steps):
    chips = lax.axis_size("head") // 2
    ring = [ring_place(i, chips) for i in range(chips)]
    pairs = [
        (2 * ring[i] + c, 2 * ring[(i + steps) % chips] + c) for i in range(chips) for c in range(2)
    ]
    return lax.ppermute(value, "head", pairs)


def next_segment(value, tick):
    count = lax.axis_size("pipe")
    pairs = []
    for low in range(tick % 2, count - 1, 2):
        pairs += [(low, low + 1), (low + 1, low)]
    return lax.ppermute(value, "pipe", pairs)


def bits(value, low, size):
    return (value >> (low.bit_length() - 1)) & (size - 1)


def iotas(rows, cols):
    return (
        lax.broadcasted_iota(jnp.int32, (rows, 1), 0),
        lax.broadcasted_iota(jnp.int32, (1, cols), 1),
    )


def device_at(head, distance, core, chips):
    place = (ring_place(head >> 1, chips) + distance) & (chips - 1)
    return 2 * ring_place(place, chips) + ((head & 1) ^ core)


def gather_order(head, rows, micro, local):
    devices = rows // (micro * local)
    chips = devices // 2
    time, place = iotas(rows, rows)
    device, block = bits(time, local, devices), bits(time, local * devices, micro)
    distance = (ring_place(head >> 1, chips) - ring_place(device >> 1, chips)) & (chips - 1)
    core = (device ^ head) & 1
    at = (((core * chips + distance) * micro) + block) * local + bits(time, 1, local)
    return (at == place).astype(F32).astype(BF)


def scatter_order(head, rows, micro, local):
    devices = rows // (micro * local)
    chips = devices // 2
    place, time = iotas(rows, rows)
    own = micro * local
    device = device_at(head, bits(place, own, chips), bits(place, own * chips, 2), chips)
    at = bits(place, local, micro) * (local * devices) + device * local + bits(place, 1, local)
    return (at == time).astype(F32).astype(BF)


def pick_columns(head, first, count, bc_cols, devices):
    chips, span = devices // 2, bc_cols // GROUPS
    column, sent = iotas(count, 2 * span * chips)
    device = device_at(head, bits(sent, 2 * span, chips), bits(sent, span, 2), chips)
    group = (device * GROUPS) >> (devices.bit_length() - 1)
    return (bits(sent, 1, span) * GROUPS + group == column + first).astype(F32).astype(BF)


def place_columns(head, core, devices):
    chips, span = devices // 2, 2 * STATE // devices
    sent, column = iotas(2 * STATE, 2 * STATE)
    device = device_at(head, -bits(sent, 2 * span, chips), core, chips)
    here = jnp.where(bits(sent, span, 2) == core, device * span + bits(sent, 1, span), -1)
    return (here == column).astype(F32).astype(BF)


def load_kernel(plan, go_ref, *refs):
    weights = max(p[0] for p in plan) + 1
    count = len(plan)
    sources, value_ref = refs[:weights], refs[weights]
    held, copy_ref, sems = refs[weights + 1:-2], refs[-2], refs[-1]
    copies = []
    for i, (which, index) in enumerate(plan):
        cols = held[i].shape[1]
        copies.append(
            pltpu.make_async_copy(sources[which].at[:, pl.ds(index * cols, cols)], held[i], sems.at[i])
        )
        copies[-1].start()

    @pl.when(go_ref[0] >= 0)
    def _():
        copy_ref[...] = value_ref[...]

    for i in range(count):
        copies[i].wait()


def load_beside(go, plan, value):
    if not plan:
        return [], value
    weights = []
    for weight, _, _ in plan:
        if not any(weight is w for w in weights):
            weights.append(weight)
    steps = [([weight is w for w in weights].index(True), index) for weight, _, index in plan]
    vmem = pl.BlockSpec(memory_space=pltpu.VMEM)
    nbytes = sum(2 * w.shape[0] * cols for w, cols, _ in plan)
    *held, value = pl.pallas_call(
        functools.partial(load_kernel, steps),
        in_specs=[pl.BlockSpec(memory_space=pltpu.SMEM)] + [pl.BlockSpec(memory_space=pl.ANY)] * len(weights) + [vmem],
        out_specs=[vmem] * (len(plan) + 1),
        out_shape=[pltpu.VMEM((w.shape[0], cols), w.dtype) for w, cols, _ in plan]
        + [jax.ShapeDtypeStruct(value.shape, value.dtype)],
        scratch_shapes=[pltpu.SemaphoreType.DMA((len(plan),))],
        compiler_params=params(2),
        cost_estimate=cost(0, nbytes),
    )(go, *[pltpu.with_memory_space_constraint(w, pltpu.HBM) for w in weights], value)
    return held, value


def first_kernel(count, micro, local, *refs):
    pieces, (go_ref, wdt_ref, wbc_ref, normed_ref, dt_ref, bc_ref, late, wdt, sems) = refs[:count], refs[count:]
    rows = pieces[0].shape[0]
    blocks, _, cols = late.shape

    def fetch(i):
        return pltpu.make_async_copy(wbc_ref.at[:, pl.ds(i * cols, cols)], late.at[i], sems.at[i])

    steps = pltpu.make_async_copy(wdt_ref, wdt, sems.at[blocks])
    steps.start()
    for i in range(blocks):
        fetch(i).start()

    @pl.when(go_ref[0] >= 0)
    def _():
        for i, piece in enumerate(pieces):
            normed_ref[i * rows:(i + 1) * rows, :] = piece[...]

    steps.wait()
    dt_ref[...] = lax.dot_general(
        normed_ref[...], wdt[...], (((1,), (1,)), ((), ())), preferred_element_type=F32
    )
    head = go_ref[0]
    all_rows = normed_ref.shape[0]
    devices = all_rows // (micro * local)
    gather = gather_order(head, all_rows, micro, local)
    total = jnp.zeros(bc_ref.shape, F32)
    for i in range(blocks):
        fetch(i).wait()
        part = dot(normed_ref[...], late[i]).astype(BF)
        part = dot(gather, part).astype(BF)
        total += dot(part, pick_columns(head, i * cols, cols, blocks * cols, devices))
    bc_ref[...] = total.astype(BF)


def project_first(go, pieces, micro, local, w_bc, w_dt):
    width, bc_cols = w_bc.shape
    rows = len(pieces) * pieces[0].shape[0]
    heads = w_dt.shape[0]
    vmem = pl.BlockSpec(memory_space=pltpu.VMEM)
    block = min(256, bc_cols)
    args = (*pieces, go, pltpu.with_memory_space_constraint(w_dt, pltpu.HBM), pltpu.with_memory_space_constraint(w_bc, pltpu.HBM))
    shapes = [
        jax.ShapeDtypeStruct((rows, width), BF),
        jax.ShapeDtypeStruct((rows, heads), F32),
        jax.ShapeDtypeStruct((rows, bc_cols // GROUPS * (rows // (micro * local))), BF),
    ]
    return pl.pallas_call(
        functools.partial(first_kernel, len(pieces), micro, local),
        in_specs=[vmem] * len(pieces) + [pl.BlockSpec(memory_space=pltpu.SMEM)]
        + [pl.BlockSpec(memory_space=pl.ANY)] * 2,
        out_specs=[vmem] * 3,
        out_shape=shapes,
        scratch_shapes=[
            pltpu.VMEM((bc_cols // block, width, block), BF),
            pltpu.VMEM(w_dt.shape, BF),
            pltpu.SemaphoreType.DMA((bc_cols // block + 1,)),
        ],
        compiler_params=params(12),
        cost_estimate=cost(2 * rows * width * (bc_cols + heads), 2 * w_bc.size),
    )(*args)


def held_kernel(count, go_ref, normed_ref, value_ref, *refs):
    held, (w_ref, x_ref, copy_ref, late, sems) = refs[:count], refs[count:]
    rest, _, cols = late.shape

    def fetch(i):
        return pltpu.make_async_copy(w_ref.at[:, pl.ds((count + i) * cols, cols)], late.at[i], sems.at[i])

    for i in range(rest):
        fetch(i).start()

    @pl.when(go_ref[0] >= 0)
    def _():
        copy_ref[...] = value_ref[...]
        for i, block_ref in enumerate(held):
            x_ref[:, i * cols:(i + 1) * cols] = dot(normed_ref[...], block_ref[...])

    for i in range(rest):
        fetch(i).wait()
        x_ref[:, (count + i) * cols:(count + i + 1) * cols] = dot(normed_ref[...], late[i])


def held_inner(go, normed, held, weight, block, value):
    rows, width = normed.shape
    cols = weight.shape[1]
    rest = cols // block - len(held)
    vmem = pl.BlockSpec(memory_space=pltpu.VMEM)
    return pl.pallas_call(
        functools.partial(held_kernel, len(held)),
        in_specs=[pl.BlockSpec(memory_space=pltpu.SMEM)] + [vmem] * (len(held) + 2) + [pl.BlockSpec(memory_space=pl.ANY)],
        out_specs=[vmem, vmem],
        out_shape=[jax.ShapeDtypeStruct((rows, cols), F32), jax.ShapeDtypeStruct(value.shape, value.dtype)],
        scratch_shapes=[pltpu.VMEM((rest, width, block), BF), pltpu.SemaphoreType.DMA((rest,))],
        compiler_params=params(4 + 2 * rest * width * block // MIB),
        cost_estimate=cost(2 * rows * width * cols, 2 * rows * width),
    )(go, normed, value, *[pltpu.with_memory_space_constraint(w, pltpu.VMEM) for w in held],
      pltpu.with_memory_space_constraint(weight, pltpu.HBM))


def join_kernel(*refs):
    lanes = refs[0].shape[1]
    for i, ref in enumerate(refs[:-1]):
        refs[-1][:, i * lanes:(i + 1) * lanes] = ref[...]


def join(parts):
    rows, lanes = parts[0].shape
    if lanes % 128:
        return jnp.concatenate(parts, axis=1)
    vmem = pl.BlockSpec(memory_space=pltpu.VMEM)
    return pl.pallas_call(
        join_kernel,
        in_specs=[vmem] * len(parts),
        out_specs=vmem,
        out_shape=jax.ShapeDtypeStruct((rows, lanes * len(parts)), parts[0].dtype),
        compiler_params=params(1),
        cost_estimate=cost(0, 4 * rows * lanes * len(parts)),
    )(*parts)


def conv_silu(pad_ref, const_ref, first, taps):
    rows, cols = pad_ref.shape[0] - 8, pad_ref.shape[1]
    pad_ref[8 - (taps - 1):8, :] = const_ref[first:first + taps - 1, :cols]
    at = first + taps - 1
    total = const_ref[at:at + 1, :cols] * pad_ref[pl.ds(9 - taps, rows), :]
    for k in range(1, taps):
        total = total + const_ref[at + k:at + k + 1, :cols] * pad_ref[pl.ds(9 - taps + k, rows), :]
    return total * jax.nn.sigmoid(total)


def in_time(order, groups_ref, group_rows, src_ref, dst_ref):
    rows = src_ref.shape[0]
    if group_rows % 8:
        dst_ref[8:, :] = dot(order.astype(F32), src_ref[...], precision=HIGHEST)
        return
    for g in range(rows // group_rows):
        start = pl.multiple_of(groups_ref[1 + g] * group_rows, group_rows)
        dst_ref[8 + g * group_rows:8 + (g + 1) * group_rows, :] = src_ref[pl.ds(start, group_rows), :]


def spread_exact(values, spread):
    high = values.astype(BF)
    rest = values - high.astype(F32)
    mid = rest.astype(BF)
    low = (rest - mid.astype(F32)).astype(BF)
    return dot(jnp.concatenate([high, mid, low], axis=1), spread)


def scan_kernel(micro, group_rows, slots, taps, groups_ref, flag_ref, x_ref, here_ref, over_ref, dt_ref, const_ref, state_ref,
                w_ref, _weighted, _b, _end, own_ref, other_ref, weighted_ref, b_ref, end_ref, pad_x, pad_bc, scaled, y_ref,
                sorted_ref, const, state_buf, weighted_buf, b_buf, end_buf, ring, sems, own_sems):
    pieces = (own_ref, other_ref)
    count = 0
    rows, channels = y_ref.shape
    active = flag_ref[0] == 1
    heads = dt_ref.shape[1]
    dim = channels // heads
    half = STATE
    devices = rows // (micro * group_rows)
    head = groups_ref[0]
    block = ring.shape[2]
    blocks = w_ref.shape[1] // block

    def fetch(i):
        slot = lax.rem(i, slots)
        cols = pl.ds(pl.multiple_of(i * block, block), block)
        return pltpu.make_async_copy(w_ref.at[:, cols], ring.at[slot], sems.at[slot])

    loads = [pltpu.make_async_copy(const_ref, const, own_sems.at[0]), pltpu.make_async_copy(state_ref, state_buf, own_sems.at[1])]
    for copy in loads:
        copy.start()
    for i in range(min(slots, blocks)):
        fetch(i).start()

    @pl.when(groups_ref[0] >= 0)
    def _():
        arrived = dot(here_ref[...], place_columns(head, 0, devices)) + dot(over_ref[...], place_columns(head, 1, devices))
        pad_bc[8:, :] = arrived
        gather = gather_order(head, rows, micro, group_rows)
        loads[0].wait()
        bc = conv_silu(pad_bc, const, 2 * taps, taps)
        b_mat, c_mat = bc[:, :half], bc[:, half:]
        b_bf, c_bf = b_mat.astype(BF), c_mat.astype(BF)
        b_buf[...] = b_bf
        contract = (((1,), (1,)), ((), ()))
        scores = lax.dot_general(c_mat, b_mat, contract, precision=HIGHEST, preferred_element_type=F32)
        t_ids = lax.broadcasted_iota(jnp.int32, (rows, rows), 0)
        s_ids = lax.broadcasted_iota(jnp.int32, (rows, rows), 1)
        causal = t_ids >= s_ids
        scores = jnp.where(causal, scores, 0.0)

        raw = dot(gather.astype(F32), dt_ref[...], precision=HIGHEST) + const[4 * taps - 1:4 * taps, :heads]
        step = jnp.maximum(raw, 0.0) + jnp.log1p(jnp.exp(-jnp.abs(raw)))
        log_decay = dot(causal.astype(F32), -step * const[4 * taps:4 * taps + 1, :heads], precision=HIGHEST)
        end_log = log_decay[rows - 1:rows, :]
        end_buf[...] = jnp.exp(end_log)
        part_head, channel = iotas(3 * heads, channels)
        spread = (bits(part_head, 1, heads) == (channel >> (dim.bit_length() - 1))).astype(F32).astype(BF)
        step_full = spread_exact(step, spread)
        to_end_full = spread_exact(jnp.exp(end_log - log_decay), spread)
        decay_full = spread_exact(jnp.exp(log_decay), spread)
        log_rows = log_decay.T

        in_time(gather, groups_ref, group_rows, x_ref, pad_x)
        x_conv = conv_silu(pad_x, const, 0, taps)
        stepped = x_conv * step_full
        scaled[...] = stepped.astype(BF)
        weighted_buf[...] = (stepped * to_end_full).astype(BF)
        for j in range(heads):
            gap = jnp.minimum(log_decay[:, j:j + 1] - log_rows[j:j + 1, :], 0.0)
            weight = (scores * jnp.exp(gap)).astype(BF)
            cols = slice(j * dim, (j + 1) * dim)
            pad_x[8:, cols] = const[2 * taps - 1:2 * taps, cols] * x_conv[:, cols] + dot(weight, scaled[:, cols])

        loads[1].wait()
        state = state_buf[...].reshape(channels, half).astype(BF)
        carried = lax.dot_general(c_bf, state, contract, preferred_element_type=F32)
        y_ref[...] = (pad_x[8:, :] + carried * decay_full).astype(BF)

    kept = [
        pltpu.make_async_copy(src, dst, own_sems.at[i])
        for i, (src, dst) in enumerate(((weighted_buf, weighted_ref), (b_buf, b_ref), (end_buf, end_ref)))
    ]

    @pl.when(active)
    def _():
        for copy in kept:
            copy.start()

    sorted_ref[...] = dot(scatter_order(head, rows, micro, group_rows), y_ref[...]).astype(BF)
    size = rows // 2

    @pl.loop(0, blocks)
    def _(i):
        fetch(i).wait()
        part = dot(sorted_ref[...], ring[lax.rem(i, slots)]).astype(BF)
        cols = pl.ds(pl.multiple_of(i * block, block), block)
        for q, piece in enumerate(pieces):
            piece[:, cols] = part[q * size:(q + 1) * size, :]

        @pl.when(i + slots < blocks)
        def _():
            fetch(i + slots).start()

    @pl.when(active)
    def _():
        for copy in kept:
            copy.wait()


def scan_and_out(micro, group_rows, taps, groups, flag, x_proj, here, over, dt_raw, const, state, old, w_out):
    rows, channels = x_proj.shape
    width = w_out.shape[1]
    block, slots = OUT_COLS, 4
    far = [pltpu.with_memory_space_constraint(a, pltpu.HBM) for a in (const, state, w_out, *old)]
    shapes = [jax.ShapeDtypeStruct((rows // 2, width), BF)] * 2 + [jax.ShapeDtypeStruct(o.shape, o.dtype) for o in old]
    vmem = pl.BlockSpec(memory_space=pltpu.VMEM)
    smem = pl.BlockSpec(memory_space=pltpu.SMEM)
    hbm = pl.BlockSpec(memory_space=pl.ANY)
    return pl.pallas_call(
        functools.partial(scan_kernel, micro, group_rows, slots, taps),
        in_specs=[smem, smem] + [vmem] * 4 + [hbm] * 6,
        out_specs=[vmem] * 2 + [hbm] * 3,
        out_shape=shapes,
        input_output_aliases={9: 2, 10: 3, 11: 4},
        scratch_shapes=[
            pltpu.VMEM((rows + 8, channels), F32),
            pltpu.VMEM((rows + 8, 2 * STATE), F32),
            pltpu.VMEM((rows, channels), BF),
            pltpu.VMEM((rows, channels), BF),
            pltpu.VMEM((rows, channels), BF),
            pltpu.VMEM(const.shape, F32),
            pltpu.VMEM(state.shape, F32),
            *[pltpu.VMEM(o.shape, o.dtype) for o in old],
            pltpu.VMEM((slots, channels, block), BF),
            pltpu.SemaphoreType.DMA((slots,)),
            pltpu.SemaphoreType.DMA((3,)),
        ],
        compiler_params=params(SCAN_MIB),
        cost_estimate=cost(2 * rows * channels * (rows + STATE + width), 2 * w_out.size),
    )(groups, flag, x_proj, here, over, dt_raw, *far)


def state_kernel(end_ref, weighted_ref, b_ref, state_ref, value_ref, out_ref, copy_ref):
    heads, dim, _ = state_ref.shape
    copy_ref[...] = value_ref[...]
    added = lax.dot_general(
        weighted_ref[...], b_ref[...], (((0,), (0,)), ((), ())), preferred_element_type=F32
    )
    for j in range(heads):
        out_ref[j] = end_ref[0, j] * state_ref[j] + added[j * dim:(j + 1) * dim, :]


def state_update(end, weighted, b_mat, state, value):
    vmem = pl.BlockSpec(memory_space=pltpu.VMEM)
    return pl.pallas_call(
        state_kernel,
        in_specs=[pl.BlockSpec(memory_space=pltpu.SMEM)] + [vmem] * 4,
        out_specs=[vmem, vmem],
        out_shape=[jax.ShapeDtypeStruct(state.shape, F32), jax.ShapeDtypeStruct(value.shape, value.dtype)],
        compiler_params=params(12),
        cost_estimate=cost(2 * weighted.size * b_mat.shape[1], 8 * state.size),
    )(end, weighted, b_mat, state, value)


def rms_rows(rows_in, gain):
    floats = rows_in.astype(F32)
    scaled = floats * lax.rsqrt(jnp.mean(floats * floats, axis=-1, keepdims=True) + 1e-05)
    return (scaled * gain[None, :]).astype(BF)


def per_device(hidden, norm_gain, w_x, w_bc, w_dt, conv_x, conv_bc, dt_bias, a_rate, d_skip, w_out,
               ssm_init, conv_x_init, conv_bc_init):
    segment = lax.axis_index("pipe")
    segments = lax.axis_size("pipe")
    head = lax.axis_index("head")
    devices = lax.axis_size("head")
    chips = devices // 2
    micro, local, width = hidden.shape
    own_rows = micro * local
    rows = own_rows * devices
    half = rows // 2
    local_heads = dt_bias.shape[1]
    channels = w_x.shape[2]
    bc_cols = w_bc.shape[2]
    span = bc_cols // GROUPS

    everyone = jnp.arange(devices)
    distance = (ring_place(head // 2, chips) - ring_place(everyone // 2, chips)) % chips
    place = ((everyone ^ head) % 2) * chips + distance
    groups = (place[None, :] * micro + jnp.arange(micro)[:, None]).reshape(-1)
    groups = jnp.concatenate([head[None], groups]).astype(jnp.int32)

    my_group = head * GROUPS // devices
    tail_bc = lax.dynamic_index_in_dim(conv_bc_init[0].reshape(-1, 2 * STATE, GROUPS), my_group, 2, keepdims=False)
    taps_bc = lax.dynamic_index_in_dim(conv_bc[0].reshape(-1, 2 * STATE, GROUPS), my_group, 2, keepdims=False)
    skip = jnp.repeat(d_skip[0], channels // local_heads)[None, :]

    taps = conv_x.shape[1]
    const_cols = max(channels, 2 * STATE)

    def wide(values):
        return jnp.pad(values, ((0, 0), (0, const_cols - values.shape[1])))

    const = jnp.concatenate([
        wide(a) for a in (conv_x_init[0], conv_x[0], skip, tail_bc, taps_bc, dt_bias, a_rate)
    ])
    const = jnp.pad(const, ((0, -const.shape[0] % 8), (0, 0)))

    block = 256 if channels >= 2048 else 128
    count = channels // block
    kept = min(HELD, count - 1)
    in_sum = min(SUM_LOADS, kept)
    inner_plan = [(w_x[0], block, i) for i in range(kept)]
    go = groups

    current = hidden.reshape(own_rows, width)
    out_rows = jnp.zeros((own_rows, width), BF)
    old = (
        jnp.zeros((rows, channels), BF),
        jnp.zeros((rows, STATE), BF),
        jnp.zeros((1, local_heads), F32),
    )
    held = []
    for tick in range(segments):
        last = tick + 1 == segments
        active = segment == tick
        flag = active.astype(jnp.int32).reshape(1)
        normed = rms_rows(current, norm_gain[0])
        arrived = [ring_shift(normed, s) for s in range(1, chips)]
        if tick:
            more, normed = load_beside(go, inner_plan[in_sum:], normed)
            held = held + more
        pieces = [normed] + arrived
        if own_rows % 16:
            pieces = [jnp.concatenate(pieces, axis=0)]
        pieces = pieces + [core_swap(piece) for piece in pieces]
        normed_all, dt_raw, bc_out = project_first(go, pieces, micro, local, w_bc[0], w_dt[0].T)
        bc_parts = [bc_out[:, s * 2 * span:(s + 1) * 2 * span] for s in range(chips)]
        bc_here = bc_parts[0]
        bc_parts = [ring_shift(bc_parts[s], s) for s in range(1, chips)]
        x_proj, bc_here = held_inner(go, normed_all, held, w_x[0], block, bc_here)
        bc_here = join([bc_here] + bc_parts)
        mine, other, *old = scan_and_out(
            micro, local, taps, groups, flag, x_proj, bc_here, core_swap(bc_here), dt_raw, const, ssm_init[0], old, w_out[0]
        )
        received = core_swap(other)
        pair = (mine.astype(F32) + received.astype(F32)).astype(BF)
        arrived = [ring_shift(pair[s * own_rows:(s + 1) * own_rows], s) for s in range(1, chips)]
        own = pair[:own_rows]
        if last:
            state_out, own = state_update(old[2], old[0], old[1], ssm_init[0], own)
        else:
            held, own = load_beside(go, inner_plan[:in_sum], own)
        total = own.astype(F32)
        for piece in arrived:
            total = total + piece.astype(F32)
        new_rows = (current.astype(F32) + total).astype(BF)
        out_rows = jnp.where(active, new_rows, out_rows)
        if not last:
            current = next_segment(new_rows, tick)
    return (out_rows.reshape(1, micro, local, width), state_out[None])


def solution(mesh):
    in_specs = (
        P(None, "head", None),
        P("pipe", None),
        P("pipe", None, "head"),
        P("pipe", None, "head"),
        P("pipe", None, "head"),
        P("pipe", None, "head"),
        P("pipe", None, None),
        P("pipe", "head"),
        P("pipe", "head"),
        P("pipe", "head"),
        P("pipe", "head", None),
        P("pipe", "head", None, None),
        P("pipe", None, "head"),
        P("pipe", None, None),
    )
    out_specs = (P("pipe", None, "head", None), P("pipe", "head", None, None))
    return jax.shard_map(
        per_device, mesh=mesh, in_specs=in_specs, out_specs=out_specs, check_vma=False
    )
```

time: 831 us -> 317 us (0.38)
  matrix products: 285 us -> 0 us
  waiting for transfers between devices: 358 us -> 88.5 us
  Pallas kernels: 0 us -> 153 us
  local copies, waits for them, and re-layouts: 63.2 us -> 5.86 us
  blocking collectives: 46.1 us -> 0 us
  starting transfers between devices: 16.5 us -> 59.3 us
  other arithmetic: 38.9 us -> 5.88 us
  between operations: 15.6 us -> 1.68 us
    dot_general x50 -> x0, matrix products: 285 us -> none  [the longest x5 73.8 us: per_device(): jnp.dot(mixed_bf, out_weight, preferred_element_type=jnp.float32)]
    psum x5 -> x0, waiting for transfers between devices: 268 us -> none  [per_device(): lax.psum(jnp.dot(mixed_bf, out_weight, preferred_element_type=jnp.float32...]
    pallas_call x0 -> x23, Pallas kernels: none -> 153 us  [the longest x4 62.8 us: scan_and_out(): pl.pallas_call(functools.partial(scan_kernel, micro, group_rows, slots, t...]
    ppermute x4 -> x63, waiting for transfers between devices: 10.9 us -> 88.5 us  [the longest x36 57.8 us: ring_shift(): return lax.ppermute(value, 'head', pairs)]
    all_gather x5 -> x0, waiting for transfers between devices: 77.2 us -> none  [per_device(): entry_rows = lax.all_gather(own_rows, 'head', axis=0, tiled=True)]
    all_gather x5 -> x0, blocking collectives: 46.1 us -> none  [mix_block(): bc_all = lax.all_gather(bc_part, 'head', axis=1, tiled=True)]
    ppermute x4 -> x63, starting transfers between devices: 16.1 us -> 59.3 us  [the longest x36 43.9 us: ring_shift(): return lax.ppermute(value, 'head', pairs)]
    unnamed x115 -> x31, local copies, waits for them, and re-layouts: 23 us -> 0.1 us
  transfers between devices with their start and end apart: 14 -> 63, of which waited for: 14 -> 38; matrix products, arithmetic and copies ran while one was open for 6% -> 1% of each run, Pallas kernels for 0% -> 21%
where the time goes in v2:
time: 317 us; the launch traced here: 314 us
  Pallas kernels  153 us (48%)
  waiting for transfers between devices  88.5 us (28%)
  starting transfers between devices  59.3 us (19%)
  other arithmetic  5.88 us (2%)
  local copies, waits for them, and re-layouts  5.86 us (2%)
    pallas_call x4, Pallas kernels, scan_and_out(): pl.pallas_call(functools.partial(scan_kernel, micro, group_rows, slots, t...  62.8 us
    ppermute x36, waiting for transfers between devices, ring_shift(): return lax.ppermute(value, 'head', pairs)  57.8 us
    ppermute x36, starting transfers between devices, ring_shift(): return lax.ppermute(value, 'head', pairs)  43.9 us
    pallas_call x4, Pallas kernels, held_inner(): pl.pallas_call(functools.partial(held_kernel, len(held)), in_specs=[pl.Bl...  32.7 us
    pallas_call x6, Pallas kernels, load_beside(): pl.pallas_call(functools.partial(load_kernel, steps), in_specs=[pl.BlockS...  31.5 us
    pallas_call x4, Pallas kernels, project_first(): pl.pallas_call(functools.partial(first_kernel, len(pieces), micro, local)...  23.2 us
    ppermute x24, waiting for transfers between devices, core_swap(): return lax.ppermute(value, 'head', [(i, i ^ 1) for i in range(count)])  19.4 us
    ppermute x3, starting transfers between devices, next_segment(): return lax.ppermute(value, 'pipe', pairs)  12.5 us
  transfers between devices with their start and end apart: 63, of which 38 were waited for; matrix products, arithmetic and copies ran while one was open for 1% of the time, Pallas kernels for 21%

profile of v2, /device:TPU:0, one launch (start us, length us, event | category | flops | bytes accessed | tf_op | source)
XLA Modules:
  0.0 313.9 jit_solution(17336367315879048180)
XLA Ops:
  2.9 3.0 collective-permute-start
  8.9 3.7 %collective-permute-done.refs_1_ = bf16[16,8192]{1,0:T(8,128)(2,1)S(1)} collective-permute-done((bf16[16,8192]{1,0:T(8,128)(2,1)S(1)}, bf16[16,8192]{1,0:T(8,128)(2,1)S(1)}, u32[]{:S(2)}, u32[]{:S(2)}) %collective-permute-start) | collective-permute-done | bytes 262176 | tf_op jit(solution)/shard_map/ppermute | solution.py:53
  12.6 6.4 %collective-permute-done.1.refs_2_ = bf16[16,8192]{1,0:T(8,128)(2,1)S(1)} collective-permute-done((bf16[16,8192]{1,0:T(8,128)(2,1)S(1)}, bf16[16,8192]{1,0:T(8,128)(2,1)S(1)}, u32[]{:S(2)}, u32[]{:S(2)}) %collective-permute-start.1) | collective-permute-done | bytes 262176 | tf_op jit(solution)/shard_map/ppermute | solution.py:53
  21.0 5.8 %shard_map.149 = (bf16[128,8192]{1,0:T(8,128)(2,1)S(1)}, f32[128,32]{1,0:T(8,128)S(1)}, bf16[128,512]{1,0:T(8,128)(2,1)S(1)}) custom-call(bf16[16,8192]{1,0:T(8,128)(2,1)S(1)} %fusion.3.refs_0_, bf16[16,8192]{1,0:T(8,128)(2,1)S(1)} %collective-permute-done.refs_1_, bf16[16,8192]{1,0:T(8,128)(2,1)S(1)} %collective-permute-done.1.refs_2_, ...), custom_call_target="tpu_custom_call" | custom-call | flops 1140850688 | bytes 8388608 | tf_op jit(solution)/shard_map/pallas_call | solution.py:208
  31.2 12.7 %shard_map.150 = (f32[128,2048]{1,0:T(8,128)S(1)}, bf16[128,128]{1,0:T(8,128)(2,1)S(1)}) custom-call(s32[17]{0:T(128)S(1)} %pad_add_fusion.refs_8_.go_ref.groups_ref, bf16[128,8192]{1,0:T(8,128)(2,1)S(1)} %get-tuple-element.68.normed_ref, bf16[128,128]{1,0:T(8,128)(2,1)S(1)} %get-tuple-element.165.value_ref, bf16[8192,2048]{1,0:T(8,128)(2,1)} %bitcast.38), custom_call_target="tpu_custom_call" | custom-call | flops 4294967296 | bytes 2097152 | tf_op jit(solution)/shard_map/pallas_call | solution.py:250
  49.6 15.7 %shard_map.152 = (bf16[64,8192]{1,0:T(8,128)(2,1)S(1)}, bf16[64,8192]{1,0:T(8,128)(2,1)S(1)}, bf16[128,2048]{1,0:T(8,128)(2,1)}, bf16[128,256]{1,0:T(8,128)(2,1)}, f32[1,32]{1,0:T(1,128)}) custom-call(s32[17]{0:T(128)S(1)} %pad_add_fusion.refs_8_.go_ref.groups_ref, s32[1]{0:T(128)} %bitcast.3.flag_ref, ...), custom_call_target="tpu_custom_call", output_to_operand_aliasing={{2}: (9, {}), {3}: (10, {}), {4}: (11, {})} | custom-call | flops 4496293888 | bytes 33554432 | tf_op jit(solution)/shard_map/pallas_call | solution.py:422
  71.2 6.5 %shard_map.153 = (bf16[8192,256]{1,0:T(8,128)(2,1)S(1)}, bf16[8192,256]{1,0:T(8,128)(2,1)S(1)}, bf16[8192,256]{1,0:T(8,128)(2,1)S(1)}, bf16[8192,256]{1,0:T(8,128)(2,1)S(1)}, bf16[16,8192]{1,0:T(8,128)(2,1)S(1)}) custom-call(s32[17]{0:T(128)S(1)} %pad_add_fusion.refs_8_.go_ref.groups_ref, bf16[8192,2048]{1,0:T(8,128)(2,1)} %bitcast.39, ...), custom_call_target="tpu_custom_call" | custom-call | bytes 16777216 | tf_op jit(solution)/shard_map/pallas_call | solution.py:148
  77.7 5.1 %collective-permute-done.13 = bf16[16,8192]{1,0:T(8,128)(2,1)S(1)} collective-permute-done((bf16[16,8192]{1,0:T(8,128)(2,1)S(1)}, bf16[16,8192]{1,0:T(8,128)(2,1)S(1)}, u32[]{:S(2)}, u32[]{:S(2)}) %collective-permute-start.13) | collective-permute-done | bytes 262176 | tf_op jit(solution)/shard_map/ppermute | solution.py:53
  85.8 5.9 %collective-permute-done.15 = bf16[16,8192]{1,0:T(8,128)(2,1)S(1)} collective-permute-done((bf16[16,8192]{1,0:T(8,128)(2,1)S(1)}, bf16[16,8192]{1,0:T(8,128)(2,1)S(1)}, u32[]{:S(2)}, u32[]{:S(2)}) %collective-permute-start.15) | collective-permute-done | bytes 262176 | tf_op jit(solution)/shard_map/ppermute | solution.py:61
  94.9 4.0 %shard_map.154 = (bf16[8192,256]{1,0:T(8,128)(2,1)S(1)}, bf16[8192,256]{1,0:T(8,128)(2,1)S(1)}, bf16[16,8192]{1,0:T(8,128)(2,1)S(1)}) custom-call(s32[17]{0:T(128)S(1)} %pad_add_fusion.refs_8_.go_ref.groups_ref, bf16[8192,2048]{1,0:T(8,128)(2,1)} %bitcast.43, bf16[8192,2048]{1,0:T(8,128)(2,1)} %bitcast.44, bf16[16,8192]{1,0:T(8,128)(2,1)S(1)} %fusion.8.refs_2_), custom_call_target="tpu_custom_call" | custom-call | bytes 8388608 | tf_op jit(solution)/shard_map/pallas_call | solution.py:148
  100.6 4.2 %collective-permute-done.17.refs_2_ = bf16[16,8192]{1,0:T(8,128)(2,1)S(1)} collective-permute-done((bf16[16,8192]{1,0:T(8,128)(2,1)S(1)}, bf16[16,8192]{1,0:T(8,128)(2,1)S(1)}, u32[]{:S(2)}, u32[]{:S(2)}) %collective-permute-start.17) | collective-permute-done | bytes 262176 | tf_op jit(solution)/shard_map/ppermute | solution.py:53
  107.0 5.8 %shard_map.155 = (bf16[128,8192]{1,0:T(8,128)(2,1)S(1)}, f32[128,32]{1,0:T(8,128)S(1)}, bf16[128,512]{1,0:T(8,128)(2,1)S(1)}) custom-call(bf16[16,8192]{1,0:T(8,128)(2,1)S(1)} %get-tuple-element.76.refs_0_, bf16[16,8192]{1,0:T(8,128)(2,1)S(1)} %collective-permute-done.16.refs_1_, bf16[16,8192]{1,0:T(8,128)(2,1)S(1)} %collective-permute-done.17.refs_2_, ...), custom_call_target="tpu_custom_call" | custom-call | flops 1140850688 | bytes 8388608 | tf_op jit(solution)/shard_map/pallas_call | solution.py:208
  117.1 6.8 %shard_map.156 = (f32[128,2048]{1,0:T(8,128)S(1)}, bf16[128,128]{1,0:T(8,128)(2,1)S(1)}) custom-call(s32[17]{0:T(128)S(1)} %pad_add_fusion.refs_8_.go_ref.groups_ref, bf16[128,8192]{1,0:T(8,128)(2,1)S(1)} %get-tuple-element.77.normed_ref, bf16[128,128]{1,0:T(8,128)(2,1)S(1)} %get-tuple-element.161.value_ref, ...), custom_call_target="tpu_custom_call" | custom-call | flops 4294967296 | bytes 2097152 | tf_op jit(solution)/shard_map/pallas_call | solution.py:250
  125.5 15.7 %shard_map.158 = (bf16[64,8192]{1,0:T(8,128)(2,1)S(1)}, bf16[64,8192]{1,0:T(8,128)(2,1)S(1)}, bf16[128,2048]{1,0:T(8,128)(2,1)}, bf16[128,256]{1,0:T(8,128)(2,1)}, f32[1,32]{1,0:T(1,128)}) custom-call(s32[17]{0:T(128)S(1)} %pad_add_fusion.refs_8_.go_ref.groups_ref, s32[1]{0:T(128)} %bitcast.12.flag_ref, ...), custom_call_target="tpu_custom_call", output_to_operand_aliasing={{2}: (9, {}), {3}: (10, {}), {4}: (11, {})} | custom-call | flops 4496293888 | bytes 33554432 | tf_op jit(solution)/shard_map/pallas_call | solution.py:422
  141.4 2.5 collective-permute-done.27
  147.0 6.5 %shard_map.159 = (bf16[8192,256]{1,0:T(8,128)(2,1)S(1)}, bf16[8192,256]{1,0:T(8,128)(2,1)S(1)}, bf16[8192,256]{1,0:T(8,128)(2,1)S(1)}, bf16[8192,256]{1,0:T(8,128)(2,1)S(1)}, bf16[16,8192]{1,0:T(8,128)(2,1)S(1)}) custom-call(s32[17]{0:T(128)S(1)} %pad_add_fusion.refs_8_.go_ref.groups_ref, bf16[8192,2048]{1,0:T(8,128)(2,1)} %bitcast.46, ...), custom_call_target="tpu_custom_call" | custom-call | bytes 16777216 | tf_op jit(solution)/shard_map/pallas_call | solution.py:148
  153.5 5.3 %collective-permute-done.29 = bf16[16,8192]{1,0:T(8,128)(2,1)S(1)} collective-permute-done((bf16[16,8192]{1,0:T(8,128)(2,1)S(1)}, bf16[16,8192]{1,0:T(8,128)(2,1)S(1)}, u32[]{:S(2)}, u32[]{:S(2)}) %collective-permute-start.29) | collective-permute-done | bytes 262176 | tf_op jit(solution)/shard_map/ppermute | solution.py:53
  163.5 4.0 %shard_map.160 = (bf16[8192,256]{1,0:T(8,128)(2,1)S(1)}, bf16[8192,256]{1,0:T(8,128)(2,1)S(1)}, bf16[16,8192]{1,0:T(8,128)(2,1)S(1)}) custom-call(s32[17]{0:T(128)S(1)} %pad_add_fusion.refs_8_.go_ref.groups_ref, bf16[8192,2048]{1,0:T(8,128)(2,1)} %bitcast.50, bf16[8192,2048]{1,0:T(8,128)(2,1)} %bitcast.51, bf16[16,8192]{1,0:T(8,128)(2,1)S(1)} %fusion.12.refs_2_), custom_call_target="tpu_custom_call" | custom-call | bytes 8388608 | tf_op jit(solution)/shard_map/pallas_call | solution.py:148
  168.2 6.6 %collective-permute-done.33.refs_2_ = bf16[16,8192]{1,0:T(8,128)(2,1)S(1)} collective-permute-done((bf16[16,8192]{1,0:T(8,128)(2,1)S(1)}, bf16[16,8192]{1,0:T(8,128)(2,1)S(1)}, u32[]{:S(2)}, u32[]{:S(2)}) %collective-permute-start.33) | collective-permute-done | bytes 262176 | tf_op jit(solution)/shard_map/ppermute | solution.py:53
  176.7 5.8 %shard_map.161 = (bf16[128,8192]{1,0:T(8,128)(2,1)S(1)}, f32[128,32]{1,0:T(8,128)S(1)}, bf16[128,512]{1,0:T(8,128)(2,1)S(1)}) custom-call(bf16[16,8192]{1,0:T(8,128)(2,1)S(1)} %get-tuple-element.94.refs_0_, bf16[16,8192]{1,0:T(8,128)(2,1)S(1)} %collective-permute-done.32.refs_1_, bf16[16,8192]{1,0:T(8,128)(2,1)S(1)} %collective-permute-done.33.refs_2_, ...), custom_call_target="tpu_custom_call" | custom-call | flops 1140850688 | bytes 8388608 | tf_op jit(solution)/shard_map/pallas_call | solution.py:208
  186.0 6.4 %shard_map.162 = (f32[128,2048]{1,0:T(8,128)S(1)}, bf16[128,128]{1,0:T(8,128)(2,1)S(1)}) custom-call(s32[17]{0:T(128)S(1)} %pad_add_fusion.refs_8_.go_ref.groups_ref, bf16[128,8192]{1,0:T(8,128)(2,1)S(1)} %get-tuple-element.95.normed_ref, bf16[128,128]{1,0:T(8,128)(2,1)S(1)} %get-tuple-element.157.value_ref, ...), custom_call_target="tpu_custom_call" | custom-call | flops 4294967296 | bytes 2097152 | tf_op jit(solution)/shard_map/pallas_call | solution.py:250
  193.9 15.7 %shard_map.164 = (bf16[64,8192]{1,0:T(8,128)(2,1)S(1)}, bf16[64,8192]{1,0:T(8,128)(2,1)S(1)}, bf16[128,2048]{1,0:T(8,128)(2,1)}, bf16[128,256]{1,0:T(8,128)(2,1)}, f32[1,32]{1,0:T(1,128)}) custom-call(s32[17]{0:T(128)S(1)} %pad_add_fusion.refs_8_.go_ref.groups_ref, s32[1]{0:T(128)} %bitcast.14.flag_ref, ...), custom_call_target="tpu_custom_call", output_to_operand_aliasing={{2}: (9, {}), {3}: (10, {}), {4}: (11, {})} | custom-call | flops 4496293888 | bytes 33554432 | tf_op jit(solution)/shard_map/pallas_call | solution.py:422
  216.3 6.5 %shard_map.165 = (bf16[8192,256]{1,0:T(8,128)(2,1)S(1)}, bf16[8192,256]{1,0:T(8,128)(2,1)S(1)}, bf16[8192,256]{1,0:T(8,128)(2,1)S(1)}, bf16[8192,256]{1,0:T(8,128)(2,1)S(1)}, bf16[16,8192]{1,0:T(8,128)(2,1)S(1)}) custom-call(s32[17]{0:T(128)S(1)} %pad_add_fusion.refs_8_.go_ref.groups_ref, bf16[8192,2048]{1,0:T(8,128)(2,1)} %bitcast.53, ...), custom_call_target="tpu_custom_call" | custom-call | bytes 16777216 | tf_op jit(solution)/shard_map/pallas_call | solution.py:148
  222.8 4.5 %collective-permute-done.45 = bf16[16,8192]{1,0:T(8,128)(2,1)S(1)} collective-permute-done((bf16[16,8192]{1,0:T(8,128)(2,1)S(1)}, bf16[16,8192]{1,0:T(8,128)(2,1)S(1)}, u32[]{:S(2)}, u32[]{:S(2)}) %collective-permute-start.45) | collective-permute-done | bytes 262176 | tf_op jit(solution)/shard_map/ppermute | solution.py:53
  228.1 10.2 %collective-permute-start.47 = (bf16[16,8192]{1,0:T(8,128)(2,1)S(1)}, bf16[16,8192]{1,0:T(8,128)(2,1)S(1)}, u32[]{:S(2)}, u32[]{:S(2)}) collective-permute-start(bf16[16,8192]{1,0:T(8,128)(2,1)S(1)} %fusion.13), channel_id=1, source_target_pairs={{0,8},{8,0},{16,24},{24,16},{1,9},{9,1},{17,25},{25,17},{2,10},{10... | collective-permute-start | bytes 786440 | tf_op jit(solution)/shard_map/ppermute | solution.py:61
  238.3 5.5 %collective-permute-done.47 = bf16[16,8192]{1,0:T(8,128)(2,1)S(1)} collective-permute-done((bf16[16,8192]{1,0:T(8,128)(2,1)S(1)}, bf16[16,8192]{1,0:T(8,128)(2,1)S(1)}, u32[]{:S(2)}, u32[]{:S(2)}) %collective-permute-start.47) | collective-permute-done | bytes 262176 | tf_op jit(solution)/shard_map/ppermute | solution.py:61
  248.1 4.0 %shard_map.166 = (bf16[8192,256]{1,0:T(8,128)(2,1)S(1)}, bf16[8192,256]{1,0:T(8,128)(2,1)S(1)}, bf16[16,8192]{1,0:T(8,128)(2,1)S(1)}) custom-call(s32[17]{0:T(128)S(1)} %pad_add_fusion.refs_8_.go_ref.groups_ref, bf16[8192,2048]{1,0:T(8,128)(2,1)} %bitcast.57, bf16[8192,2048]{1,0:T(8,128)(2,1)} %bitcast.58, bf16[16,8192]{1,0:T(8,128)(2,1)S(1)} %fusion.16.refs_2_), custom_call_target="tpu_custom_call" | custom-call | bytes 8388608 | tf_op jit(solution)/shard_map/pallas_call | solution.py:148
  253.1 6.2 %collective-permute-done.49.refs_2_ = bf16[16,8192]{1,0:T(8,128)(2,1)S(1)} collective-permute-done((bf16[16,8192]{1,0:T(8,128)(2,1)S(1)}, bf16[16,8192]{1,0:T(8,128)(2,1)S(1)}, u32[]{:S(2)}, u32[]{:S(2)}) %collective-permute-start.49) | collective-permute-done | bytes 262176 | tf_op jit(solution)/shard_map/ppermute | solution.py:53
  261.3 5.8 %shard_map.167 = (bf16[128,8192]{1,0:T(8,128)(2,1)S(1)}, f32[128,32]{1,0:T(8,128)S(1)}, bf16[128,512]{1,0:T(8,128)(2,1)S(1)}) custom-call(bf16[16,8192]{1,0:T(8,128)(2,1)S(1)} %get-tuple-element.112.refs_0_, bf16[16,8192]{1,0:T(8,128)(2,1)S(1)} %collective-permute-done.48.refs_1_, bf16[16,8192]{1,0:T(8,128)(2,1)S(1)} %collective-permute-done.49.refs_2_, ...), custom_call_target="tpu_custom_call" | custom-call | flops 1140850688 | bytes 8388608 | tf_op jit(solution)/shard_map/pallas_call | solution.py:208
  270.4 6.7 %shard_map.168 = (f32[128,2048]{1,0:T(8,128)S(1)}, bf16[128,128]{1,0:T(8,128)(2,1)S(1)}) custom-call(s32[17]{0:T(128)S(1)} %pad_add_fusion.refs_8_.go_ref.groups_ref, bf16[128,8192]{1,0:T(8,128)(2,1)S(1)} %get-tuple-element.113.normed_ref, bf16[128,128]{1,0:T(8,128)(2,1)S(1)} %get-tuple-element.153.value_ref, ...), custom_call_target="tpu_custom_call" | custom-call | flops 4294967296 | bytes 2097152 | tf_op jit(solution)/shard_map/pallas_call | solution.py:250
  278.6 15.7 %shard_map.170 = (bf16[64,8192]{1,0:T(8,128)(2,1)S(1)}, bf16[64,8192]{1,0:T(8,128)(2,1)S(1)}, bf16[128,2048]{1,0:T(8,128)(2,1)}, bf16[128,256]{1,0:T(8,128)(2,1)}, f32[1,32]{1,0:T(1,128)}) custom-call(s32[17]{0:T(128)S(1)} %pad_add_fusion.refs_8_.go_ref.groups_ref, s32[1]{0:T(128)} %bitcast.15.flag_ref, ...), custom_call_target="tpu_custom_call", output_to_operand_aliasing={{2}: (9, {}), {3}: (10, {}), {4}: (11, {})} | custom-call | flops 4496293888 | bytes 33554432 | tf_op jit(solution)/shard_map/pallas_call | solution.py:422
  306.0 6.0 %collective-permute-done.61 = bf16[16,8192]{1,0:T(8,128)(2,1)S(1)} collective-permute-done((bf16[16,8192]{1,0:T(8,128)(2,1)S(1)}, bf16[16,8192]{1,0:T(8,128)(2,1)S(1)}, u32[]{:S(2)}, u32[]{:S(2)}) %collective-permute-start.61) | collective-permute-done | bytes 262176 | tf_op jit(solution)/shard_map/ppermute | solution.py:53
  (197 shorter events, 86.8 us)
Async XLA Ops:
  2.9 9.7 %collective-permute-start = (bf16[16,8192]{1,0:T(8,128)(2,1)S(1)}, bf16[16,8192]{1,0:T(8,128)(2,1)S(1)}, u32[]{:S(2)}, u32[]{:S(2)}) collective-permute-start(bf16[16,8192]{1,0:T(8,128)(2,1)S(1)} %fusion.3.refs_0_), channel_id=1, source_target_pairs={{0,2},{1,3},{2,6},{3,7},{6,4},{7,5},{4,0},{5,1},{8,10},{9,11},{10,... | collective-permute-start | bytes 786440 | tf_op jit(solution)/shard_map/ppermute | solution.py:53
  5.9 13.1 %collective-permute-start.1 = (bf16[16,8192]{1,0:T(8,128)(2,1)S(1)}, bf16[16,8192]{1,0:T(8,128)(2,1)S(1)}, u32[]{:S(2)}, u32[]{:S(2)}) collective-permute-start(bf16[16,8192]{1,0:T(8,128)(2,1)S(1)} %fusion.3.refs_0_), channel_id=1, source_target_pairs={{0,6},{1,7},{2,4},{3,5},{6,0},{7,1},{4,2},{5,3},{8,14},{9,15},{10,... | collective-permute-start | bytes 786440 | tf_op jit(solution)/shard_map/ppermute | solution.py:53
  7.4 11.8 %collective-permute-start.2 = (bf16[16,8192]{1,0:T(8,128)(2,1)S(1)}, bf16[16,8192]{1,0:T(8,128)(2,1)S(1)}, u32[]{:S(2)}, u32[]{:S(2)}) collective-permute-start(bf16[16,8192]{1,0:T(8,128)(2,1)S(1)} %fusion.3.refs_0_), channel_id=1, source_target_pairs={{0,4},{1,5},{2,0},{3,1},{6,2},{7,3},{4,6},{5,7},{8,12},{9,13},{10,... | collective-permute-start | bytes 786440 | tf_op jit(solution)/shard_map/ppermute | solution.py:53
  8.9 10.8 %collective-permute-start.3 = (bf16[16,8192]{1,0:T(8,128)(2,1)S(1)}, bf16[16,8192]{1,0:T(8,128)(2,1)S(1)}, u32[]{:S(2)}, u32[]{:S(2)}) collective-permute-start(bf16[16,8192]{1,0:T(8,128)(2,1)S(1)} %fusion.3.refs_0_), channel_id=1, source_target_pairs={{0,1},{1,0},{2,3},{3,2},{4,5},{5,4},{6,7},{7,6},{8,9},{9,8},{10,11... | collective-permute-start | bytes 786440 | tf_op jit(solution)/shard_map/ppermute | solution.py:44
  26.8 17.2 %collective-permute-start.7 = (bf16[128,128]{1,0:T(8,128)(2,1)S(1)}, bf16[128,128]{1,0:T(8,128)(2,1)S(1)}, u32[]{:S(2)}, u32[]{:S(2)}) collective-permute-start(bf16[128,128]{1,0:T(8,128)(2,1)S(1)} %get-tuple-element.164), channel_id=1, source_target_pairs={{0,2},{1,3},{2,6},{3,7},{6,4},{7,5},{4,0},{5,1},{8,10},{9,11},{10,... | collective-permute-start | bytes 98312 | tf_op jit(solution)/shard_map/ppermute | solution.py:53
  28.3 15.7 %collective-permute-start.8 = (bf16[128,128]{1,0:T(8,128)(2,1)S(1)}, bf16[128,128]{1,0:T(8,128)(2,1)S(1)}, u32[]{:S(2)}, u32[]{:S(2)}) collective-permute-start(bf16[128,128]{1,0:T(8,128)(2,1)S(1)} %get-tuple-element.163), channel_id=1, source_target_pairs={{0,6},{1,7},{2,4},{3,5},{6,0},{7,1},{4,2},{5,3},{8,14},{9,15},{10,... | collective-permute-start | bytes 98312 | tf_op jit(solution)/shard_map/ppermute | solution.py:53
  29.5 14.5 %collective-permute-start.9 = (bf16[128,128]{1,0:T(8,128)(2,1)S(1)}, bf16[128,128]{1,0:T(8,128)(2,1)S(1)}, u32[]{:S(2)}, u32[]{:S(2)}) collective-permute-start(bf16[128,128]{1,0:T(8,128)(2,1)S(1)} %get-tuple-element.162), channel_id=1, source_target_pairs={{0,4},{1,5},{2,0},{3,1},{6,2},{7,3},{4,6},{5,7},{8,12},{9,13},{10,... | collective-permute-start | bytes 98312 | tf_op jit(solution)/shard_map/ppermute | solution.py:53
  68.5 9.2 %collective-permute-start.12 = (bf16[16,8192]{1,0:T(8,128)(2,1)S(1)}, bf16[16,8192]{1,0:T(8,128)(2,1)S(1)}, u32[]{:S(2)}, u32[]{:S(2)}) collective-permute-start(bf16[16,8192]{1,0:T(8,128)(2,1)S(1)} %get-tuple-element.149), channel_id=1, source_target_pairs={{0,2},{1,3},{2,6},{3,7},{6,4},{7,5},{4,0},{5,1},{8,10},{9,11},{10,... | collective-permute-start | bytes 786440 | tf_op jit(solution)/shard_map/ppermute | solution.py:53
  68.9 13.9 %collective-permute-start.13 = (bf16[16,8192]{1,0:T(8,128)(2,1)S(1)}, bf16[16,8192]{1,0:T(8,128)(2,1)S(1)}, u32[]{:S(2)}, u32[]{:S(2)}) collective-permute-start(bf16[16,8192]{1,0:T(8,128)(2,1)S(1)} %get-tuple-element.148), channel_id=1, source_target_pairs={{0,6},{1,7},{2,4},{3,5},{6,0},{7,1},{4,2},{5,3},{8,14},{9,15},{10,... | collective-permute-start | bytes 786440 | tf_op jit(solution)/shard_map/ppermute | solution.py:53
  70.6 13.4 %collective-permute-start.14 = (bf16[16,8192]{1,0:T(8,128)(2,1)S(1)}, bf16[16,8192]{1,0:T(8,128)(2,1)S(1)}, u32[]{:S(2)}, u32[]{:S(2)}) collective-permute-start(bf16[16,8192]{1,0:T(8,128)(2,1)S(1)} %get-tuple-element.147), channel_id=1, source_target_pairs={{0,4},{1,5},{2,0},{3,1},{6,2},{7,3},{4,6},{5,7},{8,12},{9,13},{10,... | collective-permute-start | bytes 786440 | tf_op jit(solution)/shard_map/ppermute | solution.py:53
  93.4 11.4 %collective-permute-start.17 = (bf16[16,8192]{1,0:T(8,128)(2,1)S(1)}, bf16[16,8192]{1,0:T(8,128)(2,1)S(1)}, u32[]{:S(2)}, u32[]{:S(2)}) collective-permute-start(bf16[16,8192]{1,0:T(8,128)(2,1)S(1)} %fusion.8.refs_2_), channel_id=1, source_target_pairs={{0,6},{1,7},{2,4},{3,5},{6,0},{7,1},{4,2},{5,3},{8,14},{9,15},{10,... | collective-permute-start | bytes 786440 | tf_op jit(solution)/shard_map/ppermute | solution.py:53
  94.5 10.9 %collective-permute-start.18 = (bf16[16,8192]{1,0:T(8,128)(2,1)S(1)}, bf16[16,8192]{1,0:T(8,128)(2,1)S(1)}, u32[]{:S(2)}, u32[]{:S(2)}) collective-permute-start(bf16[16,8192]{1,0:T(8,128)(2,1)S(1)} %fusion.8.refs_2_), channel_id=1, source_target_pairs={{0,4},{1,5},{2,0},{3,1},{6,2},{7,3},{4,6},{5,7},{8,12},{9,13},{10,... | collective-permute-start | bytes 786440 | tf_op jit(solution)/shard_map/ppermute | solution.py:53
  112.8 11.2 %collective-permute-start.23 = (bf16[128,128]{1,0:T(8,128)(2,1)S(1)}, bf16[128,128]{1,0:T(8,128)(2,1)S(1)}, u32[]{:S(2)}, u32[]{:S(2)}) collective-permute-start(bf16[128,128]{1,0:T(8,128)(2,1)S(1)} %get-tuple-element.160), channel_id=1, source_target_pairs={{0,2},{1,3},{2,6},{3,7},{6,4},{7,5},{4,0},{5,1},{8,10},{9,11},{10,... | collective-permute-start | bytes 98312 | tf_op jit(solution)/shard_map/ppermute | solution.py:53
  114.8 9.2 %collective-permute-start.24 = (bf16[128,128]{1,0:T(8,128)(2,1)S(1)}, bf16[128,128]{1,0:T(8,128)(2,1)S(1)}, u32[]{:S(2)}, u32[]{:S(2)}) collective-permute-start(bf16[128,128]{1,0:T(8,128)(2,1)S(1)} %get-tuple-element.159), channel_id=1, source_target_pairs={{0,6},{1,7},{2,4},{3,5},{6,0},{7,1},{4,2},{5,3},{8,14},{9,15},{10,... | collective-permute-start | bytes 98312 | tf_op jit(solution)/shard_map/ppermute | solution.py:53
  144.2 9.3 %collective-permute-start.28 = (bf16[16,8192]{1,0:T(8,128)(2,1)S(1)}, bf16[16,8192]{1,0:T(8,128)(2,1)S(1)}, u32[]{:S(2)}, u32[]{:S(2)}) collective-permute-start(bf16[16,8192]{1,0:T(8,128)(2,1)S(1)} %get-tuple-element.145), channel_id=1, source_target_pairs={{0,2},{1,3},{2,6},{3,7},{6,4},{7,5},{4,0},{5,1},{8,10},{9,11},{10,... | collective-permute-start | bytes 786440 | tf_op jit(solution)/shard_map/ppermute | solution.py:53
  144.9 13.9 %collective-permute-start.29 = (bf16[16,8192]{1,0:T(8,128)(2,1)S(1)}, bf16[16,8192]{1,0:T(8,128)(2,1)S(1)}, u32[]{:S(2)}, u32[]{:S(2)}) collective-permute-start(bf16[16,8192]{1,0:T(8,128)(2,1)S(1)} %get-tuple-element.144), channel_id=1, source_target_pairs={{0,6},{1,7},{2,4},{3,5},{6,0},{7,1},{4,2},{5,3},{8,14},{9,15},{10,... | collective-permute-start | bytes 786440 | tf_op jit(solution)/shard_map/ppermute | solution.py:53
  146.9 12.6 %collective-permute-start.30 = (bf16[16,8192]{1,0:T(8,128)(2,1)S(1)}, bf16[16,8192]{1,0:T(8,128)(2,1)S(1)}, u32[]{:S(2)}, u32[]{:S(2)}) collective-permute-start(bf16[16,8192]{1,0:T(8,128)(2,1)S(1)} %get-tuple-element.143), channel_id=1, source_target_pairs={{0,4},{1,5},{2,0},{3,1},{6,2},{7,3},{4,6},{5,7},{8,12},{9,13},{10,... | collective-permute-start | bytes 786440 | tf_op jit(solution)/shard_map/ppermute | solution.py:53
  161.4 13.4 %collective-permute-start.33 = (bf16[16,8192]{1,0:T(8,128)(2,1)S(1)}, bf16[16,8192]{1,0:T(8,128)(2,1)S(1)}, u32[]{:S(2)}, u32[]{:S(2)}) collective-permute-start(bf16[16,8192]{1,0:T(8,128)(2,1)S(1)} %fusion.12.refs_2_), channel_id=1, source_target_pairs={{0,6},{1,7},{2,4},{3,5},{6,0},{7,1},{4,2},{5,3},{8,14},{9,15},{10,... | collective-permute-start | bytes 786440 | tf_op jit(solution)/shard_map/ppermute | solution.py:53
  163.3 11.6 %collective-permute-start.34 = (bf16[16,8192]{1,0:T(8,128)(2,1)S(1)}, bf16[16,8192]{1,0:T(8,128)(2,1)S(1)}, u32[]{:S(2)}, u32[]{:S(2)}) collective-permute-start(bf16[16,8192]{1,0:T(8,128)(2,1)S(1)} %fusion.12.refs_2_), channel_id=1, source_target_pairs={{0,4},{1,5},{2,0},{3,1},{6,2},{7,3},{4,6},{5,7},{8,12},{9,13},{10,... | collective-permute-start | bytes 786440 | tf_op jit(solution)/shard_map/ppermute | solution.py:53
  182.6 9.9 %collective-permute-start.39 = (bf16[128,128]{1,0:T(8,128)(2,1)S(1)}, bf16[128,128]{1,0:T(8,128)(2,1)S(1)}, u32[]{:S(2)}, u32[]{:S(2)}) collective-permute-start(bf16[128,128]{1,0:T(8,128)(2,1)S(1)} %get-tuple-element.156), channel_id=1, source_target_pairs={{0,2},{1,3},{2,6},{3,7},{6,4},{7,5},{4,0},{5,1},{8,10},{9,11},{10,... | collective-permute-start | bytes 98312 | tf_op jit(solution)/shard_map/ppermute | solution.py:53
  183.7 8.8 %collective-permute-start.40 = (bf16[128,128]{1,0:T(8,128)(2,1)S(1)}, bf16[128,128]{1,0:T(8,128)(2,1)S(1)}, u32[]{:S(2)}, u32[]{:S(2)}) collective-permute-start(bf16[128,128]{1,0:T(8,128)(2,1)S(1)} %get-tuple-element.155), channel_id=1, source_target_pairs={{0,6},{1,7},{2,4},{3,5},{6,0},{7,1},{4,2},{5,3},{8,14},{9,15},{10,... | collective-permute-start | bytes 98312 | tf_op jit(solution)/shard_map/ppermute | solution.py:53
  212.7 10.1 %collective-permute-start.44 = (bf16[16,8192]{1,0:T(8,128)(2,1)S(1)}, bf16[16,8192]{1,0:T(8,128)(2,1)S(1)}, u32[]{:S(2)}, u32[]{:S(2)}) collective-permute-start(bf16[16,8192]{1,0:T(8,128)(2,1)S(1)} %get-tuple-element.141), channel_id=1, source_target_pairs={{0,2},{1,3},{2,6},{3,7},{6,4},{7,5},{4,0},{5,1},{8,10},{9,11},{10,... | collective-permute-start | bytes 786440 | tf_op jit(solution)/shard_map/ppermute | solution.py:53
  214.0 13.3 %collective-permute-start.45 = (bf16[16,8192]{1,0:T(8,128)(2,1)S(1)}, bf16[16,8192]{1,0:T(8,128)(2,1)S(1)}, u32[]{:S(2)}, u32[]{:S(2)}) collective-permute-start(bf16[16,8192]{1,0:T(8,128)(2,1)S(1)} %get-tuple-element.140), channel_id=1, source_target_pairs={{0,6},{1,7},{2,4},{3,5},{6,0},{7,1},{4,2},{5,3},{8,14},{9,15},{10,... | collective-permute-start | bytes 786440 | tf_op jit(solution)/shard_map/ppermute | solution.py:53
  215.3 12.6 %collective-permute-start.46 = (bf16[16,8192]{1,0:T(8,128)(2,1)S(1)}, bf16[16,8192]{1,0:T(8,128)(2,1)S(1)}, u32[]{:S(2)}, u32[]{:S(2)}) collective-permute-start(bf16[16,8192]{1,0:T(8,128)(2,1)S(1)} %get-tuple-element.139), channel_id=1, source_target_pairs={{0,4},{1,5},{2,0},{3,1},{6,2},{7,3},{4,6},{5,7},{8,12},{9,13},{10,... | collective-permute-start | bytes 786440 | tf_op jit(solution)/shard_map/ppermute | solution.py:53
  228.1 15.7 %collective-permute-start.47 = (bf16[16,8192]{1,0:T(8,128)(2,1)S(1)}, bf16[16,8192]{1,0:T(8,128)(2,1)S(1)}, u32[]{:S(2)}, u32[]{:S(2)}) collective-permute-start(bf16[16,8192]{1,0:T(8,128)(2,1)S(1)} %fusion.13), channel_id=1, source_target_pairs={{0,8},{8,0},{16,24},{24,16},{1,9},{9,1},{17,25},{25,17},{2,10},{10... | collective-permute-start | bytes 786440 | tf_op jit(solution)/shard_map/ppermute | solution.py:61
  244.1 9.0 %collective-permute-start.48 = (bf16[16,8192]{1,0:T(8,128)(2,1)S(1)}, bf16[16,8192]{1,0:T(8,128)(2,1)S(1)}, u32[]{:S(2)}, u32[]{:S(2)}) collective-permute-start(bf16[16,8192]{1,0:T(8,128)(2,1)S(1)} %fusion.16.refs_2_), channel_id=1, source_target_pairs={{0,2},{1,3},{2,6},{3,7},{6,4},{7,5},{4,0},{5,1},{8,10},{9,11},{10,... | collective-permute-start | bytes 786440 | tf_op jit(solution)/shard_map/ppermute | solution.py:53
  246.4 13.0 %collective-permute-start.49 = (bf16[16,8192]{1,0:T(8,128)(2,1)S(1)}, bf16[16,8192]{1,0:T(8,128)(2,1)S(1)}, u32[]{:S(2)}, u32[]{:S(2)}) collective-permute-start(bf16[16,8192]{1,0:T(8,128)(2,1)S(1)} %fusion.16.refs_2_), channel_id=1, source_target_pairs={{0,6},{1,7},{2,4},{3,5},{6,0},{7,1},{4,2},{5,3},{8,14},{9,15},{10,... | collective-permute-start | bytes 786440 | tf_op jit(solution)/shard_map/ppermute | solution.py:53
  248.1 11.4 %collective-permute-start.50 = (bf16[16,8192]{1,0:T(8,128)(2,1)S(1)}, bf16[16,8192]{1,0:T(8,128)(2,1)S(1)}, u32[]{:S(2)}, u32[]{:S(2)}) collective-permute-start(bf16[16,8192]{1,0:T(8,128)(2,1)S(1)} %fusion.16.refs_2_), channel_id=1, source_target_pairs={{0,4},{1,5},{2,0},{3,1},{6,2},{7,3},{4,6},{5,7},{8,12},{9,13},{10,... | collective-permute-start | bytes 786440 | tf_op jit(solution)/shard_map/ppermute | solution.py:53
  267.1 10.0 %collective-permute-start.55 = (bf16[128,128]{1,0:T(8,128)(2,1)S(1)}, bf16[128,128]{1,0:T(8,128)(2,1)S(1)}, u32[]{:S(2)}, u32[]{:S(2)}) collective-permute-start(bf16[128,128]{1,0:T(8,128)(2,1)S(1)} %get-tuple-element.152), channel_id=1, source_target_pairs={{0,2},{1,3},{2,6},{3,7},{6,4},{7,5},{4,0},{5,1},{8,10},{9,11},{10,... | collective-permute-start | bytes 98312 | tf_op jit(solution)/shard_map/ppermute | solution.py:53
  268.1 9.0 %collective-permute-start.56 = (bf16[128,128]{1,0:T(8,128)(2,1)S(1)}, bf16[128,128]{1,0:T(8,128)(2,1)S(1)}, u32[]{:S(2)}, u32[]{:S(2)}) collective-permute-start(bf16[128,128]{1,0:T(8,128)(2,1)S(1)} %get-tuple-element.151), channel_id=1, source_target_pairs={{0,6},{1,7},{2,4},{3,5},{6,0},{7,1},{4,2},{5,3},{8,14},{9,15},{10,... | collective-permute-start | bytes 98312 | tf_op jit(solution)/shard_map/ppermute | solution.py:53
  298.9 13.2 %collective-permute-start.61 = (bf16[16,8192]{1,0:T(8,128)(2,1)S(1)}, bf16[16,8192]{1,0:T(8,128)(2,1)S(1)}, u32[]{:S(2)}, u32[]{:S(2)}) collective-permute-start(bf16[16,8192]{1,0:T(8,128)(2,1)S(1)} %get-tuple-element.136), channel_id=1, source_target_pairs={{0,6},{1,7},{2,4},{3,5},{6,0},{7,1},{4,2},{5,3},{8,14},{9,15},{10,... | collective-permute-start | bytes 786440 | tf_op jit(solution)/shard_map/ppermute | solution.py:53
  300.1 12.6 %collective-permute-start.62 = (bf16[16,8192]{1,0:T(8,128)(2,1)S(1)}, bf16[16,8192]{1,0:T(8,128)(2,1)S(1)}, u32[]{:S(2)}, u32[]{:S(2)}) collective-permute-start(bf16[16,8192]{1,0:T(8,128)(2,1)S(1)} %get-tuple-element.135), channel_id=1, source_target_pairs={{0,4},{1,5},{2,0},{3,1},{6,2},{7,3},{4,6},{5,7},{8,12},{9,13},{10,... | collective-permute-start | bytes 786440 | tf_op jit(solution)/shard_map/ppermute | solution.py:53
  (46 other events, 269.7 us)

commit v3 on v2

--- a/solution.py
+++ b/solution.py
@@ -13,8 +13,10 @@
 BF = jnp.bfloat16
 F32 = jnp.float32
 HIGHEST = lax.Precision.HIGHEST
-SUM_LOADS = 4
-HELD = 6
+SUM_LOADS = 5
+HELD = 8
+SLOTS = 4
+BC_HELD = True
 OUT_COLS = 1024
 SCAN_MIB = 28
 
@@ -158,18 +160,22 @@
     return held, value
 
 
-def first_kernel(count, micro, local, *refs):
-    pieces, (go_ref, wdt_ref, wbc_ref, normed_ref, dt_ref, bc_ref, late, wdt, sems) = refs[:count], refs[count:]
+def first_kernel(count, held_count, micro, local, *refs):
+    pieces, go_ref, wdt_ref, wbc_ref = refs[:count], *refs[count:count + 3]
+    held, (normed_ref, dt_ref, bc_ref, late, wdt, sems) = refs[count + 3:count + 3 + held_count], refs[count + 3 + held_count:]
     rows = pieces[0].shape[0]
-    blocks, _, cols = late.shape
+    bc_cols = wbc_ref.shape[1]
+    cols = held[0].shape[1] if held else late.shape[2]
+    blocks = bc_cols // cols
 
     def fetch(i):
         return pltpu.make_async_copy(wbc_ref.at[:, pl.ds(i * cols, cols)], late.at[i], sems.at[i])
 
-    steps = pltpu.make_async_copy(wdt_ref, wdt, sems.at[blocks])
+    steps = pltpu.make_async_copy(wdt_ref, wdt, sems.at[sems.shape[0] - 1])
     steps.start()
-    for i in range(blocks):
-        fetch(i).start()
+    if not held:
+        for i in range(blocks):
+            fetch(i).start()
 
     @pl.when(go_ref[0] >= 0)
     def _():
@@ -186,44 +192,48 @@
     gather = gather_order(head, all_rows, micro, local)
     total = jnp.zeros(bc_ref.shape, F32)
     for i in range(blocks):
-        fetch(i).wait()
-        part = dot(normed_ref[...], late[i]).astype(BF)
+        if not held:
+            fetch(i).wait()
+        part = dot(normed_ref[...], held[i][...] if held else late[i]).astype(BF)
         part = dot(gather, part).astype(BF)
         total += dot(part, pick_columns(head, i * cols, cols, blocks * cols, devices))
     bc_ref[...] = total.astype(BF)
 
 
-def project_first(go, pieces, micro, local, w_bc, w_dt):
+def project_first(go, pieces, micro, local, w_bc, w_dt, held):
     width, bc_cols = w_bc.shape
     rows = len(pieces) * pieces[0].shape[0]
     heads = w_dt.shape[0]
     vmem = pl.BlockSpec(memory_space=pltpu.VMEM)
     block = min(256, bc_cols)
     args = (*pieces, go, pltpu.with_memory_space_constraint(w_dt, pltpu.HBM), pltpu.with_memory_space_constraint(w_bc, pltpu.HBM))
+    args += tuple(pltpu.with_memory_space_constraint(w, pltpu.VMEM) for w in held)
+    late = (1, 16, 128) if held else (bc_cols // block, width, block)
     shapes = [
         jax.ShapeDtypeStruct((rows, width), BF),
         jax.ShapeDtypeStruct((rows, heads), F32),
         jax.ShapeDtypeStruct((rows, bc_cols // GROUPS * (rows // (micro * local))), BF),
     ]
     return pl.pallas_call(
-        functools.partial(first_kernel, len(pieces), micro, local),
+        functools.partial(first_kernel, len(pieces), len(held), micro, local),
         in_specs=[vmem] * len(pieces) + [pl.BlockSpec(memory_space=pltpu.SMEM)]
-        + [pl.BlockSpec(memory_space=pl.ANY)] * 2,
+        + [pl.BlockSpec(memory_space=pl.ANY)] * 2 + [vmem] * len(held),
         out_specs=[vmem] * 3,
         out_shape=shapes,
         scratch_shapes=[
-            pltpu.VMEM((bc_cols // block, width, block), BF),
+            pltpu.VMEM(late, BF),
             pltpu.VMEM(w_dt.shape, BF),
-            pltpu.SemaphoreType.DMA((bc_cols // block + 1,)),
+            pltpu.SemaphoreType.DMA((late[0] + 1,)),
         ],
-        compiler_params=params(12),
+        compiler_params=params(4 if held else 12),
         cost_estimate=cost(2 * rows * width * (bc_cols + heads), 2 * w_bc.size),
     )(*args)
 
 
 def held_kernel(count, go_ref, normed_ref, value_ref, *refs):
     held, (w_ref, x_ref, copy_ref, late, sems) = refs[:count], refs[count:]
-    rest, _, cols = late.shape
+    cols = late.shape[2]
+    rest = w_ref.shape[1] // cols - count
 
     def fetch(i):
         return pltpu.make_async_copy(w_ref.at[:, pl.ds((count + i) * cols, cols)], late.at[i], sems.at[i])
@@ -252,7 +262,10 @@
         in_specs=[pl.BlockSpec(memory_space=pltpu.SMEM)] + [vmem] * (len(held) + 2) + [pl.BlockSpec(memory_space=pl.ANY)],
         out_specs=[vmem, vmem],
         out_shape=[jax.ShapeDtypeStruct((rows, cols), F32), jax.ShapeDtypeStruct(value.shape, value.dtype)],
-        scratch_shapes=[pltpu.VMEM((rest, width, block), BF), pltpu.SemaphoreType.DMA((rest,))],
+        scratch_shapes=[
+            pltpu.VMEM((rest, width, block) if rest else (1, 16, block), BF),
+            pltpu.SemaphoreType.DMA((max(rest, 1),)),
+        ],
         compiler_params=params(4 + 2 * rest * width * block // MIB),
         cost_estimate=cost(2 * rows * width * cols, 2 * rows * width),
     )(go, normed, value, *[pltpu.with_memory_space_constraint(w, pltpu.VMEM) for w in held],
@@ -413,7 +426,7 @@
 def scan_and_out(micro, group_rows, taps, groups, flag, x_proj, here, over, dt_raw, const, state, old, w_out):
     rows, channels = x_proj.shape
     width = w_out.shape[1]
-    block, slots = OUT_COLS, 4
+    block, slots = OUT_COLS, SLOTS
     far = [pltpu.with_memory_space_constraint(a, pltpu.HBM) for a in (const, state, w_out, *old)]
     shapes = [jax.ShapeDtypeStruct((rows // 2, width), BF)] * 2 + [jax.ShapeDtypeStruct(o.shape, o.dtype) for o in old]
     vmem = pl.BlockSpec(memory_space=pltpu.VMEM)
@@ -511,7 +524,7 @@
 
     block = 256 if channels >= 2048 else 128
     count = channels // block
-    kept = min(HELD, count - 1)
+    kept = min(HELD, count)
     in_sum = min(SUM_LOADS, kept)
     inner_plan = [(w_x[0], block, i) for i in range(kept)]
     go = groups
@@ -523,7 +536,8 @@
         jnp.zeros((rows, STATE), BF),
         jnp.zeros((1, local_heads), F32),
     )
-    held = []
+    bc_plan = [(w_bc[0], 256, i) for i in range(bc_cols // 256)] if BC_HELD else []
+    held, held_bc = [], []
     for tick in range(segments):
         last = tick + 1 == segments
         active = segment == tick
@@ -531,13 +545,13 @@
         normed = rms_rows(current, norm_gain[0])
         arrived = [ring_shift(normed, s) for s in range(1, chips)]
         if tick:
-            more, normed = load_beside(go, inner_plan[in_sum:], normed)
-            held = held + more
+            more, normed = load_beside(go, inner_plan[in_sum:] + bc_plan, normed)
+            held, held_bc = held + more[:kept - in_sum], more[kept - in_sum:]
         pieces = [normed] + arrived
         if own_rows % 16:
             pieces = [jnp.concatenate(pieces, axis=0)]
         pieces = pieces + [core_swap(piece) for piece in pieces]
-        normed_all, dt_raw, bc_out = project_first(go, pieces, micro, local, w_bc[0], w_dt[0].T)
+        normed_all, dt_raw, bc_out = project_first(go, pieces, micro, local, w_bc[0], w_dt[0].T, held_bc)
         bc_parts = [bc_out[:, s * 2 * span:(s + 1) * 2 * span] for s in range(chips)]
         bc_here = bc_parts[0]
         bc_parts = [ring_shift(bc_parts[s], s) for s in range(1, chips)]

time: 317 us -> 308 us (0.972)
  waiting for transfers between devices: 88.5 us -> 72.4 us
  Pallas kernels: 153 us -> 157 us
    ppermute x36, waiting for transfers between devices: 57.8 us -> 41.7 us  [ring_shift(): return lax.ppermute(value, 'head', pairs)]
    pallas_call x6, Pallas kernels: 31.5 us -> 46.1 us  [load_beside(): pl.pallas_call(functools.partial(load_kernel, steps), in_specs=[pl.BlockS...]
    pallas_call x4, Pallas kernels: 23.2 us -> 17.6 us  [project_first(): pl.pallas_call(functools.partial(first_kernel, len(pieces), len(held), mi...]
    pallas_call x4, Pallas kernels: 32.7 us -> 28.2 us  [held_inner(): pl.pallas_call(functools.partial(held_kernel, len(held)), in_specs=[pl.Bl...]
  transfers between devices with their start and end apart: 63 -> 63, of which waited for: 38 -> 35; matrix products, arithmetic and copies ran while one was open for 1% -> 1% of each run, Pallas kernels for 21% -> 25%
where the time goes in v3:
time: 308 us; the launch traced here: 304 us
  Pallas kernels  157 us (51%)
  waiting for transfers between devices  72.4 us (24%)
  starting transfers between devices  60.8 us (20%)
  other arithmetic  5.91 us (2%)
  local copies, waits for them, and re-layouts  5.86 us (2%)
    pallas_call x4, Pallas kernels, scan_and_out(): pl.pallas_call(functools.partial(scan_kernel, micro, group_rows, slots, t...  63.1 us
    pallas_call x6, Pallas kernels, load_beside(): pl.pallas_call(functools.partial(load_kernel, steps), in_specs=[pl.BlockS...  46.1 us
    ppermute x36, starting transfers between devices, ring_shift(): return lax.ppermute(value, 'head', pairs)  44 us
    ppermute x36, waiting for transfers between devices, ring_shift(): return lax.ppermute(value, 'head', pairs)  41.7 us
    pallas_call x4, Pallas kernels, held_inner(): pl.pallas_call(functools.partial(held_kernel, len(held)), in_specs=[pl.Bl...  28.2 us
    ppermute x24, waiting for transfers between devices, core_swap(): return lax.ppermute(value, 'head', [(i, i ^ 1) for i in range(count)])  19.4 us
    pallas_call x4, Pallas kernels, project_first(): pl.pallas_call(functools.partial(first_kernel, len(pieces), len(held), mi...  17.6 us
    ppermute x3, starting transfers between devices, next_segment(): return lax.ppermute(value, 'pipe', pairs)  12.5 us
  transfers between devices with their start and end apart: 63, of which 35 were waited for; matrix products, arithmetic and copies ran while one was open for 1% of the time, Pallas kernels for 25%

profile of v3, /device:TPU:0, one launch (start us, length us, event | category | flops | bytes accessed | tf_op | source)
XLA Modules:
  0.0 304.2 jit_solution(2755428612646432395)
XLA Ops:
  2.9 3.0 collective-permute-start
  8.9 3.7 %collective-permute-done.refs_1_ = bf16[16,8192]{1,0:T(8,128)(2,1)S(1)} collective-permute-done((bf16[16,8192]{1,0:T(8,128)(2,1)S(1)}, bf16[16,8192]{1,0:T(8,128)(2,1)S(1)}, u32[]{:S(2)}, u32[]{:S(2)}) %collective-permute-start) | collective-permute-done | bytes 262176 | tf_op jit(solution)/shard_map/ppermute | solution.py:55
  12.6 6.4 %collective-permute-done.1.refs_2_ = bf16[16,8192]{1,0:T(8,128)(2,1)S(1)} collective-permute-done((bf16[16,8192]{1,0:T(8,128)(2,1)S(1)}, bf16[16,8192]{1,0:T(8,128)(2,1)S(1)}, u32[]{:S(2)}, u32[]{:S(2)}) %collective-permute-start.1) | collective-permute-done | bytes 262176 | tf_op jit(solution)/shard_map/ppermute | solution.py:55
  21.0 5.8 %shard_map.149 = (bf16[128,8192]{1,0:T(8,128)(2,1)S(1)}, f32[128,32]{1,0:T(8,128)S(1)}, bf16[128,512]{1,0:T(8,128)(2,1)S(1)}) custom-call(bf16[16,8192]{1,0:T(8,128)(2,1)S(1)} %fusion.3.refs_0_, bf16[16,8192]{1,0:T(8,128)(2,1)S(1)} %collective-permute-done.refs_1_, bf16[16,8192]{1,0:T(8,128)(2,1)S(1)} %collective-permute-done.1.refs_2_, ...), custom_call_target="tpu_custom_call" | custom-call | flops 1140850688 | bytes 8388608 | tf_op jit(solution)/shard_map/pallas_call | solution.py:217
  31.2 12.7 %shard_map.150 = (f32[128,2048]{1,0:T(8,128)S(1)}, bf16[128,128]{1,0:T(8,128)(2,1)S(1)}) custom-call(s32[17]{0:T(128)S(1)} %pad_add_fusion.refs_8_.go_ref.groups_ref, bf16[128,8192]{1,0:T(8,128)(2,1)S(1)} %get-tuple-element.80.normed_ref, bf16[128,128]{1,0:T(8,128)(2,1)S(1)} %get-tuple-element.189.value_ref, bf16[8192,2048]{1,0:T(8,128)(2,1)} %bitcast.38), custom_call_target="tpu_custom_call" | custom-call | flops 4294967296 | bytes 2097152 | tf_op jit(solution)/shard_map/pallas_call | solution.py:260
  49.6 15.7 %shard_map.152 = (bf16[64,8192]{1,0:T(8,128)(2,1)S(1)}, bf16[64,8192]{1,0:T(8,128)(2,1)S(1)}, bf16[128,2048]{1,0:T(8,128)(2,1)}, bf16[128,256]{1,0:T(8,128)(2,1)}, f32[1,32]{1,0:T(1,128)}) custom-call(s32[17]{0:T(128)S(1)} %pad_add_fusion.refs_8_.go_ref.groups_ref, s32[1]{0:T(128)} %bitcast.3.flag_ref, ...), custom_call_target="tpu_custom_call", output_to_operand_aliasing={{2}: (9, {}), {3}: (10, {}), {4}: (11, {})} | custom-call | flops 4496293888 | bytes 33554432 | tf_op jit(solution)/shard_map/pallas_call | solution.py:435
  71.2 7.7 %shard_map.153 = (bf16[8192,256]{1,0:T(8,128)(2,1)S(1)}, bf16[8192,256]{1,0:T(8,128)(2,1)S(1)}, bf16[8192,256]{1,0:T(8,128)(2,1)S(1)}, bf16[8192,256]{1,0:T(8,12...) custom-call(s32[17]{0:T(128)S(1)} %pad_add_fusion.refs_8_.go_ref.groups_ref, ...), custom_call_target="tpu_custom_call" | custom-call | bytes 20971520 | tf_op jit(solution)/shard_map/pallas_call | solution.py:150
  78.9 3.9 %collective-permute-done.13 = bf16[16,8192]{1,0:T(8,128)(2,1)S(1)} collective-permute-done((bf16[16,8192]{1,0:T(8,128)(2,1)S(1)}, bf16[16,8192]{1,0:T(8,128)(2,1)S(1)}, u32[]{:S(2)}, u32[]{:S(2)}) %collective-permute-start.13) | collective-permute-done | bytes 262176 | tf_op jit(solution)/shard_map/ppermute | solution.py:55
  85.8 5.9 %collective-permute-done.15 = bf16[16,8192]{1,0:T(8,128)(2,1)S(1)} collective-permute-done((bf16[16,8192]{1,0:T(8,128)(2,1)S(1)}, bf16[16,8192]{1,0:T(8,128)(2,1)S(1)}, u32[]{:S(2)}, u32[]{:S(2)}) %collective-permute-start.15) | collective-permute-done | bytes 262176 | tf_op jit(solution)/shard_map/ppermute | solution.py:63
  94.9 7.7 %shard_map.154 = (bf16[8192,256]{1,0:T(8,128)(2,1)S(1)}, bf16[8192,256]{1,0:T(8,128)(2,1)S(1)}, bf16[8192,256]{1,0:T(8,128)(2,1)S(1)}, bf16[8192,256]{1,0:T(8,12...) custom-call(s32[17]{0:T(128)S(1)} %pad_add_fusion.refs_8_.go_ref.groups_ref, ...), custom_call_target="tpu_custom_call" | custom-call | bytes 20971520 | tf_op jit(solution)/shard_map/pallas_call | solution.py:150
  107.0 3.9 %shard_map.155 = (bf16[128,8192]{1,0:T(8,128)(2,1)S(1)}, f32[128,32]{1,0:T(8,128)S(1)}, bf16[128,512]{1,0:T(8,128)(2,1)S(1)}) custom-call(bf16[16,8192]{1,0:T(8,128)(2,1)S(1)} %get-tuple-element.88.refs_0_, bf16[16,8192]{1,0:T(8,128)(2,1)S(1)} %collective-permute-done.16.refs_1_, bf16[16,8192]{1,0:T(8,128)(2,1)S(1)} %collective-permute-done.17.refs_2_, ...), custom_call_target="tpu_custom_call" | custom-call | flops 1140850688 | bytes 8388608 | tf_op jit(solution)/shard_map/pallas_call | solution.py:217
  115.3 5.5 %shard_map.156 = (f32[128,2048]{1,0:T(8,128)S(1)}, bf16[128,128]{1,0:T(8,128)(2,1)S(1)}) custom-call(s32[17]{0:T(128)S(1)} %pad_add_fusion.refs_8_.go_ref.groups_ref, bf16[128,8192]{1,0:T(8,128)(2,1)S(1)} %get-tuple-element.91.normed_ref, bf16[128,128]{1,0:T(8,128)(2,1)S(1)} %get-tuple-element.185.value_ref, ...), custom_call_target="tpu_custom_call" | custom-call | flops 4294967296 | bytes 2097152 | tf_op jit(solution)/shard_map/pallas_call | solution.py:260
  122.2 15.7 %shard_map.158 = (bf16[64,8192]{1,0:T(8,128)(2,1)S(1)}, bf16[64,8192]{1,0:T(8,128)(2,1)S(1)}, bf16[128,2048]{1,0:T(8,128)(2,1)}, bf16[128,256]{1,0:T(8,128)(2,1)}, f32[1,32]{1,0:T(1,128)}) custom-call(s32[17]{0:T(128)S(1)} %pad_add_fusion.refs_8_.go_ref.groups_ref, s32[1]{0:T(128)} %bitcast.12.flag_ref, ...), custom_call_target="tpu_custom_call", output_to_operand_aliasing={{2}: (9, {}), {3}: (10, {}), {4}: (11, {})} | custom-call | flops 4496293888 | bytes 33554432 | tf_op jit(solution)/shard_map/pallas_call | solution.py:435
  138.1 2.5 collective-permute-done.27
  143.8 7.7 %shard_map.159 = (bf16[8192,256]{1,0:T(8,128)(2,1)S(1)}, bf16[8192,256]{1,0:T(8,128)(2,1)S(1)}, bf16[8192,256]{1,0:T(8,128)(2,1)S(1)}, bf16[8192,256]{1,0:T(8,12...) custom-call(s32[17]{0:T(128)S(1)} %pad_add_fusion.refs_8_.go_ref.groups_ref, ...), custom_call_target="tpu_custom_call" | custom-call | bytes 20971520 | tf_op jit(solution)/shard_map/pallas_call | solution.py:150
  151.5 4.1 %collective-permute-done.29 = bf16[16,8192]{1,0:T(8,128)(2,1)S(1)} collective-permute-done((bf16[16,8192]{1,0:T(8,128)(2,1)S(1)}, bf16[16,8192]{1,0:T(8,128)(2,1)S(1)}, u32[]{:S(2)}, u32[]{:S(2)}) %collective-permute-start.29) | collective-permute-done | bytes 262176 | tf_op jit(solution)/shard_map/ppermute | solution.py:55
  160.2 7.7 %shard_map.160 = (bf16[8192,256]{1,0:T(8,128)(2,1)S(1)}, bf16[8192,256]{1,0:T(8,128)(2,1)S(1)}, bf16[8192,256]{1,0:T(8,128)(2,1)S(1)}, bf16[8192,256]{1,0:T(8,12...) custom-call(s32[17]{0:T(128)S(1)} %pad_add_fusion.refs_8_.go_ref.groups_ref, ...), custom_call_target="tpu_custom_call" | custom-call | bytes 20971520 | tf_op jit(solution)/shard_map/pallas_call | solution.py:150
  168.5 3.1 %collective-permute-done.33.refs_2_ = bf16[16,8192]{1,0:T(8,128)(2,1)S(1)} collective-permute-done((bf16[16,8192]{1,0:T(8,128)(2,1)S(1)}, bf16[16,8192]{1,0:T(8,128)(2,1)S(1)}, u32[]{:S(2)}, u32[]{:S(2)}) %collective-permute-start.33) | collective-permute-done | bytes 262176 | tf_op jit(solution)/shard_map/ppermute | solution.py:55
  173.5 3.9 %shard_map.161 = (bf16[128,8192]{1,0:T(8,128)(2,1)S(1)}, f32[128,32]{1,0:T(8,128)S(1)}, bf16[128,512]{1,0:T(8,128)(2,1)S(1)}) custom-call(bf16[16,8192]{1,0:T(8,128)(2,1)S(1)} %get-tuple-element.110.refs_0_, bf16[16,8192]{1,0:T(8,128)(2,1)S(1)} %collective-permute-done.32.refs_1_, bf16[16,8192]{1,0:T(8,128)(2,1)S(1)} %collective-permute-done.33.refs_2_, ...), custom_call_target="tpu_custom_call" | custom-call | flops 1140850688 | bytes 8388608 | tf_op jit(solution)/shard_map/pallas_call | solution.py:217
  180.9 5.0 %shard_map.162 = (f32[128,2048]{1,0:T(8,128)S(1)}, bf16[128,128]{1,0:T(8,128)(2,1)S(1)}) custom-call(s32[17]{0:T(128)S(1)} %pad_add_fusion.refs_8_.go_ref.groups_ref, bf16[128,8192]{1,0:T(8,128)(2,1)S(1)} %get-tuple-element.113.normed_ref, bf16[128,128]{1,0:T(8,128)(2,1)S(1)} %get-tuple-element.181.value_ref, ...), custom_call_target="tpu_custom_call" | custom-call | flops 4294967296 | bytes 2097152 | tf_op jit(solution)/shard_map/pallas_call | solution.py:260
  187.4 15.9 %shard_map.164 = (bf16[64,8192]{1,0:T(8,128)(2,1)S(1)}, bf16[64,8192]{1,0:T(8,128)(2,1)S(1)}, bf16[128,2048]{1,0:T(8,128)(2,1)}, bf16[128,256]{1,0:T(8,128)(2,1)}, f32[1,32]{1,0:T(1,128)}) custom-call(s32[17]{0:T(128)S(1)} %pad_add_fusion.refs_8_.go_ref.groups_ref, s32[1]{0:T(128)} %bitcast.14.flag_ref, ...), custom_call_target="tpu_custom_call", output_to_operand_aliasing={{2}: (9, {}), {3}: (10, {}), {4}: (11, {})} | custom-call | flops 4496293888 | bytes 33554432 | tf_op jit(solution)/shard_map/pallas_call | solution.py:435
  210.1 7.7 %shard_map.165 = (bf16[8192,256]{1,0:T(8,128)(2,1)S(1)}, bf16[8192,256]{1,0:T(8,128)(2,1)S(1)}, bf16[8192,256]{1,0:T(8,128)(2,1)S(1)}, bf16[8192,256]{1,0:T(8,12...) custom-call(s32[17]{0:T(128)S(1)} %pad_add_fusion.refs_8_.go_ref.groups_ref, ...), custom_call_target="tpu_custom_call" | custom-call | bytes 20971520 | tf_op jit(solution)/shard_map/pallas_call | solution.py:150
  217.8 3.2 %collective-permute-done.45 = bf16[16,8192]{1,0:T(8,128)(2,1)S(1)} collective-permute-done((bf16[16,8192]{1,0:T(8,128)(2,1)S(1)}, bf16[16,8192]{1,0:T(8,128)(2,1)S(1)}, u32[]{:S(2)}, u32[]{:S(2)}) %collective-permute-start.45) | collective-permute-done | bytes 262176 | tf_op jit(solution)/shard_map/ppermute | solution.py:55
  221.8 10.2 %collective-permute-start.47 = (bf16[16,8192]{1,0:T(8,128)(2,1)S(1)}, bf16[16,8192]{1,0:T(8,128)(2,1)S(1)}, u32[]{:S(2)}, u32[]{:S(2)}) collective-permute-start(bf16[16,8192]{1,0:T(8,128)(2,1)S(1)} %fusion.13), channel_id=1, source_target_pairs={{0,8},{8,0},{16,24},{24,16},{1,9},{9,1},{17,25},{25,17},{2,10},{10... | collective-permute-start | bytes 786440 | tf_op jit(solution)/shard_map/ppermute | solution.py:63
  232.0 5.5 %collective-permute-done.47 = bf16[16,8192]{1,0:T(8,128)(2,1)S(1)} collective-permute-done((bf16[16,8192]{1,0:T(8,128)(2,1)S(1)}, bf16[16,8192]{1,0:T(8,128)(2,1)S(1)}, u32[]{:S(2)}, u32[]{:S(2)}) %collective-permute-start.47) | collective-permute-done | bytes 262176 | tf_op jit(solution)/shard_map/ppermute | solution.py:63
  241.8 7.7 %shard_map.166 = (bf16[8192,256]{1,0:T(8,128)(2,1)S(1)}, bf16[8192,256]{1,0:T(8,128)(2,1)S(1)}, bf16[8192,256]{1,0:T(8,128)(2,1)S(1)}, bf16[8192,256]{1,0:T(8,12...) custom-call(s32[17]{0:T(128)S(1)} %pad_add_fusion.refs_8_.go_ref.groups_ref, ...), custom_call_target="tpu_custom_call" | custom-call | bytes 20971520 | tf_op jit(solution)/shard_map/pallas_call | solution.py:150
  250.1 3.0 collective-permute-done.49.refs_2_
  255.0 3.9 %shard_map.167 = (bf16[128,8192]{1,0:T(8,128)(2,1)S(1)}, f32[128,32]{1,0:T(8,128)S(1)}, bf16[128,512]{1,0:T(8,128)(2,1)S(1)}) custom-call(bf16[16,8192]{1,0:T(8,128)(2,1)S(1)} %get-tuple-element.132.refs_0_, bf16[16,8192]{1,0:T(8,128)(2,1)S(1)} %collective-permute-done.48.refs_1_, bf16[16,8192]{1,0:T(8,128)(2,1)S(1)} %collective-permute-done.49.refs_2_, ...), custom_call_target="tpu_custom_call" | custom-call | flops 1140850688 | bytes 8388608 | tf_op jit(solution)/shard_map/pallas_call | solution.py:217
  262.3 5.0 %shard_map.168 = (f32[128,2048]{1,0:T(8,128)S(1)}, bf16[128,128]{1,0:T(8,128)(2,1)S(1)}) custom-call(s32[17]{0:T(128)S(1)} %pad_add_fusion.refs_8_.go_ref.groups_ref, bf16[128,8192]{1,0:T(8,128)(2,1)S(1)} %get-tuple-element.135.normed_ref, bf16[128,128]{1,0:T(8,128)(2,1)S(1)} %get-tuple-element.177.value_ref, ...), custom_call_target="tpu_custom_call" | custom-call | flops 4294967296 | bytes 2097152 | tf_op jit(solution)/shard_map/pallas_call | solution.py:260
  268.8 15.7 %shard_map.170 = (bf16[64,8192]{1,0:T(8,128)(2,1)S(1)}, bf16[64,8192]{1,0:T(8,128)(2,1)S(1)}, bf16[128,2048]{1,0:T(8,128)(2,1)}, bf16[128,256]{1,0:T(8,128)(2,1)}, f32[1,32]{1,0:T(1,128)}) custom-call(s32[17]{0:T(128)S(1)} %pad_add_fusion.refs_8_.go_ref.groups_ref, s32[1]{0:T(128)} %bitcast.15.flag_ref, ...), custom_call_target="tpu_custom_call", output_to_operand_aliasing={{2}: (9, {}), {3}: (10, {}), {4}: (11, {})} | custom-call | flops 4496293888 | bytes 33554432 | tf_op jit(solution)/shard_map/pallas_call | solution.py:435
  284.8 2.5 collective-permute-done.59
  296.3 6.0 %collective-permute-done.61 = bf16[16,8192]{1,0:T(8,128)(2,1)S(1)} collective-permute-done((bf16[16,8192]{1,0:T(8,128)(2,1)S(1)}, bf16[16,8192]{1,0:T(8,128)(2,1)S(1)}, u32[]{:S(2)}, u32[]{:S(2)}) %collective-permute-start.61) | collective-permute-done | bytes 262176 | tf_op jit(solution)/shard_map/ppermute | solution.py:55
  (201 shorter events, 84.4 us)
Async XLA Ops:
  2.9 9.7 %collective-permute-start = (bf16[16,8192]{1,0:T(8,128)(2,1)S(1)}, bf16[16,8192]{1,0:T(8,128)(2,1)S(1)}, u32[]{:S(2)}, u32[]{:S(2)}) collective-permute-start(bf16[16,8192]{1,0:T(8,128)(2,1)S(1)} %fusion.3.refs_0_), channel_id=1, source_target_pairs={{0,2},{1,3},{2,6},{3,7},{6,4},{7,5},{4,0},{5,1},{8,10},{9,11},{10,... | collective-permute-start | bytes 786440 | tf_op jit(solution)/shard_map/ppermute | solution.py:55
  5.9 13.1 %collective-permute-start.1 = (bf16[16,8192]{1,0:T(8,128)(2,1)S(1)}, bf16[16,8192]{1,0:T(8,128)(2,1)S(1)}, u32[]{:S(2)}, u32[]{:S(2)}) collective-permute-start(bf16[16,8192]{1,0:T(8,128)(2,1)S(1)} %fusion.3.refs_0_), channel_id=1, source_target_pairs={{0,6},{1,7},{2,4},{3,5},{6,0},{7,1},{4,2},{5,3},{8,14},{9,15},{10,... | collective-permute-start | bytes 786440 | tf_op jit(solution)/shard_map/ppermute | solution.py:55
  7.4 11.8 %collective-permute-start.2 = (bf16[16,8192]{1,0:T(8,128)(2,1)S(1)}, bf16[16,8192]{1,0:T(8,128)(2,1)S(1)}, u32[]{:S(2)}, u32[]{:S(2)}) collective-permute-start(bf16[16,8192]{1,0:T(8,128)(2,1)S(1)} %fusion.3.refs_0_), channel_id=1, source_target_pairs={{0,4},{1,5},{2,0},{3,1},{6,2},{7,3},{4,6},{5,7},{8,12},{9,13},{10,... | collective-permute-start | bytes 786440 | tf_op jit(solution)/shard_map/ppermute | solution.py:55
  8.9 10.8 %collective-permute-start.3 = (bf16[16,8192]{1,0:T(8,128)(2,1)S(1)}, bf16[16,8192]{1,0:T(8,128)(2,1)S(1)}, u32[]{:S(2)}, u32[]{:S(2)}) collective-permute-start(bf16[16,8192]{1,0:T(8,128)(2,1)S(1)} %fusion.3.refs_0_), channel_id=1, source_target_pairs={{0,1},{1,0},{2,3},{3,2},{4,5},{5,4},{6,7},{7,6},{8,9},{9,8},{10,11... | collective-permute-start | bytes 786440 | tf_op jit(solution)/shard_map/ppermute | solution.py:46
  26.8 17.2 %collective-permute-start.7 = (bf16[128,128]{1,0:T(8,128)(2,1)S(1)}, bf16[128,128]{1,0:T(8,128)(2,1)S(1)}, u32[]{:S(2)}, u32[]{:S(2)}) collective-permute-start(bf16[128,128]{1,0:T(8,128)(2,1)S(1)} %get-tuple-element.188), channel_id=1, source_target_pairs={{0,2},{1,3},{2,6},{3,7},{6,4},{7,5},{4,0},{5,1},{8,10},{9,11},{10,... | collective-permute-start | bytes 98312 | tf_op jit(solution)/shard_map/ppermute | solution.py:55
  28.3 15.7 %collective-permute-start.8 = (bf16[128,128]{1,0:T(8,128)(2,1)S(1)}, bf16[128,128]{1,0:T(8,128)(2,1)S(1)}, u32[]{:S(2)}, u32[]{:S(2)}) collective-permute-start(bf16[128,128]{1,0:T(8,128)(2,1)S(1)} %get-tuple-element.187), channel_id=1, source_target_pairs={{0,6},{1,7},{2,4},{3,5},{6,0},{7,1},{4,2},{5,3},{8,14},{9,15},{10,... | collective-permute-start | bytes 98312 | tf_op jit(solution)/shard_map/ppermute | solution.py:55
  29.5 14.5 %collective-permute-start.9 = (bf16[128,128]{1,0:T(8,128)(2,1)S(1)}, bf16[128,128]{1,0:T(8,128)(2,1)S(1)}, u32[]{:S(2)}, u32[]{:S(2)}) collective-permute-start(bf16[128,128]{1,0:T(8,128)(2,1)S(1)} %get-tuple-element.186), channel_id=1, source_target_pairs={{0,4},{1,5},{2,0},{3,1},{6,2},{7,3},{4,6},{5,7},{8,12},{9,13},{10,... | collective-permute-start | bytes 98312 | tf_op jit(solution)/shard_map/ppermute | solution.py:55
  68.5 10.4 %collective-permute-start.12 = (bf16[16,8192]{1,0:T(8,128)(2,1)S(1)}, bf16[16,8192]{1,0:T(8,128)(2,1)S(1)}, u32[]{:S(2)}, u32[]{:S(2)}) collective-permute-start(bf16[16,8192]{1,0:T(8,128)(2,1)S(1)} %get-tuple-element.173), channel_id=1, source_target_pairs={{0,2},{1,3},{2,6},{3,7},{6,4},{7,5},{4,0},{5,1},{8,10},{9,11},{10,... | collective-permute-start | bytes 786440 | tf_op jit(solution)/shard_map/ppermute | solution.py:55
  68.8 13.9 %collective-permute-start.13 = (bf16[16,8192]{1,0:T(8,128)(2,1)S(1)}, bf16[16,8192]{1,0:T(8,128)(2,1)S(1)}, u32[]{:S(2)}, u32[]{:S(2)}) collective-permute-start(bf16[16,8192]{1,0:T(8,128)(2,1)S(1)} %get-tuple-element.172), channel_id=1, source_target_pairs={{0,6},{1,7},{2,4},{3,5},{6,0},{7,1},{4,2},{5,3},{8,14},{9,15},{10,... | collective-permute-start | bytes 786440 | tf_op jit(solution)/shard_map/ppermute | solution.py:55
  70.6 13.4 %collective-permute-start.14 = (bf16[16,8192]{1,0:T(8,128)(2,1)S(1)}, bf16[16,8192]{1,0:T(8,128)(2,1)S(1)}, u32[]{:S(2)}, u32[]{:S(2)}) collective-permute-start(bf16[16,8192]{1,0:T(8,128)(2,1)S(1)} %get-tuple-element.171), channel_id=1, source_target_pairs={{0,4},{1,5},{2,0},{3,1},{6,2},{7,3},{4,6},{5,7},{8,12},{9,13},{10,... | collective-permute-start | bytes 786440 | tf_op jit(solution)/shard_map/ppermute | solution.py:55
  92.0 10.7 %collective-permute-start.16 = (bf16[16,8192]{1,0:T(8,128)(2,1)S(1)}, bf16[16,8192]{1,0:T(8,128)(2,1)S(1)}, u32[]{:S(2)}, u32[]{:S(2)}) collective-permute-start(bf16[16,8192]{1,0:T(8,128)(2,1)S(1)} %fusion.8.refs_5_), channel_id=1, source_target_pairs={{0,2},{1,3},{2,6},{3,7},{6,4},{7,5},{4,0},{5,1},{8,10},{9,11},{10,... | collective-permute-start | bytes 786440 | tf_op jit(solution)/shard_map/ppermute | solution.py:55
  93.4 11.4 %collective-permute-start.17 = (bf16[16,8192]{1,0:T(8,128)(2,1)S(1)}, bf16[16,8192]{1,0:T(8,128)(2,1)S(1)}, u32[]{:S(2)}, u32[]{:S(2)}) collective-permute-start(bf16[16,8192]{1,0:T(8,128)(2,1)S(1)} %fusion.8.refs_5_), channel_id=1, source_target_pairs={{0,6},{1,7},{2,4},{3,5},{6,0},{7,1},{4,2},{5,3},{8,14},{9,15},{10,... | collective-permute-start | bytes 786440 | tf_op jit(solution)/shard_map/ppermute | solution.py:55
  94.5 10.9 %collective-permute-start.18 = (bf16[16,8192]{1,0:T(8,128)(2,1)S(1)}, bf16[16,8192]{1,0:T(8,128)(2,1)S(1)}, u32[]{:S(2)}, u32[]{:S(2)}) collective-permute-start(bf16[16,8192]{1,0:T(8,128)(2,1)S(1)} %fusion.8.refs_5_), channel_id=1, source_target_pairs={{0,4},{1,5},{2,0},{3,1},{6,2},{7,3},{4,6},{5,7},{8,12},{9,13},{10,... | collective-permute-start | bytes 786440 | tf_op jit(solution)/shard_map/ppermute | solution.py:55
  111.0 9.8 %collective-permute-start.23 = (bf16[128,128]{1,0:T(8,128)(2,1)S(1)}, bf16[128,128]{1,0:T(8,128)(2,1)S(1)}, u32[]{:S(2)}, u32[]{:S(2)}) collective-permute-start(bf16[128,128]{1,0:T(8,128)(2,1)S(1)} %get-tuple-element.184), channel_id=1, source_target_pairs={{0,2},{1,3},{2,6},{3,7},{6,4},{7,5},{4,0},{5,1},{8,10},{9,11},{10,... | collective-permute-start | bytes 98312 | tf_op jit(solution)/shard_map/ppermute | solution.py:55
  141.0 10.5 %collective-permute-start.28 = (bf16[16,8192]{1,0:T(8,128)(2,1)S(1)}, bf16[16,8192]{1,0:T(8,128)(2,1)S(1)}, u32[]{:S(2)}, u32[]{:S(2)}) collective-permute-start(bf16[16,8192]{1,0:T(8,128)(2,1)S(1)} %get-tuple-element.169), channel_id=1, source_target_pairs={{0,2},{1,3},{2,6},{3,7},{6,4},{7,5},{4,0},{5,1},{8,10},{9,11},{10,... | collective-permute-start | bytes 786440 | tf_op jit(solution)/shard_map/ppermute | solution.py:55
  141.7 13.9 %collective-permute-start.29 = (bf16[16,8192]{1,0:T(8,128)(2,1)S(1)}, bf16[16,8192]{1,0:T(8,128)(2,1)S(1)}, u32[]{:S(2)}, u32[]{:S(2)}) collective-permute-start(bf16[16,8192]{1,0:T(8,128)(2,1)S(1)} %get-tuple-element.168), channel_id=1, source_target_pairs={{0,6},{1,7},{2,4},{3,5},{6,0},{7,1},{4,2},{5,3},{8,14},{9,15},{10,... | collective-permute-start | bytes 786440 | tf_op jit(solution)/shard_map/ppermute | solution.py:55
  143.7 12.6 %collective-permute-start.30 = (bf16[16,8192]{1,0:T(8,128)(2,1)S(1)}, bf16[16,8192]{1,0:T(8,128)(2,1)S(1)}, u32[]{:S(2)}, u32[]{:S(2)}) collective-permute-start(bf16[16,8192]{1,0:T(8,128)(2,1)S(1)} %get-tuple-element.167), channel_id=1, source_target_pairs={{0,4},{1,5},{2,0},{3,1},{6,2},{7,3},{4,6},{5,7},{8,12},{9,13},{10,... | collective-permute-start | bytes 786440 | tf_op jit(solution)/shard_map/ppermute | solution.py:55
  157.5 10.6 %collective-permute-start.32 = (bf16[16,8192]{1,0:T(8,128)(2,1)S(1)}, bf16[16,8192]{1,0:T(8,128)(2,1)S(1)}, u32[]{:S(2)}, u32[]{:S(2)}) collective-permute-start(bf16[16,8192]{1,0:T(8,128)(2,1)S(1)} %fusion.12.refs_5_), channel_id=1, source_target_pairs={{0,2},{1,3},{2,6},{3,7},{6,4},{7,5},{4,0},{5,1},{8,10},{9,11},{10,... | collective-permute-start | bytes 786440 | tf_op jit(solution)/shard_map/ppermute | solution.py:55
  158.2 13.4 %collective-permute-start.33 = (bf16[16,8192]{1,0:T(8,128)(2,1)S(1)}, bf16[16,8192]{1,0:T(8,128)(2,1)S(1)}, u32[]{:S(2)}, u32[]{:S(2)}) collective-permute-start(bf16[16,8192]{1,0:T(8,128)(2,1)S(1)} %fusion.12.refs_5_), channel_id=1, source_target_pairs={{0,6},{1,7},{2,4},{3,5},{6,0},{7,1},{4,2},{5,3},{8,14},{9,15},{10,... | collective-permute-start | bytes 786440 | tf_op jit(solution)/shard_map/ppermute | solution.py:55
  160.1 11.6 %collective-permute-start.34 = (bf16[16,8192]{1,0:T(8,128)(2,1)S(1)}, bf16[16,8192]{1,0:T(8,128)(2,1)S(1)}, u32[]{:S(2)}, u32[]{:S(2)}) collective-permute-start(bf16[16,8192]{1,0:T(8,128)(2,1)S(1)} %fusion.12.refs_5_), channel_id=1, source_target_pairs={{0,4},{1,5},{2,0},{3,1},{6,2},{7,3},{4,6},{5,7},{8,12},{9,13},{10,... | collective-permute-start | bytes 786440 | tf_op jit(solution)/shard_map/ppermute | solution.py:55
  177.5 8.4 %collective-permute-start.39 = (bf16[128,128]{1,0:T(8,128)(2,1)S(1)}, bf16[128,128]{1,0:T(8,128)(2,1)S(1)}, u32[]{:S(2)}, u32[]{:S(2)}) collective-permute-start(bf16[128,128]{1,0:T(8,128)(2,1)S(1)} %get-tuple-element.180), channel_id=1, source_target_pairs={{0,2},{1,3},{2,6},{3,7},{6,4},{7,5},{4,0},{5,1},{8,10},{9,11},{10,... | collective-permute-start | bytes 98312 | tf_op jit(solution)/shard_map/ppermute | solution.py:55
  206.4 11.4 %collective-permute-start.44 = (bf16[16,8192]{1,0:T(8,128)(2,1)S(1)}, bf16[16,8192]{1,0:T(8,128)(2,1)S(1)}, u32[]{:S(2)}, u32[]{:S(2)}) collective-permute-start(bf16[16,8192]{1,0:T(8,128)(2,1)S(1)} %get-tuple-element.165), channel_id=1, source_target_pairs={{0,2},{1,3},{2,6},{3,7},{6,4},{7,5},{4,0},{5,1},{8,10},{9,11},{10,... | collective-permute-start | bytes 786440 | tf_op jit(solution)/shard_map/ppermute | solution.py:55
  207.8 13.3 %collective-permute-start.45 = (bf16[16,8192]{1,0:T(8,128)(2,1)S(1)}, bf16[16,8192]{1,0:T(8,128)(2,1)S(1)}, u32[]{:S(2)}, u32[]{:S(2)}) collective-permute-start(bf16[16,8192]{1,0:T(8,128)(2,1)S(1)} %get-tuple-element.164), channel_id=1, source_target_pairs={{0,6},{1,7},{2,4},{3,5},{6,0},{7,1},{4,2},{5,3},{8,14},{9,15},{10,... | collective-permute-start | bytes 786440 | tf_op jit(solution)/shard_map/ppermute | solution.py:55
  209.1 12.6 %collective-permute-start.46 = (bf16[16,8192]{1,0:T(8,128)(2,1)S(1)}, bf16[16,8192]{1,0:T(8,128)(2,1)S(1)}, u32[]{:S(2)}, u32[]{:S(2)}) collective-permute-start(bf16[16,8192]{1,0:T(8,128)(2,1)S(1)} %get-tuple-element.163), channel_id=1, source_target_pairs={{0,4},{1,5},{2,0},{3,1},{6,2},{7,3},{4,6},{5,7},{8,12},{9,13},{10,... | collective-permute-start | bytes 786440 | tf_op jit(solution)/shard_map/ppermute | solution.py:55
  221.8 15.7 %collective-permute-start.47 = (bf16[16,8192]{1,0:T(8,128)(2,1)S(1)}, bf16[16,8192]{1,0:T(8,128)(2,1)S(1)}, u32[]{:S(2)}, u32[]{:S(2)}) collective-permute-start(bf16[16,8192]{1,0:T(8,128)(2,1)S(1)} %fusion.13), channel_id=1, source_target_pairs={{0,8},{8,0},{16,24},{24,16},{1,9},{9,1},{17,25},{25,17},{2,10},{10... | collective-permute-start | bytes 786440 | tf_op jit(solution)/shard_map/ppermute | solution.py:63
  237.8 11.7 %collective-permute-start.48 = (bf16[16,8192]{1,0:T(8,128)(2,1)S(1)}, bf16[16,8192]{1,0:T(8,128)(2,1)S(1)}, u32[]{:S(2)}, u32[]{:S(2)}) collective-permute-start(bf16[16,8192]{1,0:T(8,128)(2,1)S(1)} %fusion.16.refs_5_), channel_id=1, source_target_pairs={{0,2},{1,3},{2,6},{3,7},{6,4},{7,5},{4,0},{5,1},{8,10},{9,11},{10,... | collective-permute-start | bytes 786440 | tf_op jit(solution)/shard_map/ppermute | solution.py:55
  240.1 13.0 %collective-permute-start.49 = (bf16[16,8192]{1,0:T(8,128)(2,1)S(1)}, bf16[16,8192]{1,0:T(8,128)(2,1)S(1)}, u32[]{:S(2)}, u32[]{:S(2)}) collective-permute-start(bf16[16,8192]{1,0:T(8,128)(2,1)S(1)} %fusion.16.refs_5_), channel_id=1, source_target_pairs={{0,6},{1,7},{2,4},{3,5},{6,0},{7,1},{4,2},{5,3},{8,14},{9,15},{10,... | collective-permute-start | bytes 786440 | tf_op jit(solution)/shard_map/ppermute | solution.py:55
  241.8 11.4 %collective-permute-start.50 = (bf16[16,8192]{1,0:T(8,128)(2,1)S(1)}, bf16[16,8192]{1,0:T(8,128)(2,1)S(1)}, u32[]{:S(2)}, u32[]{:S(2)}) collective-permute-start(bf16[16,8192]{1,0:T(8,128)(2,1)S(1)} %fusion.16.refs_5_), channel_id=1, source_target_pairs={{0,4},{1,5},{2,0},{3,1},{6,2},{7,3},{4,6},{5,7},{8,12},{9,13},{10,... | collective-permute-start | bytes 786440 | tf_op jit(solution)/shard_map/ppermute | solution.py:55
  259.0 8.4 %collective-permute-start.55 = (bf16[128,128]{1,0:T(8,128)(2,1)S(1)}, bf16[128,128]{1,0:T(8,128)(2,1)S(1)}, u32[]{:S(2)}, u32[]{:S(2)}) collective-permute-start(bf16[128,128]{1,0:T(8,128)(2,1)S(1)} %get-tuple-element.176), channel_id=1, source_target_pairs={{0,2},{1,3},{2,6},{3,7},{6,4},{7,5},{4,0},{5,1},{8,10},{9,11},{10,... | collective-permute-start | bytes 98312 | tf_op jit(solution)/shard_map/ppermute | solution.py:55
  287.7 8.6 %collective-permute-start.60 = (bf16[16,8192]{1,0:T(8,128)(2,1)S(1)}, bf16[16,8192]{1,0:T(8,128)(2,1)S(1)}, u32[]{:S(2)}, u32[]{:S(2)}) collective-permute-start(bf16[16,8192]{1,0:T(8,128)(2,1)S(1)} %get-tuple-element.161), channel_id=1, source_target_pairs={{0,2},{1,3},{2,6},{3,7},{6,4},{7,5},{4,0},{5,1},{8,10},{9,11},{10,... | collective-permute-start | bytes 786440 | tf_op jit(solution)/shard_map/ppermute | solution.py:55
  289.1 13.2 %collective-permute-start.61 = (bf16[16,8192]{1,0:T(8,128)(2,1)S(1)}, bf16[16,8192]{1,0:T(8,128)(2,1)S(1)}, u32[]{:S(2)}, u32[]{:S(2)}) collective-permute-start(bf16[16,8192]{1,0:T(8,128)(2,1)S(1)} %get-tuple-element.160), channel_id=1, source_target_pairs={{0,6},{1,7},{2,4},{3,5},{6,0},{7,1},{4,2},{5,3},{8,14},{9,15},{10,... | collective-permute-start | bytes 786440 | tf_op jit(solution)/shard_map/ppermute | solution.py:55
  290.3 12.6 %collective-permute-start.62 = (bf16[16,8192]{1,0:T(8,128)(2,1)S(1)}, bf16[16,8192]{1,0:T(8,128)(2,1)S(1)}, u32[]{:S(2)}, u32[]{:S(2)}) collective-permute-start(bf16[16,8192]{1,0:T(8,128)(2,1)S(1)} %get-tuple-element.159), channel_id=1, source_target_pairs={{0,4},{1,5},{2,0},{3,1},{6,2},{7,3},{4,6},{5,7},{8,12},{9,13},{10,... | collective-permute-start | bytes 786440 | tf_op jit(solution)/shard_map/ppermute | solution.py:55
  (48 other events, 277.8 us)
